TPU v7x, 32 devices: a whole 2x2x4 slice. The times are simulated.
32 devices in a mesh: dp: 4 (over x, core), seq: 8 (over z, y).
Axes of the slice: x: 2, y: 2, z: 4, core: 2. Of those that a mesh axis runs over, the one named last changes fastest.
Arguments:
- tokens: bfloat16 [4, 2048, 768], P('dp', 'seq'), may hold values from -6 to 6
- cotangent: bfloat16 [4, 2048, 768], P('dp', 'seq'), may hold values from -6 to 6
- gain_attn: bfloat16 [768], P(('dp', 'seq')), may hold values from 0.5 to 1.5
- query_w: bfloat16 [768, 768], P(('dp', 'seq')), may hold values from -0.0546875 to 0.0546875
- key_w: bfloat16 [768, 768], P(('dp', 'seq')), may hold values from -0.21875 to 0.21875
- value_w: bfloat16 [768, 768], P(('dp', 'seq')), may hold values from -0.21875 to 0.21875
- output_w: bfloat16 [768, 768], P(None, ('dp', 'seq')), may hold values from -1.25 to 1.25
- rel_table: bfloat16 [32, 12], P('seq'), may hold values from -4 to 4
- rel_bucket: int32 [4095], replicated, may hold values from 0 to 31, as said below
- gain_ffn: bfloat16 [768], P(('dp', 'seq')), may hold values from 0.5 to 1.5
- router_w: bfloat16 [768, 4], P(('dp', 'seq')), may hold values from -0.15625 to 0.15625
- routes: int32 [4, 8, 256, 1], P('dp', 'seq'), may hold values from 0 to 3; in each aligned block of 256 rows (0 to 255, 256 to 511, ..., all dimensions but the last counted through in order) at most 128 rows name the same one
- expert_in: bfloat16 [4, 768, 3072], P('dp', None, 'seq'), may hold values from -0.21875 to 0.21875
- expert_out: bfloat16 [4, 768, 3072], P('dp', None, 'seq'), may hold values from -1.75 to 1.75
Outputs:
- mixed: bfloat16 [4, 2048, 768], P('dp', 'seq')
- grad_tokens: float32 [4, 2048, 768], P('dp', 'seq')
- grad_gain_attn: float32 [768], P(('dp', 'seq'))
- grad_query: float32 [768, 768], P(('dp', 'seq'))
- grad_key: float32 [768, 768], P(('dp', 'seq'))
- grad_value: float32 [768, 768], P(('dp', 'seq'))
- grad_output: float32 [768, 768], P(None, ('dp', 'seq'))
- grad_table: float32 [32, 12], P('seq')
- grad_gain_ffn: float32 [768], P(('dp', 'seq'))
- grad_router: float32 [768, 4], P(('dp', 'seq'))
- grad_expert_in: float32 [4, 768, 3072], P('dp', None, 'seq')
- grad_expert_out: float32 [4, 768, 3072], P('dp', None, 'seq')
Inputs may be any that keep to these rules, and one draw needn't show every extreme that they name: `routes`: among the 256 tokens of one device no expert is named more than 128 times, a bound that some block reaches. `rel_bucket`: entry r is the bucket of key position minus query position r - 2047; buckets never fall as the distance grows on either side.
All inputs are finite; a program needn't handle non-finite values.
Results may differ from a plain program's by a relative error of at most 0.018.
Values may be sent and summed in bfloat16 or wider, within the bound.
No kernel may reach another device: no remote copies, remote signals or barrier semaphores. Data moves between devices by JAX's collectives and lax.ppermute only.
A program may use at most 256 MiB of HBM per device.

v0:
```python
from functools import partial

import jax
import jax.numpy as jnp
from jax import lax
from jax.sharding import PartitionSpec as P

epsilon = 1e-06
highest = lax.Precision.HIGHEST


def contract_first(left_mat, right_mat):
    return lax.dot_general(
        left_mat, right_mat, (((0,), (0,)), ((), ())), preferred_element_type=jnp.float32
    )


def contract_last(left_mat, right_mat):
    return lax.dot_general(
        left_mat, right_mat, (((1,), (1,)), ((), ())), preferred_element_type=jnp.float32
    )


def norm_back(values, row_scale, gain_vec, grad_normed):
    scaled = gain_vec * grad_normed
    grad_values = row_scale * scaled - values * row_scale**3 * jnp.mean(
        scaled * values, axis=-1, keepdims=True
    )
    grad_gain = jnp.sum(grad_normed * values * row_scale, axis=0)
    return (grad_values, grad_gain)


def toeplitz(vec_pad, row_count, col_count, row_start):
    half_len = vec_pad.shape[0] // 2
    span = row_count + col_count
    window = lax.dynamic_slice_in_dim(vec_pad, half_len - row_start - row_count, span, 0).T
    head_count = window.shape[0]
    tiled_rows = jnp.broadcast_to(window[:, None, :], (head_count, row_count, span))
    skewed = tiled_rows.reshape(head_count, row_count * span)[:, : row_count * (span - 1)]
    skewed = skewed.reshape(head_count, row_count, span - 1)
    return skewed[:, :, row_count - 1 : row_count - 1 + col_count]


def table_grad(grad_block, rel_bucket, row_start, bucket_count):
    head_count, row_count, col_count = grad_block.shape
    padded = jnp.pad(grad_block, ((0, 0), (0, 0), (row_count, 0)))
    flat = padded.reshape(head_count, row_count * (row_count + col_count))
    flat = jnp.pad(flat, ((0, 0), (0, row_count)))
    diagonals = jnp.sum(flat.reshape(head_count, row_count, row_count + col_count + 1), axis=1)
    fill_ids = jnp.full((row_count + 1,), -1, jnp.int32)
    padded_ids = jnp.concatenate([fill_ids, rel_bucket, fill_ids])
    window = lax.dynamic_slice_in_dim(
        padded_ids, col_count - row_start, row_count + col_count + 1, 0
    )
    one_hot = (window[:, None] == jnp.arange(bucket_count, dtype=jnp.int32)[None, :]).astype(
        jnp.float32
    )
    return jnp.dot(diagonals, one_hot, precision=highest).T


def expert_step(arrived, pieces):
    w_up = pieces[0][0]
    w_down = pieces[1][0]
    pre_act = jnp.dot(arrived, w_up, preferred_element_type=jnp.float32)
    hidden = jax.nn.gelu(pre_act, approximate=True).astype(jnp.bfloat16)
    produced = contract_last(hidden, w_down)
    return (produced, pre_act)


def attn_scores(query_h, key_h, bias_block):
    raw_scores = jnp.einsum("bihd,bjhd->bhij", query_h, key_h, preferred_element_type=jnp.float32)
    return raw_scores + bias_block[None].astype(jnp.float32)


def local(
    tokens,
    cotangent,
    gain_attn,
    query_w,
    key_w,
    value_w,
    output_w,
    rel_table,
    rel_bucket,
    gain_ffn,
    router_w,
    routes,
    expert_in,
    expert_out,
):
    seq_count, local_len, model_width = tokens.shape
    tok_count = seq_count * local_len
    length = local_len * lax.axis_size("seq")
    head_count = rel_table.shape[1]
    inner_width = query_w.shape[1]
    head_size = inner_width // head_count
    experts = router_w.shape[1]
    capacity = 2 * tok_count // experts
    bucket_count = rel_table.shape[0] * lax.axis_size("seq")
    gain_a, gain_f, w_query, w_key, w_value, w_out, w_router = (
        lax.all_gather(gain_attn, ("dp", "seq"), axis=0, tiled=True),
        lax.all_gather(gain_ffn, ("dp", "seq"), axis=0, tiled=True),
        lax.all_gather(query_w, ("dp", "seq"), axis=0, tiled=True),
        lax.all_gather(key_w, ("dp", "seq"), axis=0, tiled=True),
        lax.all_gather(value_w, ("dp", "seq"), axis=0, tiled=True),
        lax.all_gather(output_w, ("dp", "seq"), axis=1, tiled=True),
        lax.all_gather(router_w, ("dp", "seq"), axis=0, tiled=True),
    )
    inputs = tokens.reshape(tok_count, model_width).astype(jnp.float32)
    scale_a = lax.rsqrt(jnp.mean(inputs * inputs, axis=-1, keepdims=True) + epsilon)
    normed_a = (inputs * scale_a * gain_a.astype(jnp.float32)).astype(jnp.bfloat16)
    merged_fwd = jnp.concatenate([w_query, w_key, w_value], axis=1)
    qkv_rows = jnp.dot(normed_a, merged_fwd, preferred_element_type=jnp.float32).astype(
        jnp.bfloat16
    )
    queries = qkv_rows[:, :inner_width]
    keys_loc = qkv_rows[:, inner_width : 2 * inner_width]
    values_loc = qkv_rows[:, 2 * inner_width :]
    keys_all, values_all, bias_table = (
        lax.all_gather(
            keys_loc.reshape(seq_count, local_len, inner_width), "seq", axis=1, tiled=True
        ),
        lax.all_gather(
            values_loc.reshape(seq_count, local_len, inner_width), "seq", axis=1, tiled=True
        ),
        lax.all_gather(rel_table, "seq", axis=0, tiled=True),
    )
    start_q = lax.axis_index("seq") * local_len
    bucket_hot = (rel_bucket[:, None] == jnp.arange(bucket_count, dtype=jnp.int32)[None, :]).astype(
        jnp.float32
    )
    bias_vec = jnp.dot(bucket_hot, bias_table.astype(jnp.float32), precision=highest)
    zero_row = jnp.zeros((1, head_count), jnp.float32)
    vec_pad = jnp.concatenate([bias_vec, zero_row], axis=0).astype(jnp.bfloat16)
    bias_q = toeplitz(vec_pad, local_len, length, start_q)
    query_h = queries.reshape(seq_count, local_len, head_count, head_size)
    key_h = keys_all.reshape(seq_count, length, head_count, head_size)
    value_h = values_all.reshape(seq_count, length, head_count, head_size)
    raw_scores = attn_scores(query_h, key_h, bias_q)
    row_max = jnp.max(raw_scores, axis=-1, keepdims=True)
    exp_scores = jnp.exp(raw_scores - row_max)
    row_total = jnp.sum(exp_scores, axis=-1, keepdims=True)
    log_total = row_max[..., 0] + jnp.log(row_total[..., 0])
    attn_probs = exp_scores / row_total
    context = jnp.einsum(
        "bhij,bjhd->bihd",
        attn_probs.astype(jnp.bfloat16),
        value_h,
        preferred_element_type=jnp.float32,
    )
    context = context.astype(jnp.bfloat16).reshape(tok_count, inner_width)
    hidden_attn = inputs + jnp.dot(context, w_out, preferred_element_type=jnp.float32)
    scale_f = lax.rsqrt(jnp.mean(hidden_attn * hidden_attn, axis=-1, keepdims=True) + epsilon)
    normed_f = (hidden_attn * scale_f * gain_f.astype(jnp.float32)).astype(jnp.bfloat16)
    logits = jnp.dot(normed_f, w_router, preferred_element_type=jnp.float32)
    router_p = jax.nn.softmax(logits, axis=-1)
    route_ids = routes.reshape(tok_count)
    choose = (route_ids[:, None] == jnp.arange(experts, dtype=jnp.int32)[None, :]).astype(jnp.int32)
    choose_f = choose.astype(jnp.float32)
    gate_prob = jnp.sum(router_p * choose_f, axis=-1)
    earlier = jnp.cumsum(choose, axis=0) - choose
    place_ids = route_ids * capacity + jnp.sum(earlier * choose, axis=-1)
    send_buf = (
        jnp.zeros((experts * capacity, model_width), jnp.bfloat16).at[place_ids].set(normed_f)
    )
    arrived = lax.all_to_all(
        send_buf.reshape(experts, capacity, model_width),
        "dp",
        split_axis=0,
        concat_axis=0,
        tiled=True,
    ).reshape(-1, model_width)
    produced, pre_all = expert_step(
        arrived,
        (
            lax.all_gather(expert_in, "seq", axis=2, tiled=True),
            lax.all_gather(expert_out, "seq", axis=2, tiled=True),
        ),
    )
    returned = lax.all_to_all(
        produced.astype(jnp.bfloat16).reshape(-1, capacity, model_width),
        "dp",
        split_axis=0,
        concat_axis=0,
        tiled=True,
    ).reshape(experts * capacity, model_width)
    expert_tok = jnp.take(returned, place_ids, axis=0).astype(jnp.float32)
    mixed = (
        (hidden_attn + gate_prob[:, None] * expert_tok)
        .astype(jnp.bfloat16)
        .reshape(seq_count, local_len, model_width)
    )
    back_ga, back_gf, back_query, back_key, back_value, back_out, back_router = (
        lax.all_gather(gain_attn, ("dp", "seq"), axis=0, tiled=True),
        lax.all_gather(gain_ffn, ("dp", "seq"), axis=0, tiled=True),
        lax.all_gather(query_w, ("dp", "seq"), axis=0, tiled=True),
        lax.all_gather(key_w, ("dp", "seq"), axis=0, tiled=True),
        lax.all_gather(value_w, ("dp", "seq"), axis=0, tiled=True),
        lax.all_gather(output_w, ("dp", "seq"), axis=1, tiled=True),
        lax.all_gather(router_w, ("dp", "seq"), axis=0, tiled=True),
    )
    upstream = cotangent.reshape(tok_count, model_width).astype(jnp.float32)
    grad_gate = jnp.sum(upstream * expert_tok, axis=-1)
    grad_expert = (gate_prob[:, None] * upstream).astype(jnp.bfloat16)
    grad_buf = (
        jnp.zeros((experts * capacity, model_width), jnp.bfloat16).at[place_ids].set(grad_expert)
    )
    grad_rows = lax.all_to_all(
        grad_buf.reshape(experts, capacity, model_width),
        "dp",
        split_axis=0,
        concat_axis=0,
        tiled=True,
    ).reshape(-1, model_width)
    full_up, full_down = (
        lax.all_gather(expert_in, "seq", axis=2, tiled=True),
        lax.all_gather(expert_out, "seq", axis=2, tiled=True),
    )
    full_up = full_up[0]
    full_down = full_down[0]
    hidden, gelu_back = jax.vjp(partial(jax.nn.gelu, approximate=True), pre_all)
    grad_hidden = jnp.dot(grad_rows, full_down, preferred_element_type=jnp.float32)
    grad_pre = gelu_back(grad_hidden)[0].astype(jnp.bfloat16)
    grad_arrived = contract_last(grad_pre, full_up).astype(jnp.bfloat16)
    grad_sent = lax.all_to_all(
        grad_arrived.reshape(-1, capacity, model_width),
        "dp",
        split_axis=0,
        concat_axis=0,
        tiled=True,
    ).reshape(experts * capacity, model_width)
    hidden_b = hidden.astype(jnp.bfloat16)
    grad_down = contract_first(grad_rows, hidden_b)
    grad_up = contract_first(arrived, grad_pre)
    grad_up_shard, grad_down_shard = (
        lax.psum_scatter(
            grad_up[None].astype(jnp.bfloat16), "seq", scatter_dimension=2, tiled=True
        ).astype(jnp.float32),
        lax.psum_scatter(
            grad_down[None].astype(jnp.bfloat16), "seq", scatter_dimension=2, tiled=True
        ).astype(jnp.float32),
    )
    grad_logits = grad_gate[:, None] * router_p * (choose_f - gate_prob[:, None])
    normed_f32 = normed_f.astype(jnp.float32)
    grad_router = jnp.dot(normed_f32.T, grad_logits, precision=highest)
    grad_normed = jnp.take(grad_sent, place_ids, axis=0).astype(jnp.float32) + jnp.dot(
        grad_logits, back_router.astype(jnp.float32).T, precision=highest
    )
    grad_part_f, grad_gain_f = norm_back(
        hidden_attn, scale_f, back_gf.astype(jnp.float32), grad_normed
    )
    grad_hidden_attn = upstream + grad_part_f
    grad_attn = grad_hidden_attn.astype(jnp.bfloat16)
    grad_wo = contract_first(context, grad_attn)
    grad_ctx = contract_last(grad_attn, back_out).astype(jnp.bfloat16)
    grad_ctx_h = grad_ctx.reshape(seq_count, local_len, head_count, head_size)
    again_scores = attn_scores(query_h, key_h, bias_q)
    again_probs = jnp.exp(again_scores - log_total[..., None])
    grad_probs = jnp.einsum(
        "bihd,bjhd->bhij", grad_ctx_h, value_h, preferred_element_type=jnp.float32
    )
    row_delta = jnp.sum(again_probs * grad_probs, axis=-1)
    grad_scores = (again_probs * (grad_probs - row_delta[..., None])).astype(jnp.bfloat16)
    grad_q = jnp.einsum("bhij,bjhd->bihd", grad_scores, key_h, preferred_element_type=jnp.float32)
    grad_q = grad_q.astype(jnp.bfloat16).reshape(tok_count, inner_width)
    grad_bias = table_grad(
        jnp.sum(grad_scores.astype(jnp.float32), axis=0), rel_bucket, start_q, bucket_count
    )
    grad_k_all = jnp.einsum(
        "bhij,bihd->bjhd", grad_scores, query_h, preferred_element_type=jnp.float32
    )
    grad_v_all = jnp.einsum(
        "bhij,bihd->bjhd",
        again_probs.astype(jnp.bfloat16),
        grad_ctx_h,
        preferred_element_type=jnp.float32,
    )
    grad_keys, grad_values = (
        lax.psum_scatter(
            grad_k_all.reshape(seq_count, length, inner_width),
            "seq",
            scatter_dimension=1,
            tiled=True,
        ),
        lax.psum_scatter(
            grad_v_all.reshape(seq_count, length, inner_width),
            "seq",
            scatter_dimension=1,
            tiled=True,
        ),
    )
    grad_k = grad_keys.astype(jnp.bfloat16).reshape(tok_count, inner_width)
    grad_v = grad_values.astype(jnp.bfloat16).reshape(tok_count, inner_width)
    grad_joined = jnp.concatenate([grad_q, grad_k, grad_v], axis=1)
    merged_back = jnp.concatenate([back_query, back_key, back_value], axis=1)
    grad_w_joined = contract_first(normed_a, grad_joined)
    grad_normed_a = contract_last(grad_joined, merged_back)
    grad_part_a, grad_gain_a = norm_back(
        inputs, scale_a, back_ga.astype(jnp.float32), grad_normed_a
    )
    grad_tokens = (grad_hidden_attn + grad_part_a).reshape(seq_count, local_len, model_width)
    table_tiled = jnp.tile(grad_bias, (lax.axis_size("dp"), 1))
    summed = (
        lax.psum_scatter(grad_gain_a, ("dp", "seq"), scatter_dimension=0, tiled=True),
        lax.psum_scatter(grad_gain_f, ("dp", "seq"), scatter_dimension=0, tiled=True),
        lax.psum_scatter(
            grad_w_joined[:, :inner_width], ("dp", "seq"), scatter_dimension=0, tiled=True
        ),
        lax.psum_scatter(
            grad_w_joined[:, inner_width : 2 * inner_width],
            ("dp", "seq"),
            scatter_dimension=0,
            tiled=True,
        ),
        lax.psum_scatter(
            grad_w_joined[:, 2 * inner_width :], ("dp", "seq"), scatter_dimension=0, tiled=True
        ),
        lax.psum_scatter(grad_wo, ("dp", "seq"), scatter_dimension=1, tiled=True),
        lax.psum_scatter(grad_router, ("dp", "seq"), scatter_dimension=0, tiled=True),
        lax.psum_scatter(table_tiled, ("dp", "seq"), scatter_dimension=0, tiled=True),
    )
    return (
        mixed,
        grad_tokens,
        summed[0],
        summed[2],
        summed[3],
        summed[4],
        summed[5],
        summed[7],
        summed[1],
        summed[6],
        grad_up_shard,
        grad_down_shard,
    )


def solution(mesh):
    placed = (
        P("dp", "seq", None),
        P("dp", "seq", None),
        P(("dp", "seq")),
        P(("dp", "seq"), None),
        P(("dp", "seq"), None),
        P(("dp", "seq"), None),
        P(None, ("dp", "seq")),
        P("seq", None),
        P(),
        P(("dp", "seq")),
        P(("dp", "seq"), None),
        P("dp", "seq", None, None),
        P("dp", None, "seq"),
        P("dp", None, "seq"),
    )
    return jax.shard_map(
        local,
        mesh=mesh,
        in_specs=placed,
        out_specs=(
            P("dp", "seq", None),
            P("dp", "seq", None),
            P(("dp", "seq")),
            P(("dp", "seq"), None),
            P(("dp", "seq"), None),
            P(("dp", "seq"), None),
            P(None, ("dp", "seq")),
            P("seq", None),
            P(("dp", "seq")),
            P(("dp", "seq"), None),
            P("dp", None, "seq"),
            P("dp", None, "seq"),
        ),
        check_vma=False,
    )
```

profile of v0, /device:TPU:0, one launch (start us, length us, event | category | flops | bytes accessed | tf_op | source)
XLA Modules:
  0.0 1450.0 jit_solution(9034913648357177117)
XLA Ops:
  11.2 42.1 %all-reduce.10 = (bf16[768]{0:T(1024)(128)(2,1)S(1)}, bf16[768]{0:T(1024)(128)(2,1)S(1)}) all-reduce(bf16[768]{0:T(1024)(128)(2,1)S(1)} %dynamic-update-slice, bf16[768]{0:T(1024)(128)(2,1)S(1)} %dynamic-update-slice.1), channel_id=1, replica_groups=mesh['dp'=4,'seq'=8] {'dp','seq'}, use_global_device_ids=true, to_apply=%add.3 | all-reduce | flops 1536 | bytes 6144
  55.0 12.9 all-gather.13.cloned.1.call-done
  70.4 53.5 %all-gather.15.cloned.1.call-done = bf16[768,768]{1,0:T(8,128)(2,1)} async-done(((bf16[24,768]{1,0:T(8,128)(2,1)}), bf16[768,768]{1,0:T(8,128)(2,1)}) %all-gather.15.cloned.1.call-update) | async-done | bytes 1179664 | tf_op jit(solution)/shard_map/all_gather | solution.py:104
  126.3 53.6 %all-gather.17.cloned.1.call-done = bf16[768,768]{1,0:T(8,128)(2,1)} async-done(((bf16[24,768]{1,0:T(8,128)(2,1)}), bf16[768,768]{1,0:T(8,128)(2,1)}) %all-gather.17.cloned.1.call-update) | async-done | bytes 1179664 | tf_op jit(solution)/shard_map/all_gather | solution.py:105
  190.7 19.5 %all-gather.2 = bf16[8,4,12]{2,1,0:T(4,128)(2,1)S(1)} all-gather(bf16[1,4,12]{2,1,0:T(4,128)(2,1)S(1)} %bitcast.195), channel_id=1, replica_groups=mesh['dp'=4,'seq'=8] {'seq'}, dimensions={0}, use_global_device_ids=true | all-gather | bytes 864 | tf_op jit(solution)/shard_map/all_gather | solution.py:126
  210.2 63.8 %all-gather.3 = bf16[32,24,4]{1,2,0:T(4,128)(2,1)S(1)} all-gather(bf16[1,24,4]{1,2,0:T(4,128)(2,1)S(1)} %bitcast.196), channel_id=1, replica_groups=mesh['dp'=4,'seq'=8] {'dp','seq'}, dimensions={0}, use_global_device_ids=true | all-gather | bytes 6336 | tf_op jit(solution)/shard_map/all_gather | solution.py:107
  286.8 57.2 %copy.70 = bf16[2,8,256,2304]{3,1,2,0:T(8,128)(2,1)S(1)} copy(bf16[2,8,256,2304]{3,2,1,0:T(8,128)(2,1)S(1)} %bitcast.156) | data formatting | bytes 37748736
  351.3 57.7 %reshape.297 = bf16[12,256,2303]{2,1,0:T(8,128)(2,1)} reshape(bf16[12,589568]{1,0:T(8,128)(2,1)} %slice.47) | data formatting | bytes 28299264 | tf_op jit(solution)/shard_map/reshape | solution.py:40
  419.4 15.1 %fusion.90 = (f32[12,256]{1,0:T(8,128)S(1)}, f32[12,256,2048]{2,1,0:T(8,128)}) fusion(bf16[12,256,2303]{2,1,0:T(8,128)(2,1)} %reshape.297, bf16[256,12,64]{0,2,1:T(8,128)(2,1)} %bitcast.171, bf16[2048,12,64]{0,2,1:T(8,128)(2,1)S(1)} %bitcast.162), kind=kOutput, calls=%fused_computation.145 | convolution fusion | flops 824177664 | bytes 41299968 | tf_op jit(solution)/shard_map/bihd,bjhd->bhij/dot_general | solution.py:71
  434.5 10.6 fusion
  445.8 10.9 fusion.31
  487.9 38.9 %all-gather.23.cloned.1.call-done = bf16[1,768,3072]{2,1,0:T(8,128)(2,1)} async-done(((bf16[1,768,384]{2,1,0:T(8,128)(2,1)}), bf16[1,768,3072]{2,1,0:T(8,128)(2,1)}) %all-gather.23.cloned.1.call-update) | async-done | bytes 4718608 | tf_op jit(solution)/shard_map/all_gather | solution.py:177
  526.8 8.8 fusion.28
  539.2 9.1 fusion.12
  562.4 8.6 all-to-all-done.3
  579.1 13.1 fusion.2
  594.0 17.2 %multiply_reduce_fusion = (f32[12,256]{1,0:T(8,128)}, f32[12,256,2048]{2,1,0:T(8,128)}) fusion(f32[12,256,2048]{2,1,0:T(8,128)} %get-tuple-element.38, f32[12,256]{1,0:T(8,128)S(1)} %log_add_fusion, bf16[256,12,64]{0,2,1:T(8,128)(2,1)} %bitcast.174, bf16[2048,12,64]{0,2,1:T(8,128)(2,1)S(1)} %bitcast.170), kind=kOutput, calls=%fused_computation.5 | convolution fusion | flops 824177664 | bytes 53895168 | tf_op jit(solution)/shard_map/bihd,bjhd->bhij/dot_general | solution.py:259
  611.2 17.7 %multiply_convert_fusion = bf16[12,256,2048]{2,1,0:T(8,128)(2,1)S(1)} fusion(f32[12,256,2048]{2,1,0:T(8,128)} %get-tuple-element.45, f32[12,256,2048]{2,1,0:T(8,128)} %get-tuple-element.38, f32[12,256]{1,0:T(8,128)} %get-tuple-element.44, f32[12,256]{1,0:T(8,128)S(1)} %log_add_fusion), kind=kLoop, calls=%fused_computation.4 | loop fusion | flops 25165824 | bytes 62939136 | tf_op jit(solution)/shard_map/convert_element_type | solution.py:263
  642.7 20.6 %copy.64 = bf16[1,768,3072]{1,0,2:T(2,128)(2,1)} copy(bf16[1,768,3072]{2,1,0:T(8,128)(2,1)} %fusion.21) | data formatting | bytes 9437184
  678.0 20.7 %copy.66 = bf16[1,768,3072]{1,0,2:T(2,128)(2,1)} copy(bf16[1,768,3072]{2,1,0:T(8,128)(2,1)} %fusion.22) | data formatting | bytes 9437184
  709.0 9.3 convolution_convert_fusion.5
  719.4 109.5 %reduce-scatter.14.cloned.1.call-done = f32[1,256,768]{1,2,0:T(8,128)} async-done(((f32[1,2048,768]{1,2,0:T(8,128)}), f32[1,256,768]{1,2,0:T(8,128)}) %reduce-scatter.14.cloned.1.call-update) | async-done | bytes 786448 | tf_op jit(solution)/shard_map/reduce_scatter | solution.py:279
  845.3 12.2 copy.72
  857.4 20.8 %pad_convert_fusion = f32[12,590080]{1,0:T(8,128)} fusion(bf16[12,589824]{1,0:T(8,128)(2,1)} %bitcast.157), kind=kLoop, calls=%fused_computation.12 | loop fusion | flops 7080960 | bytes 42479616 | tf_op jit(solution)/shard_map/reshape | solution.py:49
  878.2 70.9 %reshape.322 = f32[12,256,2305]{2,1,0:T(8,128)} reshape(f32[12,590080]{1,0:T(8,128)} %pad_convert_fusion) | data formatting | bytes 56647680 | tf_op jit(solution)/shard_map/reshape | solution.py:49
  949.2 11.3 reduce_sum.135
  967.0 58.5 %reduce-scatter.28.cloned.1.call-done = bf16[384,768]{1,0:T(8,128)(2,1)} async-done(((bf16[3072,768]{1,0:T(8,128)(2,1)}), bf16[384,768]{1,0:T(8,128)(2,1)}) %reduce-scatter.28.cloned.1.call-update) | async-done | bytes 589840
  1033.6 41.3 %all-reduce.9 = (f32[768]{0:T(1024)S(1)}, f32[128,12]{1,0:T(8,128)S(1)}, f32[768]{0:T(1024)S(1)}, f32[768,4]{0,1:T(4,128)S(1)}) all-reduce(f32[768]{0:T(1024)S(1)} %get-tuple-element.15, f32[128,12]{1,0:T(8,128)S(1)} %bitcast.185, f32[768]{0:T(1024)S(1)} %copy-done.44, ...), channel_id=6, replica_groups=mesh['dp'=4,'seq'=8] {'dp','seq'}, use_global_device_ids=true, to_apply=%region_19.21.clone | all-reduce | flops 6144 | bytes 49152
  1078.4 51.7 %reduce-scatter.24.cloned.1.call-done = f32[768,24]{0,1:T(8,128)} async-done(((f32[768,768]{0,1:T(8,128)}), f32[768,24]{0,1:T(8,128)}) %reduce-scatter.24.cloned.1.call-update) | async-done | bytes 73744 | tf_op jit(solution)/shard_map/reduce_scatter | solution.py:318
  1130.2 104.6 %reduce-scatter.22.cloned.1.call-done = f32[24,768]{1,0:T(8,128)} async-done(((f32[768,768]{1,0:T(8,128)}), f32[24,768]{1,0:T(8,128)}) %reduce-scatter.22.cloned.1.call-update) | async-done | bytes 73744 | tf_op jit(solution)/shard_map/reduce_scatter | solution.py:315
  1234.8 103.8 %reduce-scatter.20.cloned.1.call-done = f32[24,768]{1,0:T(8,128)} async-done(((f32[768,768]{1,0:T(8,128)}), f32[24,768]{1,0:T(8,128)}) %reduce-scatter.20.cloned.1.call-update) | async-done | bytes 73744 | tf_op jit(solution)/shard_map/reduce_scatter | solution.py:309
  1338.6 104.6 %reduce-scatter.18.cloned.1.call-done = f32[24,768]{1,0:T(8,128)} async-done(((f32[768,768]{1,0:T(8,128)}), f32[24,768]{1,0:T(8,128)}) %reduce-scatter.18.cloned.1.call-update) | async-done | bytes 73744 | tf_op jit(solution)/shard_map/reduce_scatter | solution.py:306
  (246 shorter events, 184.9 us)
Async XLA Ops:
  7.2 175.2 %copy-start.7 = (bf16[1,256,768]{2,1,0:T(8,128)(2,1)S(1)}, bf16[1,256,768]{2,1,0:T(8,128)(2,1)}, u32[]{:S(2)}) copy-start(bf16[1,256,768]{2,1,0:T(8,128)(2,1)} %param.16) | copy-start | bytes 1179652
  7.2 60.7 %all-gather.13.cloned.1.call-start = ((), (), s32[]{:S(2)}) async-start(), calls=%async_computation.12 | async-start | bytes 1216512 | tf_op jit(solution)/shard_map/all_gather | solution.py:103
  7.9 116.0 %all-gather.15.cloned.1.call-start = ((), (), s32[]{:S(2)}) async-start(), calls=%async_computation.13 | async-start | bytes 1216512 | tf_op jit(solution)/shard_map/all_gather | solution.py:104
  8.7 171.2 %all-gather.17.cloned.1.call-start = ((), (), s32[]{:S(2)}) async-start(), calls=%async_computation.14 | async-start | bytes 1216512 | tf_op jit(solution)/shard_map/all_gather | solution.py:105
  9.4 401.2 %all-gather.27.cloned.1.call-start = ((), (), s32[]{:S(2)}) async-start(), calls=%async_computation.25 | async-start | bytes 3538944 | tf_op jit(solution)/shard_map/all_gather | solution.py:120
  53.2 129.1 %copy-start.20 = (f32[768]{0:T(1024)}, f32[768]{0:T(1024)S(1)}, u32[]{:S(2)}) copy-start(f32[768]{0:T(1024)S(1)} %convert_element_type.143) | copy-start | bytes 9220
  55.0 130.5 %copy-start.40 = (f32[256]{0:T(256)}, f32[256]{0:T(256)S(1)}, u32[]{:S(2)}) copy-start(f32[256]{0:T(256)S(1)} %get-tuple-element.34) | copy-start | bytes 3076
  126.3 62.9 %copy-start.31 = (s32[1,1,256,1]{2,3,1,0:T(1,128)S(1)}, s32[1,1,256,1]{2,3,1,0:T(1,128)}, u32[]{:S(2)}) copy-start(s32[1,1,256,1]{2,3,1,0:T(1,128)} %param.27) | copy-start | bytes 3076
  126.3 64.4 %copy-start.55 = (bf16[4,12]{1,0:T(4,128)(2,1)S(1)}, bf16[4,12]{1,0:T(4,128)(2,1)}, u32[]{:S(2)}) copy-start(bf16[4,12]{1,0:T(4,128)(2,1)} %param.23) | copy-start | bytes 292
  126.3 83.9 %copy-start.56 = (bf16[24,4]{0,1:T(4,128)(2,1)S(1)}, bf16[24,4]{0,1:T(4,128)(2,1)}, u32[]{:S(2)}) copy-start(bf16[24,4]{0,1:T(4,128)(2,1)} %param.26) | copy-start | bytes 580
  126.3 147.8 %copy-start.46 = (s32[4095]{0:T(1024)S(1)}, s32[4095]{0:T(1024)}, u32[]{:S(2)}) copy-start(s32[4095]{0:T(1024)} %param.24) | copy-start | bytes 49144
  186.5 227.4 %all-gather.25.cloned.1.call-start = ((), (), s32[]{:S(2)}) async-start(), calls=%async_computation.24 | async-start | bytes 3538944 | tf_op jit(solution)/shard_map/all_gather | solution.py:123
  187.1 269.7 %all-gather.19.cloned.1.call-start = ((), (), s32[]{:S(2)}) async-start(), calls=%async_computation.15 | async-start | bytes 1216512 | tf_op jit(solution)/shard_map/all_gather | solution.py:106
  187.6 293.4 %all-gather.21.cloned.1.call-start = ((), (), s32[]{:S(2)}) async-start(), calls=%async_computation.16 | async-start | bytes 5308416 | tf_op jit(solution)/shard_map/all_gather | solution.py:176
  188.4 338.5 %all-gather.23.cloned.1.call-start = ((), (), s32[]{:S(2)}) async-start(), calls=%async_computation.17 | async-start | bytes 5308416 | tf_op jit(solution)/shard_map/all_gather | solution.py:177
  189.1 276.5 %copy-start.26 = (f32[768]{0:T(1024)}, f32[768]{0:T(1024)S(1)}, u32[]{:S(2)}) copy-start(f32[768]{0:T(1024)S(1)} %convert_element_type.151) | copy-start | bytes 9220
  274.1 191.8 %copy-start.30 = (bf16[768,4]{0,1:T(4,128)(2,1)}, bf16[768,4]{0,1:T(4,128)(2,1)S(1)}, u32[]{:S(2)}) copy-start(bf16[768,4]{0,1:T(4,128)(2,1)S(1)} %reshape.368) | copy-start | bytes 18436
  462.2 15.1 %all-to-all-start = ((bf16[4,128,768]{2,1,0:T(8,128)(2,1)}), bf16[4,128,768]{2,1,0:T(8,128)(2,1)S(1)}, u32[]{:S(2)}, u32[]{:S(2)}) async-start(bf16[4,128,768]{2,1,0:T(8,128)(2,1)} %bitcast.19), calls=%async_computation | async-start | bytes 1572864 | tf_op jit(solution)/shard_map/all_to_all | solution.py:166
  477.3 58.4 %all-to-all-start.2 = ((bf16[4,128,768]{2,1,0:T(8,128)(2,1)}), bf16[4,128,768]{2,1,0:T(8,128)(2,1)S(1)}, u32[]{:S(2)}, u32[]{:S(2)}) async-start(bf16[4,128,768]{2,1,0:T(8,128)(2,1)} %bitcast.28), calls=%async_computation.2 | async-start | bytes 1572864 | tf_op jit(solution)/shard_map/all_to_all | solution.py:208
  535.7 20.3 %all-to-all-start.1 = ((bf16[4,128,768]{2,1,0:T(8,128)(2,1)}), bf16[4,128,768]{2,1,0:T(8,128)(2,1)S(1)}, u32[]{:S(2)}, u32[]{:S(2)}) async-start(bf16[4,128,768]{2,1,0:T(8,128)(2,1)} %bitcast.184), calls=%async_computation.1 | async-start | bytes 1572864 | tf_op jit(solution)/shard_map/all_to_all | solution.py:180
  556.0 15.1 %all-to-all-start.3 = ((bf16[4,128,768]{2,1,0:T(8,128)(2,1)}), bf16[4,128,768]{2,1,0:T(8,128)(2,1)S(1)}, u32[]{:S(2)}, u32[]{:S(2)}) async-start(bf16[4,128,768]{2,1,0:T(8,128)(2,1)} %bitcast.183), calls=%async_computation.3 | async-start | bytes 1572864 | tf_op jit(solution)/shard_map/all_to_all | solution.py:225
  559.5 158.8 %reduce-scatter.16.cloned.1.call-start = ((), (), s32[]{:S(2)}) async-start(), calls=%async_computation.19 | async-start | bytes 7077888 | tf_op jit(solution)/shard_map/reduce_scatter | solution.py:285
  592.1 236.8 %reduce-scatter.14.cloned.1.call-start = ((), (), s32[]{:S(2)}) async-start(), calls=%async_computation.18 | async-start | bytes 7077888 | tf_op jit(solution)/shard_map/reduce_scatter | solution.py:279
  635.4 327.2 %reduce-scatter.26.cloned.1.call-start = ((), (), s32[]{:S(2)}) async-start(), calls=%async_computation.26 | async-start | bytes 5308416
  670.1 355.5 %reduce-scatter.28.cloned.1.call-start = ((), (), s32[]{:S(2)}) async-start(), calls=%async_computation.27 | async-start | bytes 5308416
  705.4 424.7 %reduce-scatter.24.cloned.1.call-start = ((), (), s32[]{:S(2)}) async-start(), calls=%async_computation.23 | async-start | bytes 2433024 | tf_op jit(solution)/shard_map/reduce_scatter | solution.py:318
  708.9 122.0 %copy-start.21 = (f32[768]{0:T(1024)S(1)}, f32[768]{0:T(1024)}, u32[]{:S(2)}) copy-start(f32[768]{0:T(1024)} %copy-done.20) | copy-start | bytes 9220
  708.9 122.0 %copy-start.41 = (f32[256]{0:T(256)S(1)}, f32[256]{0:T(256)}, u32[]{:S(2)}) copy-start(f32[256]{0:T(256)} %copy-done.40) | copy-start | bytes 3076
  708.9 525.9 %reduce-scatter.22.cloned.1.call-start = ((), (), s32[]{:S(2)}) async-start(), calls=%async_computation.22 | async-start | bytes 2433024 | tf_op jit(solution)/shard_map/reduce_scatter | solution.py:315
  836.3 502.3 %reduce-scatter.20.cloned.1.call-start = ((), (), s32[]{:S(2)}) async-start(), calls=%async_computation.21 | async-start | bytes 2433024 | tf_op jit(solution)/shard_map/reduce_scatter | solution.py:309
  836.9 606.3 %reduce-scatter.18.cloned.1.call-start = ((), (), s32[]{:S(2)}) async-start(), calls=%async_computation.20 | async-start | bytes 2433024 | tf_op jit(solution)/shard_map/reduce_scatter | solution.py:306
  1027.3 50.1 %copy-start.6 = (f32[256,768]{1,0:T(8,128)S(1)}, f32[256,768]{1,0:T(8,128)}, u32[]{:S(2)}) copy-start(f32[256,768]{1,0:T(8,128)} %copy-done.5) | copy-start | bytes 2359300
  (46 other events, 494.3 us)
Sparse Core Ops, SparseCore 0:
  10.9 56.8 all-gather.12
  70.8 53.0 all-gather.14
  126.8 53.0 all-gather.16
  186.6 59.6 all-gather.26
  248.8 59.0 all-gather.24
  310.7 52.6 all-gather.18
  365.5 79.9 all-gather.20
  447.6 79.2 all-gather.22
  592.3 115.6 reduce-scatter.15
  711.4 117.4 reduce-scatter.13
  832.6 94.3 reduce-scatter.25
  930.5 94.9 reduce-scatter.27
  1031.4 98.7 reduce-scatter.23
  1136.7 98.0 reduce-scatter.21
  1240.5 98.0 reduce-scatter.19
  1345.1 97.9 reduce-scatter.17
where the time goes:
time: 1460 us; the launch traced here: 1450 us
  waiting for transfers between devices  714 us (49%)
  local copies, waits for them, and re-layouts  324 us (22%)
  blocking collectives  167 us (11%)
  matrix products  135 us (9%)
  other arithmetic  79.4 us (5%)
  starting transfers between devices  15.4 us (1%)
  between operations  15.2 us (1%)
    unnamed x139, local copies, waits for them, and re-layouts  156 us
    reduce_scatter x1, waiting for transfers between devices, local(): lax.psum_scatter(grad_k_all.reshape(seq_count, length, inner_width), 'seq...  110 us
    reduce_scatter x1, waiting for transfers between devices, local(): lax.psum_scatter(grad_w_joined[:, 2 * inner_width:], ('dp', 'seq'), scatt...  105 us
    reduce_scatter x1, waiting for transfers between devices, local(): lax.psum_scatter(grad_w_joined[:, :inner_width], ('dp', 'seq'), scatter_d...  105 us
    reduce_scatter x1, waiting for transfers between devices, local(): lax.psum_scatter(grad_w_joined[:, inner_width:2 * inner_width], ('dp', 's...  104 us
    unnamed x2, blocking collectives  83.4 us
    reshape x1, local copies, waits for them, and re-layouts, table_grad(): flat.reshape(head_count, row_count, row_count + col_count + 1)  70.9 us
    all_gather x1, blocking collectives, local(): lax.all_gather(router_w, ('dp', 'seq'), axis=0, tiled=True)  63.8 us
  transfers between devices with their start and end apart: 20, of which 12 were waited for; matrix products, arithmetic and copies ran while one was open for 35% of the time, Pallas kernels for 0%

commit v1 on v0

v1 whole, which is shorter than its diff:
```python
import math
from functools import partial

import jax
import jax.numpy as jnp
from jax import lax
from jax.experimental import pallas as pl
from jax.experimental.pallas import tpu as pltpu
from jax.sharding import PartitionSpec as P

epsilon = 1e-06
highest = lax.Precision.HIGHEST
bf16 = jnp.bfloat16
f32 = jnp.float32
VMEM = 56 * 1024 * 1024


def dot_nn(left, right):
    return lax.dot_general(left, right, (((1,), (0,)), ((), ())), preferred_element_type=f32)


def dot_tn(left, right):
    return lax.dot_general(left, right, (((0,), (0,)), ((), ())), preferred_element_type=f32)


def dot_nt(left, right):
    return lax.dot_general(left, right, (((1,), (1,)), ((), ())), preferred_element_type=f32)


def swap(value, axis, mask):
    size = lax.axis_size(axis)
    return lax.ppermute(value, axis, [(i, i ^ mask) for i in range(size)])


def bits_of(size):
    return [1 << i for i in range(size.bit_length() - 1)]


def unxor(parts, index):
    for bit in bits_of(len(parts)):
        flag = (index & bit) != 0
        parts = [jnp.where(flag, parts[j ^ bit], parts[j]) for j in range(len(parts))]
    return parts


def grow(value, axis, mask, bit_set):
    other = swap(value, axis, mask)
    return jnp.stack([jnp.where(bit_set, other, value), jnp.where(bit_set, value, other)])


def pick(value, position, flag):
    low = lax.index_in_dim(value, 0, position, keepdims=False)
    high = lax.index_in_dim(value, 1, position, keepdims=False)
    return jnp.where(flag, high, low)


def halve(value, position, axis, mask, bit_set):
    sent = pick(value, position, jnp.logical_not(bit_set))
    kept = pick(value, position, bit_set)
    got = swap(sent, axis, mask)
    return (kept.astype(f32) + got.astype(f32)).astype(bf16)


def bias_tile(vec_ref, tile_ref, head):
    rows, width = tile_ref.shape
    vec = jnp.broadcast_to(vec_ref[pl.ds(head, 1), :], (rows, width))
    tile_ref[...] = pltpu.roll(vec, width - (rows - 1), 1, stride=1, stride_axis=0)


def key_columns(pos_ref, dims, query_z):
    n_z, n_y, local_len = dims
    z, y = pos_ref[0], pos_ref[1]
    query_block = (z ^ query_z) * n_y + y
    columns = []
    for key_y in range(n_y):
        for key_z in range(n_z):
            key_block = (z ^ key_z) * n_y + (y ^ key_y)
            first = (n_z * n_y - 1 - query_block + key_block) * local_len
            columns.append(pl.ds(pl.multiple_of(first, local_len), local_len))
    return columns


def split_keys(dims, seq_count, heads, size, kv_refs, offset, plain_ref, turned_ref):
    n_z, n_y, local_len = dims
    for head in range(heads):
        lo, hi = offset + head * size, offset + (head + 1) * size
        for s in range(seq_count):
            index = head * seq_count + s
            for key_y in range(n_y):
                for key_z in range(n_z):
                    at = (key_z * seq_count + s) * local_len
                    to = (key_y * n_z + key_z) * local_len
                    block = kv_refs[key_y][at : at + local_len, lo:hi]
                    if plain_ref is not None:
                        plain_ref[index, to : to + local_len, :] = block
                    if turned_ref is not None:
                        turned_ref[index, :, to : to + local_len] = block.T


def attn_fwd_kernel(dims, seq_count, heads, size, pos_ref, vec_ref, q_ref, *refs):
    n_z, n_y, local_len = dims
    kv_refs, (c_ref, lse_ref, tile_ref, kt_ref, v_ref, qh_ref, ch_ref) = refs[:n_y], refs[n_y:]
    inner = heads * size
    split_keys(dims, seq_count, heads, size, kv_refs, 0, None, kt_ref)
    split_keys(dims, seq_count, heads, size, kv_refs, inner, v_ref, None)
    for head in range(heads):
        qh_ref[head] = q_ref[:, head * size : (head + 1) * size]

    def head_step(head, carry):
        bias_tile(vec_ref, tile_ref, head)

        def query_step(query_z, carry):
            columns = key_columns(pos_ref, dims, query_z)
            for s in range(seq_count):
                row = pl.multiple_of((query_z * seq_count + s) * local_len, local_len)
                rows = pl.ds(row, local_len)
                bias = jnp.concatenate([tile_ref[:, c] for c in columns], axis=1)
                score = dot_nn(qh_ref[head, rows, :], kt_ref[head * seq_count + s]) + bias
                top = jnp.max(score, axis=1, keepdims=True)
                weight = jnp.exp(score - top)
                total = jnp.sum(weight, axis=1, keepdims=True)
                out = dot_nn(weight.astype(bf16), v_ref[head * seq_count + s])
                ch_ref[head, rows, :] = out / total
                lse_ref[head, rows, :] = top + jnp.log(total)
            return carry

        return lax.fori_loop(0, n_z, query_step, carry)

    lax.fori_loop(0, heads, head_step, 0)
    for head in range(heads):
        c_ref[:, head * size : (head + 1) * size] = ch_ref[head].astype(bf16)


def attn_bwd_kernel(dims, seq_count, heads, size, pos_ref, vec_ref, q_ref, dc_ref, lse_ref, *refs):
    n_z, n_y, local_len = dims
    kv_refs = refs[:n_y]
    dq_ref, diag_ref = refs[n_y], refs[n_y + 1]
    dkv_refs = refs[n_y + 2 : 2 * n_y + 2]
    refs = refs[2 * n_y + 2 :]
    tile_ref, grad_ref, kt_ref, vt_ref, k_ref, qh_ref, dch_ref, dqh_ref, dk_ref, dv_ref = refs
    inner = heads * size
    split_keys(dims, seq_count, heads, size, kv_refs, 0, k_ref, kt_ref)
    split_keys(dims, seq_count, heads, size, kv_refs, inner, None, vt_ref)
    for head in range(heads):
        qh_ref[head] = q_ref[:, head * size : (head + 1) * size]
        dch_ref[head] = dc_ref[:, head * size : (head + 1) * size]
    diag_ref[...] = jnp.zeros_like(diag_ref)
    dk_ref[...] = jnp.zeros_like(dk_ref)
    dv_ref[...] = jnp.zeros_like(dv_ref)

    def head_step(head, carry):
        bias_tile(vec_ref, tile_ref, head)
        grad_ref[...] = jnp.zeros_like(grad_ref)

        def query_step(query_z, carry):
            columns = key_columns(pos_ref, dims, query_z)
            for s in range(seq_count):
                index = head * seq_count + s
                row = pl.multiple_of((query_z * seq_count + s) * local_len, local_len)
                rows = pl.ds(row, local_len)
                q = qh_ref[head, rows, :]
                dc = dch_ref[head, rows, :]
                bias = jnp.concatenate([tile_ref[:, c] for c in columns], axis=1)
                prob = jnp.exp(dot_nn(q, kt_ref[index]) + bias - lse_ref[head, rows, :])
                dprob = dot_nn(dc, vt_ref[index])
                delta = jnp.sum(prob * dprob, axis=1, keepdims=True)
                ds = (prob * (dprob - delta)).astype(bf16)
                dqh_ref[head, rows, :] = dot_nn(ds, k_ref[index])
                dk_ref[index] += dot_tn(q, ds)
                dv_ref[index] += dot_tn(dc, prob.astype(bf16))
                for i, c in enumerate(columns):
                    part = ds[:, i * local_len : (i + 1) * local_len]
                    grad_ref[:, c] += part.astype(f32)
            return carry

        lax.fori_loop(0, n_z, query_step, 0)
        folded = grad_ref[...]
        width = folded.shape[1]
        while folded.shape[0] > 1:
            half = folded.shape[0] // 2
            folded = folded[:half] + pltpu.roll(folded[half:], width - half, 1)
        diag_ref[pl.ds(head, 1), :] = folded
        return carry

    lax.fori_loop(0, heads, head_step, 0)
    for head in range(heads):
        lo, hi = head * size, (head + 1) * size
        dq_ref[:, lo:hi] = dqh_ref[head].astype(bf16)
        for s in range(seq_count):
            index = head * seq_count + s
            for key_y in range(n_y):
                for key_z in range(n_z):
                    at = (key_z * seq_count + s) * local_len
                    to = (key_y * n_z + key_z) * local_len
                    out = dkv_refs[key_y]
                    cut = slice(to, to + local_len)
                    out[at : at + local_len, lo:hi] = dk_ref[index, :, cut].T.astype(out.dtype)
                    out[at : at + local_len, inner + lo : inner + hi] = dv_ref[
                        index, :, cut
                    ].T.astype(out.dtype)


def vmem_specs(count):
    return [pl.BlockSpec(memory_space=pltpu.VMEM) for _ in range(count)]


def attn_fwd(dims, seq_count, heads, size, pos, vec, q, kvs):
    rows = q.shape[0]
    length = dims[0] * dims[1] * dims[2]
    both = heads * seq_count
    return pl.pallas_call(
        partial(attn_fwd_kernel, dims, seq_count, heads, size),
        out_shape=(
            jax.ShapeDtypeStruct((rows, heads * size), bf16),
            jax.ShapeDtypeStruct((heads, rows, 1), f32),
        ),
        in_specs=[pl.BlockSpec(memory_space=pltpu.SMEM)] + vmem_specs(2 + len(kvs)),
        out_specs=tuple(vmem_specs(2)),
        scratch_shapes=[
            pltpu.VMEM((dims[2], vec.shape[1]), f32),
            pltpu.VMEM((both, size, length), bf16),
            pltpu.VMEM((both, length, size), bf16),
            pltpu.VMEM((heads, rows, size), bf16),
            pltpu.VMEM((heads, rows, size), f32),
        ],
        compiler_params=pltpu.CompilerParams(vmem_limit_bytes=VMEM),
        name="attn_fwd",
    )(pos, vec, q, *kvs)


def attn_bwd(dims, seq_count, heads, size, pos, vec, q, dc, lse, kvs):
    rows = q.shape[0]
    length = dims[0] * dims[1] * dims[2]
    both = heads * seq_count
    shapes = [jax.ShapeDtypeStruct((rows, heads * size), bf16), jax.ShapeDtypeStruct(vec.shape, f32)]
    for key_y in range(len(kvs)):
        shapes.append(jax.ShapeDtypeStruct(kvs[0].shape, f32 if key_y == 0 else bf16))
    return pl.pallas_call(
        partial(attn_bwd_kernel, dims, seq_count, heads, size),
        out_shape=tuple(shapes),
        in_specs=[pl.BlockSpec(memory_space=pltpu.SMEM)] + vmem_specs(4 + len(kvs)),
        out_specs=tuple(vmem_specs(len(shapes))),
        scratch_shapes=[
            pltpu.VMEM((dims[2], vec.shape[1]), f32),
            pltpu.VMEM((dims[2], vec.shape[1]), f32),
            pltpu.VMEM((both, size, length), bf16),
            pltpu.VMEM((both, size, length), bf16),
            pltpu.VMEM((both, length, size), bf16),
            pltpu.VMEM((heads, rows, size), bf16),
            pltpu.VMEM((heads, rows, size), bf16),
            pltpu.VMEM((heads, rows, size), f32),
            pltpu.VMEM((both, size, length), f32),
            pltpu.VMEM((both, size, length), f32),
        ],
        compiler_params=pltpu.CompilerParams(vmem_limit_bytes=VMEM),
        name="attn_bwd",
    )(pos, vec, q, dc, lse, *kvs)


def expert_kernel(rows_ref, dy_ref, up_ref, down_ref, y_ref, db_ref, g_ref, du_ref, y_acc, db_acc):
    step = pl.program_id(0)
    up = up_ref[0]
    down = down_ref[0]
    pre = dot_nn(rows_ref[...], up)
    square = pre * pre
    tanh = jnp.tanh(0.7978845608028654 * (pre + 0.044715 * pre * square))
    hidden = (0.5 * pre * (1.0 + tanh)).astype(bf16)
    slope = 0.5 * (1.0 + tanh) + 0.5 * pre * (1.0 - tanh * tanh) * (
        0.7978845608028654 * (1.0 + 0.134145 * square)
    )
    g_ref[0] = hidden
    y = dot_nt(hidden, down)
    du = (dot_nn(dy_ref[...], down) * slope).astype(bf16)
    du_ref[0] = du
    db = dot_nt(du, up)

    @pl.when(step == 0)
    def _():
        y_acc[...] = y
        db_acc[...] = db

    @pl.when(step > 0)
    def _():
        y_acc[...] += y
        db_acc[...] += db

    @pl.when(step == pl.num_programs(0) - 1)
    def _():
        y_ref[...] = y_acc[...].astype(bf16)
        db_ref[...] = db_acc[...].astype(bf16)


def expert_call(rows, dy, up, down):
    count, width = rows.shape
    n_z, _, hidden = up.shape
    whole = pl.BlockSpec((count, width), lambda i: (0, 0))
    weight = pl.BlockSpec((1, width, hidden), lambda i: (i, 0, 0))
    kept = pl.BlockSpec((1, count, hidden), lambda i: (i, 0, 0))
    return pl.pallas_call(
        expert_kernel,
        grid=(n_z,),
        out_shape=(
            jax.ShapeDtypeStruct((count, width), bf16),
            jax.ShapeDtypeStruct((count, width), bf16),
            jax.ShapeDtypeStruct((n_z, count, hidden), bf16),
            jax.ShapeDtypeStruct((n_z, count, hidden), bf16),
        ),
        in_specs=[whole, whole, weight, weight],
        out_specs=(whole, whole, kept, kept),
        scratch_shapes=[pltpu.VMEM((count, width), f32), pltpu.VMEM((count, width), f32)],
        compiler_params=pltpu.CompilerParams(vmem_limit_bytes=VMEM),
        name="expert",
    )(rows, dy, up, down)


def expert_grad_kernel(left_ref, right_ref, out_ref):
    out_ref[0] = dot_tn(left_ref[...], right_ref[0]).astype(bf16)


def expert_grad(left, right):
    count, width = left.shape
    n_z, _, hidden = right.shape
    return pl.pallas_call(
        expert_grad_kernel,
        grid=(n_z,),
        out_shape=jax.ShapeDtypeStruct((n_z, width, hidden), bf16),
        in_specs=[
            pl.BlockSpec((count, width), lambda i: (0, 0)),
            pl.BlockSpec((1, count, hidden), lambda i: (i, 0, 0)),
        ],
        out_specs=pl.BlockSpec((1, width, hidden), lambda i: (i, 0, 0)),
        compiler_params=pltpu.CompilerParams(vmem_limit_bytes=VMEM),
        name="expert_grad",
    )(left, right)


def local(
    tokens,
    cotangent,
    gain_attn,
    query_w,
    key_w,
    value_w,
    output_w,
    rel_table,
    rel_bucket,
    gain_ffn,
    router_w,
    routes,
    expert_in,
    expert_out,
):
    seq_count, local_len, width = tokens.shape
    tok = seq_count * local_len
    n_dp, n_seq = lax.axis_size("dp"), lax.axis_size("seq")
    head_count = rel_table.shape[1]
    inner = query_w.shape[1]
    size = inner // head_count
    n_z = math.gcd(head_count, n_seq)
    n_y = n_seq // n_z
    heads = head_count // n_z
    part = heads * size
    experts = router_w.shape[1]
    capacity = 2 * tok // experts
    table_rows = rel_table.shape[0]
    buckets = table_rows * n_seq
    w_rows = query_w.shape[0]
    dims = (n_z, n_y, local_len)
    dp, seq = lax.axis_index("dp"), lax.axis_index("seq")
    z, y = seq // n_y, seq % n_y
    dp_bits, y_bits, z_bits = bits_of(n_dp), bits_of(n_y), bits_of(n_z)

    def swap_z(value, k):
        return swap(value, "seq", k * n_y) if k else value

    def swap_y(value, k):
        return swap(value, "seq", k) if k else value

    def swap_dp(value, k):
        return swap(value, "dp", k) if k else value

    extra = jnp.concatenate([gain_attn[:, None], gain_ffn[:, None], router_w], axis=1)
    extra = jnp.broadcast_to(extra[None], (n_z, w_rows, 2 + experts))
    table_at = part * 3 + 2 + experts
    table = rel_table.reshape(table_rows, n_z, heads).transpose(1, 0, 2)
    table = jnp.pad(table, ((0, 0), (0, w_rows - table_rows), (0, 0)))
    joined = [w.reshape(w_rows, n_z, part).transpose(1, 0, 2) for w in (query_w, key_w, value_w)]
    pack = jnp.concatenate(joined + [extra, table], axis=2)
    packed = -(-pack.shape[2] // 128) * 128
    pack = jnp.pad(pack, ((0, 0), (0, 0), (0, packed - pack.shape[2])))
    by_partner = unxor([pack[j] for j in range(n_z)], z)
    gathered = jnp.stack(unxor([swap_z(by_partner[k], k) for k in range(n_z)], z))

    x_own = tokens.reshape(tok, width)
    x_parts = [swap_z(x_own, k) for k in range(n_z)]

    for bit in y_bits:
        gathered = grow(gathered, "seq", bit, (y & bit) != 0)
    for bit in reversed(dp_bits):
        gathered = grow(gathered, "dp", bit, (dp & bit) != 0)
    n_bits, m_bits = len(y_bits), len(dp_bits)
    order = tuple(reversed(range(m_bits))) + (m_bits + n_bits,)
    order = order + tuple(range(m_bits, m_bits + n_bits)) + (m_bits + n_bits + 1, m_bits + n_bits + 2)
    gathered = gathered.transpose(order).reshape(width, packed)
    w_qkv = gathered[:, : 3 * part]
    gain_a = gathered[:, 3 * part].astype(f32)
    gain_f = gathered[:, 3 * part + 1].astype(f32)
    w_router = gathered[:, 3 * part + 2 : 3 * part + 2 + experts]
    table = gathered.reshape(n_dp, n_seq, w_rows, packed)[0, :, :table_rows, table_at : table_at + heads]
    table = table.reshape(buckets, heads)

    out_t = output_w.T
    for bit in z_bits:
        out_t = grow(out_t, "seq", bit * n_y, (z & bit) != 0)
    for bit in y_bits:
        out_t = grow(out_t, "seq", bit, (y & bit) != 0)
    for bit in reversed(dp_bits):
        out_t = grow(out_t, "dp", bit, (dp & bit) != 0)
    l_bits = len(z_bits)
    order = tuple(reversed(range(m_bits)))
    order = order + tuple(range(m_bits + n_bits, m_bits + n_bits + l_bits))
    order = order + tuple(range(m_bits, m_bits + n_bits))
    order = order + (m_bits + n_bits + l_bits, m_bits + n_bits + l_bits + 1)
    out_t = out_t.transpose(order).reshape(width, inner)

    z_groups = [[j * n_y + i for j in range(n_z)] for i in range(n_y)]
    up = lax.all_gather(expert_in[0], "seq", axis=0, axis_index_groups=z_groups)
    down = lax.all_gather(expert_out[0], "seq", axis=0, axis_index_groups=z_groups)

    route_ids = routes.reshape(tok)
    choose = route_ids[:, None] == jnp.arange(experts, dtype=jnp.int32)[None, :]
    choose_f = choose.astype(f32)
    before = jnp.arange(tok)[:, None] > jnp.arange(tok)[None, :]
    earlier = dot_nn(before.astype(bf16), choose.astype(bf16))
    slot = jnp.sum(earlier * choose_f, axis=1).astype(jnp.int32)
    place = (route_ids ^ dp) * capacity + slot
    place_hot = jnp.arange(experts * capacity, dtype=jnp.int32)[:, None] == place[None, :]
    place_b = place_hot.astype(bf16)

    def to_experts(values):
        sent = dot_nn(place_b, values).astype(bf16).reshape(experts, capacity, width)
        got = [swap_dp(sent[k], k) for k in range(n_dp)]
        return [[swap_y(v, k) for v in got] for k in range(n_y)]

    def from_experts(values):
        split = values.reshape(n_y, n_dp * capacity, width)
        total = split[0].astype(f32)
        for k in range(1, n_y):
            total = total + swap_y(split[k], k).astype(f32)
        blocks = total.astype(bf16).reshape(n_dp, capacity, width)
        back = [swap_dp(blocks[k], k) for k in range(n_dp)]
        return dot_tn(place_b, jnp.concatenate(back, axis=0))

    upstream_b = cotangent.reshape(tok, width)
    upstream = upstream_b.astype(f32)
    d_rows = to_experts(upstream_b)

    x_all = jnp.concatenate(x_parts, axis=0).astype(f32)
    scale_all = lax.rsqrt(jnp.mean(x_all * x_all, axis=-1, keepdims=True) + epsilon)
    normed_all = (x_all * scale_all * gain_a).astype(bf16)
    kv = dot_nn(normed_all, w_qkv[:, part:]).astype(bf16)
    kvs = [swap_y(kv, k) for k in range(n_y)]
    q = dot_nn(normed_all, w_qkv[:, :part]).astype(bf16)
    span = 2 * n_seq * local_len
    bucket_pad = jnp.concatenate([rel_bucket, jnp.full((1,), -1, jnp.int32)])
    bucket_hot = bucket_pad[None, :] == jnp.arange(buckets, dtype=jnp.int32)[:, None]
    table_pad = jnp.pad(table, ((0, 0), (0, 8 - heads)))
    vec = dot_tn(table_pad, bucket_hot.astype(bf16))
    pos = jnp.stack([z, y]).astype(jnp.int32)
    context_parts, lse = attn_fwd(dims, seq_count, heads, size, pos, vec, q, kvs)
    context_parts = context_parts.reshape(n_z, tok, part)
    context = [swap_z(context_parts[k], k) for k in range(n_z)]
    context = jnp.concatenate(unxor(context, z), axis=1)

    inputs = x_own.astype(f32)
    hidden_attn = inputs + dot_nt(context, out_t)
    scale_f = lax.rsqrt(jnp.mean(hidden_attn * hidden_attn, axis=-1, keepdims=True) + epsilon)
    normed_f = (hidden_attn * scale_f * gain_f).astype(bf16)
    logits = dot_nn(normed_f, w_router)
    router_p = jax.nn.softmax(logits, axis=-1)
    gate = jnp.sum(router_p * choose_f, axis=-1)

    b_rows = to_experts(normed_f)
    gate_rows = jnp.sum(jnp.where(place_hot, gate[None, :], 0.0), axis=1).reshape(experts, capacity)
    gate_rows = jnp.concatenate([swap_dp(gate_rows[k], k) for k in range(n_dp)])
    gate_rows = jnp.concatenate([swap_y(gate_rows, k) for k in range(n_y)])
    rows = jnp.concatenate([v for group in b_rows for v in group], axis=0)
    dy = jnp.concatenate([v for group in d_rows for v in group], axis=0)
    dy = (dy.astype(f32) * gate_rows[:, None]).astype(bf16)
    y_part, db_part, hidden, grad_pre = expert_call(rows, dy, up, down)
    grad_normed = from_experts(db_part)
    expert_tok = from_experts(y_part)
    grad_up = expert_grad(rows, grad_pre)
    grad_down = expert_grad(dy, hidden)
    grad_up = lax.psum_scatter(
        grad_up, "seq", scatter_dimension=0, axis_index_groups=z_groups, tiled=True
    ).astype(f32)
    grad_down = lax.psum_scatter(
        grad_down, "seq", scatter_dimension=0, axis_index_groups=z_groups, tiled=True
    ).astype(f32)

    mixed = (hidden_attn + gate[:, None] * expert_tok).astype(bf16).reshape(tokens.shape)
    grad_gate = jnp.sum(upstream * expert_tok, axis=-1)
    grad_logits = grad_gate[:, None] * router_p * (choose_f - gate[:, None])
    grad_router = lax.dot_general(
        normed_f.astype(f32), grad_logits, (((0,), (0,)), ((), ())), precision=highest
    )
    grad_normed = grad_normed + lax.dot_general(
        grad_logits, w_router.astype(f32), (((1,), (1,)), ((), ())), precision=highest
    )
    scaled = gain_f * grad_normed
    grad_hidden = upstream + scale_f * scaled
    grad_hidden = grad_hidden - hidden_attn * scale_f**3 * jnp.mean(
        scaled * hidden_attn, axis=-1, keepdims=True
    )
    grad_gain_f = jnp.sum(grad_normed * hidden_attn * scale_f, axis=0)
    grad_attn = grad_hidden.astype(bf16)

    grad_ctx = dot_nn(grad_attn, out_t).astype(bf16)
    grad_ctx = unxor([grad_ctx[:, j * part : (j + 1) * part] for j in range(n_z)], z)
    grad_ctx = jnp.concatenate([swap_z(grad_ctx[k], k) for k in range(n_z)], axis=0)
    grad_q, diag, *grad_kvs = attn_bwd(
        dims, seq_count, heads, size, pos, vec, q, grad_ctx, lse, kvs
    )
    grad_kv = grad_kvs[0]
    for k in range(1, n_y):
        grad_kv = grad_kv + swap_y(grad_kvs[k], k).astype(f32)
    grad_qkv = jnp.concatenate([grad_q, grad_kv.astype(bf16)], axis=1)
    grad_a_part = dot_nt(grad_qkv, w_qkv)
    grad_a_parts = grad_a_part.reshape(n_z, tok, width)
    grad_a = grad_a_parts[0]
    for k in range(1, n_z):
        grad_a = grad_a + swap_z(grad_a_parts[k].astype(bf16), k).astype(f32)
    scale_a = scale_all[:tok]
    scaled_a = gain_a * grad_a
    grad_x = grad_hidden + scale_a * scaled_a
    grad_x = grad_x - inputs * scale_a**3 * jnp.mean(scaled_a * inputs, axis=-1, keepdims=True)
    grad_tokens = grad_x.reshape(tokens.shape)

    def scatter(value, z_halves):
        columns = value.shape[1]
        shape = (2,) * m_bits + ((2,) * l_bits if z_halves else (n_z,)) + (2,) * n_bits
        value = value.astype(bf16).reshape(shape + (w_rows, columns))
        axes = list(range(m_bits))
        for bit in dp_bits:
            value = halve(value, len(axes) - 1, "dp", bit, (dp & bit) != 0)
            axes.pop()
        z_axes = l_bits if z_halves else 1
        for i, bit in enumerate(y_bits):
            value = halve(value, z_axes + n_bits - 1 - i, "seq", bit, (y & bit) != 0)
        if z_halves:
            for i, bit in enumerate(z_bits):
                value = halve(value, l_bits - 1 - i, "seq", bit * n_y, (z & bit) != 0)
            return value
        parts = unxor([value[j] for j in range(n_z)], z)
        return unxor([swap_z(parts[k], k) for k in range(n_z)], z)

    grad_out_t = dot_tn(grad_attn, context)
    grad_f = jnp.concatenate([grad_gain_f[:, None], grad_router], axis=1)
    grad_f = jnp.pad(grad_f, ((0, 0), (0, 128 - grad_f.shape[1])))
    summed_f = scatter(jnp.concatenate([grad_out_t, grad_f], axis=1), True).astype(f32)
    grad_output = summed_f[:, :inner].T
    grad_gain_ffn = summed_f[:, inner]
    grad_router = summed_f[:, inner + 1 : inner + 1 + experts]

    grad_w = dot_tn(normed_all, grad_qkv)
    grad_gain_a = jnp.sum(grad_a_part * x_all * scale_all, axis=0)
    diag = jnp.roll(diag, local_len - 1, axis=1)
    grad_table = lax.dot_general(
        diag, bucket_hot.astype(f32), (((1,), (1,)), ((), ())), precision=highest
    )
    grad_table = grad_table[:heads].T.reshape(1, n_seq, table_rows, heads)
    grad_table = jnp.pad(grad_table, ((0, 0), (0, 0), (0, w_rows - table_rows), (0, 0)))
    grad_table = jnp.broadcast_to(grad_table, (n_dp, n_seq, w_rows, heads)).reshape(width, heads)
    grad_e = jnp.concatenate([grad_gain_a[:, None], grad_table], axis=1)
    grad_e = jnp.pad(grad_e, ((0, 0), (0, packed - 3 * part - grad_e.shape[1])))
    summed = scatter(jnp.concatenate([grad_w, grad_e], axis=1), False)
    grad_query, grad_key, grad_value = (
        jnp.concatenate([v[:, i * part : (i + 1) * part] for v in summed], axis=1).astype(f32)
        for i in range(3)
    )
    grad_gain_attn = sum(v[:, 3 * part].astype(f32) for v in summed)
    grad_table = jnp.concatenate(
        [v[:table_rows, 3 * part + 1 : 3 * part + 1 + heads] for v in summed], axis=1
    ).astype(f32)

    return (
        mixed,
        grad_tokens,
        grad_gain_attn,
        grad_query,
        grad_key,
        grad_value,
        grad_output,
        grad_table,
        grad_gain_ffn,
        grad_router,
        grad_up,
        grad_down,
    )


def solution(mesh):
    vector = P(("dp", "seq"))
    matrix = P(("dp", "seq"), None)
    rows = P("dp", "seq", None)
    expert = P("dp", None, "seq")
    last = P(None, ("dp", "seq"))
    table = P("seq", None)
    return jax.shard_map(
        local,
        mesh=mesh,
        in_specs=(
            rows,
            rows,
            vector,
            matrix,
            matrix,
            matrix,
            last,
            table,
            P(),
            vector,
            matrix,
            P("dp", "seq", None, None),
            expert,
            expert,
        ),
        out_specs=(
            rows,
            rows,
            vector,
            matrix,
            matrix,
            matrix,
            last,
            table,
            vector,
            matrix,
            expert,
            expert,
        ),
        check_vma=False,
    )
```

time: 1460 us -> 483 us (0.33)
  waiting for transfers between devices: 714 us -> 177 us
  local copies, waits for them, and re-layouts: 324 us -> 24.1 us
  blocking collectives: 167 us -> 0 us
  matrix products: 135 us -> 21 us
  starting transfers between devices: 15.4 us -> 110 us
  Pallas kernels: 0 us -> 92.7 us
  other arithmetic: 79.4 us -> 35.5 us
    reduce_scatter x6 -> x2, waiting for transfers between devices: 474 us -> 0.01 us  [the longest x1 0.01 us: local(): lax.psum_scatter(grad_up, 'seq', scatter_dimension=0, axis_index_groups=z...]
    ppermute x0 -> x62, waiting for transfers between devices: none -> 176 us  [swap(): return lax.ppermute(value, axis, [(i, i ^ mask) for i in range(size)])]
    all_gather x8 -> x2, waiting for transfers between devices: 159 us -> 0.04 us  [the longest x1 0.02 us: local(): up = lax.all_gather(expert_in[0], 'seq', axis=0, axis_index_groups=z_groups)]
    unnamed x139, local copies, waits for them, and re-layouts: 156 us -> 5.91 us
    reshape x2 -> x6, local copies, waits for them, and re-layouts: 129 us -> 3.58 us  [the longest x3 2.62 us: local(): w.reshape(w_rows, n_z, part).transpose(1, 0, 2)]
    dot_general x23 -> x17, matrix products: 135 us -> 21 us  [the longest x5 7.4 us: dot_tn(): lax.dot_general(left, right, (((0,), (0,)), ((), ())), preferred_element_...]
    ppermute x0 -> x62, starting transfers between devices: none -> 110 us  [swap(): return lax.ppermute(value, axis, [(i, i ^ mask) for i in range(size)])]
    pallas_call x0 -> x5, Pallas kernels: none -> 92.7 us  [the longest x1 35.7 us: attn_bwd(): pl.pallas_call(partial(attn_bwd_kernel, dims, seq_count, heads, size), ou...]
  transfers between devices with their start and end apart: 20 -> 66, of which waited for: 12 -> 31; matrix products, arithmetic and copies ran while one was open for 35% -> 15% of each run, Pallas kernels for 0% -> 13%
where the time goes in v1:
time: 483 us; the launch traced here: 475 us
  waiting for transfers between devices  177 us (37%)
  starting transfers between devices  110 us (23%)
  Pallas kernels  92.7 us (19%)
  other arithmetic  35.5 us (7%)
  local copies, waits for them, and re-layouts  24.1 us (5%)
  matrix products  21 us (4%)
  between operations  15.5 us (3%)
    ppermute x62, waiting for transfers between devices, swap(): return lax.ppermute(value, axis, [(i, i ^ mask) for i in range(size)])  176 us
    ppermute x62, starting transfers between devices, swap(): return lax.ppermute(value, axis, [(i, i ^ mask) for i in range(size)])  110 us
    pallas_call x1, Pallas kernels, attn_bwd(): pl.pallas_call(partial(attn_bwd_kernel, dims, seq_count, heads, size), ou...  35.7 us
    pallas_call x1, Pallas kernels, expert_call(): pl.pallas_call(expert_kernel, grid=(n_z,), out_shape=(jax.ShapeDtypeStruc...  22.5 us
    pallas_call x1, Pallas kernels, attn_fwd(): pl.pallas_call(partial(attn_fwd_kernel, dims, seq_count, heads, size), ou...  20.4 us
    pallas_call x2, Pallas kernels, expert_grad(): pl.pallas_call(expert_grad_kernel, grid=(n_z,), out_shape=jax.ShapeDtypeS...  14.1 us
  transfers between devices with their start and end apart: 66, of which 31 were waited for; matrix products, arithmetic and copies ran while one was open for 15% of the time, Pallas kernels for 13%

profile of v1, /device:TPU:0, one launch (start us, length us, event | category | flops | bytes accessed | tf_op | source)
XLA Modules:
  0.0 475.3 jit_solution(17453356960706540425)
XLA Ops:
  8.0 5.1 %collective-permute-start.8 = (bf16[256,768]{1,0:T(8,128)(2,1)}, bf16[256,768]{1,0:T(8,128)(2,1)S(1)}, u32[]{:S(2)}, u32[]{:S(2)}) collective-permute-start(bf16[256,768]{1,0:T(8,128)(2,1)} %bitcast.197), channel_id=1, source_target_pairs={{0,6},{1,7},{2,4},{3,5},{4,2},{5,3},{6,0},{7,1},{8,14},{9,15},{10,... | collective-permute-start | bytes 1179656 | tf_op jit(solution)/shard_map/ppermute | solution.py:32
  25.2 17.4 %collective-permute-done = bf16[24,640]{1,0:T(8,128)(2,1)S(1)} collective-permute-done((bf16[24,640]{1,0:T(8,128)(2,1)S(1)}, bf16[24,640]{1,0:T(8,128)(2,1)S(1)}, u32[]{:S(2)}, u32[]{:S(2)}) %collective-permute-start) | collective-permute-done | bytes 30752 | tf_op jit(solution)/shard_map/ppermute | solution.py:32
  42.6 43.6 %collective-permute-start.6 = (bf16[256,768]{1,0:T(8,128)(2,1)S(1)}, bf16[256,768]{1,0:T(8,128)(2,1)S(1)}, u32[]{:S(2)}, u32[]{:S(2)}) collective-permute-start(bf16[256,768]{1,0:T(8,128)(2,1)S(1)} %bitcast.199), channel_id=1, source_target_pairs={{0,2},{1,3},{2,0},{3,1},{4,6},{5,7},{6,4},{7,5},{8,10},{9,11},{10,... | collective-permute-start | bytes 1179656 | tf_op jit(solution)/shard_map/ppermute | solution.py:32
  86.8 9.5 %collective-permute-done.13 = bf16[24,768]{1,0:T(8,128)(2,1)S(1)} collective-permute-done((bf16[24,768]{1,0:T(8,128)(2,1)S(1)}, bf16[24,768]{1,0:T(8,128)(2,1)S(1)}, u32[]{:S(2)}, u32[]{:S(2)}) %collective-permute-start.13) | collective-permute-done | bytes 36896 | tf_op jit(solution)/shard_map/ppermute | solution.py:32
  97.0 10.2 %collective-permute-done.14 = bf16[2,24,768]{2,1,0:T(8,128)(2,1)S(1)} collective-permute-done((bf16[2,24,768]{2,1,0:T(8,128)(2,1)S(1)}, bf16[2,24,768]{2,1,0:T(8,128)(2,1)S(1)}, u32[]{:S(2)}, u32[]{:S(2)}) %collective-permute-start.14) | collective-permute-done | bytes 73760 | tf_op jit(solution)/shard_map/ppermute | solution.py:32
  108.8 3.3 collective-permute-done.3
  113.8 5.4 %collective-permute-done.26 = bf16[128,768]{1,0:T(8,128)(2,1)S(1)} collective-permute-done((bf16[128,768]{1,0:T(8,128)(2,1)}, bf16[128,768]{1,0:T(8,128)(2,1)S(1)}, u32[]{:S(2)}, u32[]{:S(2)}) %collective-permute-start.26) | collective-permute-done | bytes 196640 | tf_op jit(solution)/shard_map/ppermute | solution.py:32
  125.1 3.2 collective-permute-start.4
  136.4 3.9 collective-permute-done.30
  140.4 3.3 collective-permute-done.31
  151.5 2.7 convolution_convert_fusion.5.q_ref
  155.4 12.9 %collective-permute-done.9.refs_1_ = bf16[1024,384]{1,0:T(8,128)(2,1)S(1)} collective-permute-done((bf16[1024,384]{1,0:T(8,128)(2,1)S(1)}, bf16[1024,384]{1,0:T(8,128)(2,1)S(1)}, u32[]{:S(2)}, u32[]{:S(2)}) %collective-permute-start.9) | collective-permute-done | bytes 786464 | tf_op jit(solution)/shard_map/ppermute | solution.py:32
  169.1 20.4 %attn_fwd.1 = (bf16[1024,192]{1,0:T(8,128)(2,1)}, f32[3,1024,1]{2,1,0:T(8,128)}) custom-call(s32[2]{0:T(128)} %pad_add_fusion.1.pos_ref, f32[8,4096]{1,0:T(8,128)} %fusion.39.vec_ref, bf16[1024,192]{1,0:T(8,128)(2,1)} %convolution_convert_fusion.5.q_ref, bf16[1024,384]{1,0:T(8,128)(2,1)} %copy-done.4, bf16[1024,384]{1,0:T(8,128)(2,1)} %copy-done.5), custom_call_target="tpu_custom_call" | custom-call | tf_op jit(solution)/shard_map/attn_fwd/pallas_call | solution.py:211
  195.2 3.8 collective-permute-done.10
  198.9 4.1 collective-permute-done.11
  214.0 5.2 %collective-permute-done.35 = f32[512]{0:T(512)S(1)} collective-permute-done((f32[512]{0:T(512)S(1)}, f32[512]{0:T(512)S(1)}, u32[]{:S(2)}, u32[]{:S(2)}) %collective-permute-start.35) | collective-permute-done | bytes 2080 | tf_op jit(solution)/shard_map/ppermute | solution.py:32
  224.3 4.1 collective-permute-done.22
  228.4 4.2 collective-permute-done.23
  232.6 3.0 collective-permute-done.24
  236.8 22.5 %expert.1 = (bf16[1024,768]{1,0:T(8,128)(2,1)}, bf16[1024,768]{1,0:T(8,128)(2,1)}, bf16[4,1024,384]{2,1,0:T(8,128)(2,1)}, bf16[4,1024,384]{2,1,0:T(8,128)(2,1)}) custom-call(bf16[1024,768]{1,0:T(8,128)(2,1)} %copy-done, bf16[1024,768]{1,0:T(8,128)(2,1)} %multiply_convert_fusion.dy_ref.left_ref, bf16[4,768,384]{2,1,0:T(8,128)(2,1)} %all-gather.3.cloned.1.call-done.up_ref, ...), custom_call_target="tpu_custom_call" | custom-call | tf_op jit(solution)/shard_map/expert/pallas_call | solution.py:299
  259.3 6.9 %expert_grad.2 = bf16[4,768,384]{2,1,0:T(8,128)(2,1)} custom-call(bf16[1024,768]{1,0:T(8,128)(2,1)} %copy-done, bf16[4,1024,384]{2,1,0:T(8,128)(2,1)} %get-tuple-element.30.right_ref), custom_call_target="tpu_custom_call" | custom-call | tf_op jit(solution)/shard_map/expert_grad/pallas_call | solution.py:323
  272.6 16.6 %collective-permute-done.36 = bf16[512,768]{1,0:T(8,128)(2,1)} collective-permute-done((bf16[512,768]{1,0:T(8,128)(2,1)}, bf16[512,768]{1,0:T(8,128)(2,1)}, u32[]{:S(2)}, u32[]{:S(2)}) %collective-permute-start.36) | collective-permute-done | bytes 786464 | tf_op jit(solution)/shard_map/ppermute | solution.py:32
  292.8 11.2 %collective-permute-done.40 = bf16[512,768]{1,0:T(8,128)(2,1)} collective-permute-done((bf16[512,768]{1,0:T(8,128)(2,1)}, bf16[512,768]{1,0:T(8,128)(2,1)}, u32[]{:S(2)}, u32[]{:S(2)}) %collective-permute-start.40) | collective-permute-done | bytes 786464 | tf_op jit(solution)/shard_map/ppermute | solution.py:32
  312.5 4.3 collective-permute-done.42
  318.8 2.7 fusion.11
  328.9 7.1 %expert_grad.3 = bf16[4,768,384]{2,1,0:T(8,128)(2,1)} custom-call(bf16[1024,768]{1,0:T(8,128)(2,1)} %multiply_convert_fusion.dy_ref.left_ref, bf16[4,1024,384]{2,1,0:T(8,128)(2,1)} %get-tuple-element.31.right_ref), custom_call_target="tpu_custom_call" | custom-call | tf_op jit(solution)/shard_map/expert_grad/pallas_call | solution.py:323
  338.8 35.7 %attn_bwd.1 = (bf16[1024,192]{1,0:T(8,128)(2,1)}, f32[8,4096]{1,0:T(8,128)}, f32[1024,384]{1,0:T(8,128)}, bf16[1024,384]{1,0:T(8,128)(2,1)}) custom-call(s32[2]{0:T(128)} %pad_add_fusion.1.pos_ref, f32[8,4096]{1,0:T(8,128)} %fusion.39.vec_ref, bf16[1024,192]{1,0:T(8,128)(2,1)} %convolution_convert_fusion.5.q_ref, ...), custom_call_target="tpu_custom_call" | custom-call | tf_op jit(solution)/shard_map/attn_bwd/pallas_call | solution.py:238
  380.0 15.5 %collective-permute-done.47 = bf16[1024,384]{1,0:T(8,128)(2,1)S(1)} collective-permute-done((bf16[1024,384]{1,0:T(8,128)(2,1)}, bf16[1024,384]{1,0:T(8,128)(2,1)S(1)}, u32[]{:S(2)}, u32[]{:S(2)}) %collective-permute-start.47) | collective-permute-done | bytes 786464 | tf_op jit(solution)/shard_map/ppermute | solution.py:32
  397.2 5.2 %fusion.4 = (bf16[768]{0:T(1024)(128)(2,1)S(1)}, bf16[1024,768]{1,0:T(8,128)(2,1)S(1)}, f32[1024,768]{1,0:T(8,128)}) fusion(f32[1024]{0:T(1024)S(1)} %copy-done.54, bf16[256,768]{1,0:T(8,128)(2,1)S(1)} %copy-done.27, bf16[256,768]{1,0:T(8,128)(2,1)S(1)} %copy-done.30, bf16[256,768]{1,0:T(8,128)(2,1)S(1)} %copy-done.32, bf16[256,768]{1,0:T(8,128)(2,1)S(1)} %bitcast.203, ...), kind=kOutput, calls=%fused_computation.7 | convolution fusion | flops 917765376 | bytes 8459776 | tf_op jit(solution)/shard_map/dot_general | solution.py:27
  407.8 2.6 convolution_convert_fusion.1
  418.0 19.9 %collective-permute-done.49 = bf16[256,768]{1,0:T(8,128)(2,1)S(1)} collective-permute-done((bf16[256,768]{1,0:T(8,128)(2,1)}, bf16[256,768]{1,0:T(8,128)(2,1)S(1)}, u32[]{:S(2)}, u32[]{:S(2)}) %collective-permute-start.49) | collective-permute-done | bytes 393248 | tf_op jit(solution)/shard_map/ppermute | solution.py:32
  449.2 2.5 collective-permute-done.53
  (389 shorter events, 141.9 us)
Async XLA Ops:
  7.2 228.5 %all-gather.3.cloned.1.call-start = ((), (), s32[]{:S(2)}) async-start(), calls=%async_computation.2 | async-start | bytes 2949120 | tf_op jit(solution)/shard_map/all_gather | solution.py:427
  7.9 227.8 %all-gather.5.cloned.1.call-start = ((), (), s32[]{:S(2)}) async-start(), calls=%async_computation.3 | async-start | bytes 2949120 | tf_op jit(solution)/shard_map/all_gather | solution.py:428
  8.0 122.1 %collective-permute-start.8 = (bf16[256,768]{1,0:T(8,128)(2,1)}, bf16[256,768]{1,0:T(8,128)(2,1)S(1)}, u32[]{:S(2)}, u32[]{:S(2)}) collective-permute-start(bf16[256,768]{1,0:T(8,128)(2,1)} %bitcast.197), channel_id=1, source_target_pairs={{0,6},{1,7},{2,4},{3,5},{4,2},{5,3},{6,0},{7,1},{8,14},{9,15},{10,... | collective-permute-start | bytes 1179656 | tf_op jit(solution)/shard_map/ppermute | solution.py:32
  13.1 117.5 %collective-permute-start.7 = (bf16[256,768]{1,0:T(8,128)(2,1)}, bf16[256,768]{1,0:T(8,128)(2,1)S(1)}, u32[]{:S(2)}, u32[]{:S(2)}) collective-permute-start(bf16[256,768]{1,0:T(8,128)(2,1)} %bitcast.198), channel_id=1, source_target_pairs={{0,4},{1,5},{2,6},{3,7},{4,0},{5,1},{6,2},{7,3},{8,12},{9,13},{10,... | collective-permute-start | bytes 1179656 | tf_op jit(solution)/shard_map/ppermute | solution.py:32
  18.0 24.6 %collective-permute-start = (bf16[24,640]{1,0:T(8,128)(2,1)S(1)}, bf16[24,640]{1,0:T(8,128)(2,1)S(1)}, u32[]{:S(2)}, u32[]{:S(2)}) collective-permute-start(bf16[24,640]{1,0:T(8,128)(2,1)S(1)} %bitcast.222), channel_id=1, source_target_pairs={{0,6},{1,7},{2,4},{3,5},{4,2},{5,3},{6,0},{7,1},{8,14},{9,15},{10,... | collective-permute-start | bytes 92168 | tf_op jit(solution)/shard_map/ppermute | solution.py:32
  20.0 66.7 %collective-permute-start.1 = (bf16[24,640]{1,0:T(8,128)(2,1)S(1)}, bf16[24,640]{1,0:T(8,128)(2,1)S(1)}, u32[]{:S(2)}, u32[]{:S(2)}) collective-permute-start(bf16[24,640]{1,0:T(8,128)(2,1)S(1)} %bitcast.220), channel_id=1, source_target_pairs={{0,4},{1,5},{2,6},{3,7},{4,0},{5,1},{6,2},{7,3},{8,12},{9,13},{10,... | collective-permute-start | bytes 92168 | tf_op jit(solution)/shard_map/ppermute | solution.py:32
  21.2 65.5 %collective-permute-start.2 = (bf16[24,640]{1,0:T(8,128)(2,1)S(1)}, bf16[24,640]{1,0:T(8,128)(2,1)S(1)}, u32[]{:S(2)}, u32[]{:S(2)}) collective-permute-start(bf16[24,640]{1,0:T(8,128)(2,1)S(1)} %bitcast.221), channel_id=1, source_target_pairs={{0,2},{1,3},{2,0},{3,1},{4,6},{5,7},{6,4},{7,5},{8,10},{9,11},{10,... | collective-permute-start | bytes 92168 | tf_op jit(solution)/shard_map/ppermute | solution.py:32
  22.7 441.4 %reduce-scatter.3.cloned.1.call-start = ((), (), s32[]{:S(2)}) async-start(), calls=%async_computation.4 | async-start | bytes 2949120 | tf_op jit(solution)/shard_map/reduce_scatter | solution.py:495
  42.6 89.5 %collective-permute-start.6 = (bf16[256,768]{1,0:T(8,128)(2,1)S(1)}, bf16[256,768]{1,0:T(8,128)(2,1)S(1)}, u32[]{:S(2)}, u32[]{:S(2)}) collective-permute-start(bf16[256,768]{1,0:T(8,128)(2,1)S(1)} %bitcast.199), channel_id=1, source_target_pairs={{0,2},{1,3},{2,0},{3,1},{4,6},{5,7},{6,4},{7,5},{8,10},{9,11},{10,... | collective-permute-start | bytes 1179656 | tf_op jit(solution)/shard_map/ppermute | solution.py:32
  86.7 27.0 %collective-permute-start.25 = (bf16[128,768]{1,0:T(8,128)(2,1)}, bf16[128,768]{1,0:T(8,128)(2,1)S(1)}, u32[]{:S(2)}, u32[]{:S(2)}) collective-permute-start(bf16[128,768]{1,0:T(8,128)(2,1)} %get-tuple-element.235), channel_id=1, source_target_pairs={{0,8},{8,0},{16,24},{24,16},{1,9},{9,1},{17,25},{25,17},{2,10},{10... | collective-permute-start | bytes 589832 | tf_op jit(solution)/shard_map/ppermute | solution.py:32
  130.6 13.1 %collective-permute-start.31 = (bf16[128,768]{1,0:T(8,128)(2,1)S(1)}, bf16[128,768]{1,0:T(8,128)(2,1)S(1)}, u32[]{:S(2)}, u32[]{:S(2)}) collective-permute-start(bf16[128,768]{1,0:T(8,128)(2,1)S(1)} %collective-permute-done.27), channel_id=1, source_target_pairs={{0,1},{1,0},{2,3},{3,2},{4,5},{5,4},{6,7},{7,6},{8,9},{9,8},{10,11... | collective-permute-start | bytes 589832 | tf_op jit(solution)/shard_map/ppermute | solution.py:32
  148.4 19.8 %collective-permute-start.9 = (bf16[1024,384]{1,0:T(8,128)(2,1)S(1)}, bf16[1024,384]{1,0:T(8,128)(2,1)S(1)}, u32[]{:S(2)}, u32[]{:S(2)}) collective-permute-start(bf16[1024,384]{1,0:T(8,128)(2,1)S(1)} %convolution_convert_fusion.2.refs_0_), channel_id=1, source_target_pairs={{0,1},{1,0},{2,3},{3,2},{4,5},{5,4},{6,7},{7,6},{8,9},{9,8},{10,11... | collective-permute-start | bytes 2359304 | tf_op jit(solution)/shard_map/ppermute | solution.py:32
  210.1 12.0 %collective-permute-start.19 = (bf16[128,768]{1,0:T(8,128)(2,1)S(1)}, bf16[128,768]{1,0:T(8,128)(2,1)S(1)}, u32[]{:S(2)}, u32[]{:S(2)}) collective-permute-start(bf16[128,768]{1,0:T(8,128)(2,1)S(1)} %get-tuple-element.239), channel_id=1, source_target_pairs={{0,16},{8,24},{16,0},{24,8},{1,17},{9,25},{17,1},{25,9},{2,18},{10... | collective-permute-start | bytes 589832 | tf_op jit(solution)/shard_map/ppermute | solution.py:32
  211.6 12.6 %collective-permute-start.21 = (bf16[128,768]{1,0:T(8,128)(2,1)S(1)}, bf16[128,768]{1,0:T(8,128)(2,1)S(1)}, u32[]{:S(2)}, u32[]{:S(2)}) collective-permute-start(bf16[128,768]{1,0:T(8,128)(2,1)S(1)} %get-tuple-element.236), channel_id=1, source_target_pairs={{0,1},{1,0},{2,3},{3,2},{4,5},{5,4},{6,7},{7,6},{8,9},{9,8},{10,11... | collective-permute-start | bytes 589832 | tf_op jit(solution)/shard_map/ppermute | solution.py:32
  222.6 13.0 %collective-permute-start.24 = (bf16[128,768]{1,0:T(8,128)(2,1)S(1)}, bf16[128,768]{1,0:T(8,128)(2,1)S(1)}, u32[]{:S(2)}, u32[]{:S(2)}) collective-permute-start(bf16[128,768]{1,0:T(8,128)(2,1)S(1)} %collective-permute-done.20), channel_id=1, source_target_pairs={{0,1},{1,0},{2,3},{3,2},{4,5},{5,4},{6,7},{7,6},{8,9},{9,8},{10,11... | collective-permute-start | bytes 589832 | tf_op jit(solution)/shard_map/ppermute | solution.py:32
  266.2 200.0 %reduce-scatter.5.cloned.1.call-start = ((), (), s32[]{:S(2)}) async-start(), calls=%async_computation.5 | async-start | bytes 2949120 | tf_op jit(solution)/shard_map/reduce_scatter | solution.py:498
  268.4 20.8 %collective-permute-start.36 = (bf16[512,768]{1,0:T(8,128)(2,1)}, bf16[512,768]{1,0:T(8,128)(2,1)}, u32[]{:S(2)}, u32[]{:S(2)}) collective-permute-start(bf16[512,768]{1,0:T(8,128)(2,1)} %slice.367), channel_id=1, source_target_pairs={{0,1},{1,0},{2,3},{3,2},{4,5},{5,4},{6,7},{7,6},{8,9},{9,8},{10,11... | collective-permute-start | bytes 2359304 | tf_op jit(solution)/shard_map/ppermute | solution.py:32
  270.9 33.0 %collective-permute-start.40 = (bf16[512,768]{1,0:T(8,128)(2,1)}, bf16[512,768]{1,0:T(8,128)(2,1)}, u32[]{:S(2)}, u32[]{:S(2)}) collective-permute-start(bf16[512,768]{1,0:T(8,128)(2,1)} %slice.373), channel_id=1, source_target_pairs={{0,1},{1,0},{2,3},{3,2},{4,5},{5,4},{6,7},{7,6},{8,9},{9,8},{10,11... | collective-permute-start | bytes 2359304 | tf_op jit(solution)/shard_map/ppermute | solution.py:32
  290.8 16.2 %collective-permute-start.39 = (bf16[128,768]{1,0:T(8,128)(2,1)S(1)}, bf16[128,768]{1,0:T(8,128)(2,1)S(1)}, u32[]{:S(2)}, u32[]{:S(2)}) collective-permute-start(bf16[128,768]{1,0:T(8,128)(2,1)S(1)} %get-tuple-element.228), channel_id=1, source_target_pairs={{0,24},{8,16},{16,8},{24,0},{1,25},{9,17},{17,9},{25,1},{2,26},{10... | collective-permute-start | bytes 589832 | tf_op jit(solution)/shard_map/ppermute | solution.py:32
  290.9 16.3 %collective-permute-start.38 = (bf16[128,768]{1,0:T(8,128)(2,1)S(1)}, bf16[128,768]{1,0:T(8,128)(2,1)S(1)}, u32[]{:S(2)}, u32[]{:S(2)}) collective-permute-start(bf16[128,768]{1,0:T(8,128)(2,1)S(1)} %get-tuple-element.229), channel_id=1, source_target_pairs={{0,16},{8,24},{16,0},{24,8},{1,17},{9,25},{17,1},{25,9},{2,18},{10... | collective-permute-start | bytes 589832 | tf_op jit(solution)/shard_map/ppermute | solution.py:32
  292.4 14.8 %collective-permute-start.37 = (bf16[128,768]{1,0:T(8,128)(2,1)S(1)}, bf16[128,768]{1,0:T(8,128)(2,1)S(1)}, u32[]{:S(2)}, u32[]{:S(2)}) collective-permute-start(bf16[128,768]{1,0:T(8,128)(2,1)S(1)} %get-tuple-element.230), channel_id=1, source_target_pairs={{0,8},{8,0},{16,24},{24,16},{1,9},{9,1},{17,25},{25,17},{2,10},{10... | collective-permute-start | bytes 589832 | tf_op jit(solution)/shard_map/ppermute | solution.py:32
  323.2 55.0 %collective-permute-start.57 = (bf16[2,2,2,2,24,896]{5,4,3,2,1,0:T(8,128)(2,1)}, bf16[2,2,2,2,24,896]{5,4,3,2,1,0:T(8,128)(2,1)}, u32[]{:S(2)}, u32[]{:S(2)}) collective-permute-start(bf16[2,2,2,2,24,896]{5,4,3,2,1,0:T(8,128)(2,1)} %select_bitcast_fusion), channel_id=1, source_target_pairs={{0,8},{8,0},{16,24},{24,16},{1,9},{9,1},{17,25},{25,17},{2,10},{10... | collective-permute-start | bytes 2064392 | tf_op jit(solution)/shard_map/ppermute | solution.py:32
  323.9 12.2 %collective-permute-start.46 = (bf16[256,192]{1,0:T(8,128)(2,1)S(1)}, bf16[256,192]{1,0:T(8,128)(2,1)S(1)}, u32[]{:S(2)}, u32[]{:S(2)}) collective-permute-start(bf16[256,192]{1,0:T(8,128)(2,1)S(1)} %get-tuple-element.251), channel_id=1, source_target_pairs={{0,6},{1,7},{2,4},{3,5},{4,2},{5,3},{6,0},{7,1},{8,14},{9,15},{10,... | collective-permute-start | bytes 294920 | tf_op jit(solution)/shard_map/ppermute | solution.py:32
  326.0 11.8 %collective-permute-start.45 = (bf16[256,192]{1,0:T(8,128)(2,1)S(1)}, bf16[256,192]{1,0:T(8,128)(2,1)S(1)}, u32[]{:S(2)}, u32[]{:S(2)}) collective-permute-start(bf16[256,192]{1,0:T(8,128)(2,1)S(1)} %get-tuple-element.250), channel_id=1, source_target_pairs={{0,4},{1,5},{2,6},{3,7},{4,0},{5,1},{6,2},{7,3},{8,12},{9,13},{10,... | collective-permute-start | bytes 294920 | tf_op jit(solution)/shard_map/ppermute | solution.py:32
  326.0 11.8 %collective-permute-start.44 = (bf16[256,192]{1,0:T(8,128)(2,1)S(1)}, bf16[256,192]{1,0:T(8,128)(2,1)S(1)}, u32[]{:S(2)}, u32[]{:S(2)}) collective-permute-start(bf16[256,192]{1,0:T(8,128)(2,1)S(1)} %get-tuple-element.249), channel_id=1, source_target_pairs={{0,2},{1,3},{2,0},{3,1},{4,6},{5,7},{6,4},{7,5},{8,10},{9,11},{10,... | collective-permute-start | bytes 294920 | tf_op jit(solution)/shard_map/ppermute | solution.py:32
  376.2 19.3 %collective-permute-start.47 = (bf16[1024,384]{1,0:T(8,128)(2,1)}, bf16[1024,384]{1,0:T(8,128)(2,1)S(1)}, u32[]{:S(2)}, u32[]{:S(2)}) collective-permute-start(bf16[1024,384]{1,0:T(8,128)(2,1)} %get-tuple-element.28), channel_id=1, source_target_pairs={{0,1},{1,0},{2,3},{3,2},{4,5},{5,4},{6,7},{7,6},{8,9},{9,8},{10,11... | collective-permute-start | bytes 2359304 | tf_op jit(solution)/shard_map/ppermute | solution.py:32
  379.8 30.5 %collective-permute-start.58 = (bf16[2,2,2,24,896]{4,3,2,1,0:T(8,128)(2,1)S(1)}, bf16[2,2,2,24,896]{4,3,2,1,0:T(8,128)(2,1)S(1)}, u32[]{:S(2)}, u32[]{:S(2)}) collective-permute-start(bf16[2,2,2,24,896]{4,3,2,1,0:T(8,128)(2,1)S(1)} %select_bitcast_fusion.6), channel_id=1, source_target_pairs={{0,16},{8,24},{16,0},{24,8},{1,17},{9,25},{17,1},{25,9},{2,18},{10... | collective-permute-start | bytes 1032200 | tf_op jit(solution)/shard_map/ppermute | solution.py:32
  403.4 14.6 %collective-permute-start.50 = (bf16[256,768]{1,0:T(8,128)(2,1)}, bf16[256,768]{1,0:T(8,128)(2,1)S(1)}, u32[]{:S(2)}, u32[]{:S(2)}) collective-permute-start(bf16[256,768]{1,0:T(8,128)(2,1)} %get-tuple-element.211), channel_id=1, source_target_pairs={{0,6},{1,7},{2,4},{3,5},{4,2},{5,3},{6,0},{7,1},{8,14},{9,15},{10,... | collective-permute-start | bytes 1179656 | tf_op jit(solution)/shard_map/ppermute | solution.py:32
  405.4 32.5 %collective-permute-start.49 = (bf16[256,768]{1,0:T(8,128)(2,1)}, bf16[256,768]{1,0:T(8,128)(2,1)S(1)}, u32[]{:S(2)}, u32[]{:S(2)}) collective-permute-start(bf16[256,768]{1,0:T(8,128)(2,1)} %get-tuple-element.212), channel_id=1, source_target_pairs={{0,4},{1,5},{2,6},{3,7},{4,0},{5,1},{6,2},{7,3},{8,12},{9,13},{10,... | collective-permute-start | bytes 1179656 | tf_op jit(solution)/shard_map/ppermute | solution.py:32
  405.4 32.5 %collective-permute-start.48 = (bf16[256,768]{1,0:T(8,128)(2,1)}, bf16[256,768]{1,0:T(8,128)(2,1)}, u32[]{:S(2)}, u32[]{:S(2)}) collective-permute-start(bf16[256,768]{1,0:T(8,128)(2,1)} %get-tuple-element.210), channel_id=1, source_target_pairs={{0,2},{1,3},{2,0},{3,1},{4,6},{5,7},{6,4},{7,5},{8,10},{9,11},{10,... | collective-permute-start | bytes 1179656 | tf_op jit(solution)/shard_map/ppermute | solution.py:32
  415.6 23.8 %collective-permute-start.51 = (bf16[2,4,2,24,640]{4,1,3,2,0:T(4,128)(2,1)S(1)}, bf16[2,4,2,24,640]{4,1,3,2,0:T(4,128)(2,1)S(1)}, u32[]{:S(2)}, u32[]{:S(2)}) collective-permute-start(bf16[2,4,2,24,640]{4,1,3,2,0:T(4,128)(2,1)S(1)} %select_bitcast_fusion.3), channel_id=1, source_target_pairs={{0,8},{8,0},{16,24},{24,16},{1,9},{9,1},{17,25},{25,17},{2,10},{10... | collective-permute-start | bytes 1474568 | tf_op jit(solution)/shard_map/ppermute | solution.py:32
  417.9 21.3 %collective-permute-start.60 = (bf16[2,24,896]{2,1,0:T(8,128)(2,1)S(1)}, bf16[2,24,896]{2,1,0:T(8,128)(2,1)S(1)}, u32[]{:S(2)}, u32[]{:S(2)}) collective-permute-start(bf16[2,24,896]{2,1,0:T(8,128)(2,1)S(1)} %select_bitcast_fusion.18), channel_id=1, source_target_pairs={{0,2},{1,3},{2,0},{3,1},{4,6},{5,7},{6,4},{7,5},{8,10},{9,11},{10,... | collective-permute-start | bytes 258056 | tf_op jit(solution)/shard_map/ppermute | solution.py:32
  (92 other events, 793.2 us)
Sparse Core Ops, SparseCore 0:
  9.6 78.1 all-gather.2
  89.4 51.8 all-gather.4
  266.3 47.6 reduce-scatter.2
  336.2 46.8 reduce-scatter.4

commit v2 on v1

v2 whole, which is shorter than its diff:
```python
import math
from functools import partial

import jax
import jax.numpy as jnp
from jax import lax
from jax.experimental import pallas as pl
from jax.experimental.pallas import tpu as pltpu
from jax.sharding import PartitionSpec as P

epsilon = 1e-06
highest = lax.Precision.HIGHEST
bf16 = jnp.bfloat16
f32 = jnp.float32
VMEM = 56 * 1024 * 1024


def dot_nn(left, right):
    return lax.dot_general(left, right, (((1,), (0,)), ((), ())), preferred_element_type=f32)


def dot_tn(left, right):
    return lax.dot_general(left, right, (((0,), (0,)), ((), ())), preferred_element_type=f32)


def dot_nt(left, right):
    return lax.dot_general(left, right, (((1,), (1,)), ((), ())), preferred_element_type=f32)


def swap(value, axis, mask):
    size = lax.axis_size(axis)
    return lax.ppermute(value, axis, [(i, i ^ mask) for i in range(size)])


def bits_of(size):
    return [1 << i for i in range(size.bit_length() - 1)]


def unxor(parts, index):
    for bit in bits_of(len(parts)):
        flag = (index & bit) != 0
        parts = [jnp.where(flag, parts[j ^ bit], parts[j]) for j in range(len(parts))]
    return parts


def after(value, *others):
    return lax.optimization_barrier((value, *others))[0]


def grow(value, axis, mask, bit_set):
    other = swap(value, axis, mask)
    return jnp.stack([jnp.where(bit_set, other, value), jnp.where(bit_set, value, other)])


def pick(value, position, flag):
    low = lax.index_in_dim(value, 0, position, keepdims=False)
    high = lax.index_in_dim(value, 1, position, keepdims=False)
    return jnp.where(flag, high, low)


def halve(value, position, axis, mask, bit_set):
    sent = pick(value, position, jnp.logical_not(bit_set))
    kept = pick(value, position, bit_set)
    got = swap(sent, axis, mask)
    return (kept.astype(f32) + got.astype(f32)).astype(bf16)


def bias_tile(vec_ref, tile_ref, head):
    rows, width = tile_ref.shape
    vec = jnp.broadcast_to(vec_ref[pl.ds(head, 1), :], (rows, width))
    tile_ref[...] = pltpu.roll(vec, width - (rows - 1), 1, stride=1, stride_axis=0)


def key_columns(pos_ref, dims, key_ys, query_z):
    n_z, n_y, local_len = dims
    z, y = pos_ref[0], pos_ref[1]
    query_block = (z ^ query_z) * n_y + y
    columns = []
    for key_y in key_ys:
        for key_z in range(n_z):
            key_block = (z ^ key_z) * n_y + (y ^ key_y)
            first = (n_z * n_y - 1 - query_block + key_block) * local_len
            columns.append(pl.ds(pl.multiple_of(first, local_len), local_len))
    return columns


def split_keys(dims, seq_count, heads, size, kv_refs, offset, plain_ref, turned_ref):
    n_z, _, local_len = dims
    for head in range(heads):
        lo, hi = offset + head * size, offset + (head + 1) * size
        for s in range(seq_count):
            index = head * seq_count + s
            for group, kv_ref in enumerate(kv_refs):
                for key_z in range(n_z):
                    at = (key_z * seq_count + s) * local_len
                    to = (group * n_z + key_z) * local_len
                    block = kv_ref[at : at + local_len, lo:hi]
                    if plain_ref is not None:
                        plain_ref[index, to : to + local_len, :] = block
                    if turned_ref is not None:
                        turned_ref[index, :, to : to + local_len] = block.T


def attn_fwd_kernel(dims, seq_count, heads, size, key_ys, first, pos_ref, vec_ref, q_ref, *refs):
    n_z, _, local_len = dims
    kv_refs, refs = refs[: len(key_ys)], refs[len(key_ys) :]
    if first:
        out_ref, *refs = refs
    else:
        out_in, c_ref, out_ref, *refs = refs
    tile_ref, kt_ref, v_ref, qh_ref = refs
    inner = heads * size
    split_keys(dims, seq_count, heads, size, kv_refs, 0, None, kt_ref)
    split_keys(dims, seq_count, heads, size, kv_refs, inner, v_ref, None)
    for head in range(heads):
        qh_ref[head] = q_ref[:, head * size : (head + 1) * size]

    def head_step(head, carry):
        bias_tile(vec_ref, tile_ref, head)

        def query_step(query_z, carry):
            columns = key_columns(pos_ref, dims, key_ys, query_z)
            for s in range(seq_count):
                row = pl.multiple_of((query_z * seq_count + s) * local_len, local_len)
                rows = pl.ds(row, local_len)
                bias = jnp.concatenate([tile_ref[:, c] for c in columns], axis=1)
                score = dot_nn(qh_ref[head, rows, :], kt_ref[head * seq_count + s]) + bias
                top = jnp.max(score, axis=1, keepdims=True)
                if not first:
                    top_before = out_in[head, rows, size : size + 1]
                    top = jnp.maximum(top, top_before)
                weight = jnp.exp(score - top)
                total = jnp.sum(weight, axis=1, keepdims=True)
                out = dot_nn(weight.astype(bf16), v_ref[head * seq_count + s])
                if first:
                    out_ref[head, rows, :size] = out
                    out_ref[head, rows, size : size + 1] = top
                    out_ref[head, rows, size + 1 : size + 2] = total
                else:
                    fade = jnp.exp(top_before - top)
                    total = total + fade * out_in[head, rows, size + 1 : size + 2]
                    out_ref[head, rows, :size] = (out + fade * out_in[head, rows, :size]) / total
                    out_ref[head, rows, size : size + 1] = top + jnp.log(total)
            return carry

        return lax.fori_loop(0, n_z, query_step, carry)

    lax.fori_loop(0, heads, head_step, 0)
    if not first:
        for head in range(heads):
            c_ref[:, head * size : (head + 1) * size] = out_ref[head, :, :size].astype(bf16)


def attn_bwd_kernel(dims, seq_count, heads, size, key_ys, first, pos_ref, vec_ref, q_ref, *refs):
    n_z, _, local_len = dims
    count = len(key_ys)
    dc_ref, c_ref, *refs = refs
    kv_refs, refs = refs[:count], refs[count:]
    if first:
        dq_ref, diag_ref, *refs = refs
        dqh_ref = dq_ref
    else:
        dq_in, diag_in, dq_ref, diag_ref, *refs = refs
    dkv_refs, refs = refs[:count], refs[count:]
    tile_ref, grad_ref, kt_ref, vt_ref, k_ref, qh_ref, dch_ref, delta_ref, dk_ref, dv_ref = refs[:10]
    if not first:
        dqh_ref = refs[10]
    inner = heads * size
    split_keys(dims, seq_count, heads, size, kv_refs, 0, k_ref, kt_ref)
    split_keys(dims, seq_count, heads, size, kv_refs, inner, None, vt_ref)
    for head in range(heads):
        qh_ref[head] = q_ref[:, head * size : (head + 1) * size]
        dc = dc_ref[:, head * size : (head + 1) * size]
        dch_ref[head] = dc
        delta_ref[head] = jnp.sum(dc.astype(f32) * c_ref[head, :, :size], axis=1, keepdims=True)
    if first:
        diag_ref[...] = jnp.zeros_like(diag_ref)
    else:
        diag_ref[...] = diag_in[...]
    dk_ref[...] = jnp.zeros_like(dk_ref)
    dv_ref[...] = jnp.zeros_like(dv_ref)

    def head_step(head, carry):
        bias_tile(vec_ref, tile_ref, head)
        grad_ref[...] = jnp.zeros_like(grad_ref)

        def query_step(query_z, carry):
            columns = key_columns(pos_ref, dims, key_ys, query_z)
            for s in range(seq_count):
                index = head * seq_count + s
                row = pl.multiple_of((query_z * seq_count + s) * local_len, local_len)
                rows = pl.ds(row, local_len)
                q = qh_ref[head, rows, :]
                dc = dch_ref[head, rows, :]
                bias = jnp.concatenate([tile_ref[:, c] for c in columns], axis=1)
                prob = jnp.exp(dot_nn(q, kt_ref[index]) + bias - c_ref[head, rows, size : size + 1])
                dprob = dot_nn(dc, vt_ref[index])
                ds = (prob * (dprob - delta_ref[head, rows, :])).astype(bf16)
                dq = dot_nn(ds, k_ref[index])
                if not first:
                    dq = dq + dq_in[head, rows, :]
                dqh_ref[head, rows, :] = dq
                dk_ref[index] += dot_tn(q, ds)
                dv_ref[index] += dot_tn(dc, prob.astype(bf16))
                for i, c in enumerate(columns):
                    part = ds[:, i * local_len : (i + 1) * local_len]
                    grad_ref[:, c] += part.astype(f32)
            return carry

        lax.fori_loop(0, n_z, query_step, 0)
        folded = grad_ref[...]
        width = folded.shape[1]
        while folded.shape[0] > 1:
            half = folded.shape[0] // 2
            folded = folded[:half] + pltpu.roll(folded[half:], width - half, 1)
        diag_ref[pl.ds(head, 1), :] += folded
        return carry

    lax.fori_loop(0, heads, head_step, 0)
    for head in range(heads):
        lo, hi = head * size, (head + 1) * size
        if not first:
            dq_ref[:, lo:hi] = dqh_ref[head].astype(bf16)
        for s in range(seq_count):
            index = head * seq_count + s
            for group, out in enumerate(dkv_refs):
                for key_z in range(n_z):
                    at = (key_z * seq_count + s) * local_len
                    to = (group * n_z + key_z) * local_len
                    cut = slice(to, to + local_len)
                    out[at : at + local_len, lo:hi] = dk_ref[index, :, cut].T.astype(out.dtype)
                    out[at : at + local_len, inner + lo : inner + hi] = dv_ref[
                        index, :, cut
                    ].T.astype(out.dtype)


def vmem_specs(count):
    return [pl.BlockSpec(memory_space=pltpu.VMEM) for _ in range(count)]


def attn_fwd(dims, seq_count, heads, size, key_ys, pos, vec, q, kvs, before=()):
    rows = q.shape[0]
    length = len(key_ys) * dims[0] * dims[2]
    both = heads * seq_count
    first = not before
    wide = jax.ShapeDtypeStruct((heads, rows, 2 * size), f32)
    joined = jax.ShapeDtypeStruct((rows, heads * size), bf16)
    return pl.pallas_call(
        partial(attn_fwd_kernel, dims, seq_count, heads, size, key_ys, first),
        out_shape=(wide,) if first else (joined, wide),
        in_specs=[pl.BlockSpec(memory_space=pltpu.SMEM)]
        + vmem_specs(2 + len(kvs) + len(before)),
        out_specs=tuple(vmem_specs(1 if first else 2)),
        scratch_shapes=[
            pltpu.VMEM((dims[2], vec.shape[1]), f32),
            pltpu.VMEM((both, size, length), bf16),
            pltpu.VMEM((both, length, size), bf16),
            pltpu.VMEM((heads, rows, size), bf16),
        ],
        compiler_params=pltpu.CompilerParams(vmem_limit_bytes=VMEM),
        name="attn_fwd",
    )(pos, vec, q, *kvs, *before)


def attn_bwd(dims, seq_count, heads, size, key_ys, pos, vec, q, dc, c, kvs, before=()):
    rows = q.shape[0]
    length = len(key_ys) * dims[0] * dims[2]
    both = heads * seq_count
    first = not before
    wide = jax.ShapeDtypeStruct((heads, rows, size), f32)
    joined = jax.ShapeDtypeStruct((rows, heads * size), bf16)
    shapes = [wide if first else joined, jax.ShapeDtypeStruct(vec.shape, f32)]
    for key_y in key_ys:
        shapes.append(jax.ShapeDtypeStruct(kvs[0].shape, bf16 if key_y else f32))
    scratch = [
        pltpu.VMEM((dims[2], vec.shape[1]), f32),
        pltpu.VMEM((dims[2], vec.shape[1]), f32),
        pltpu.VMEM((both, size, length), bf16),
        pltpu.VMEM((both, size, length), bf16),
        pltpu.VMEM((both, length, size), bf16),
        pltpu.VMEM((heads, rows, size), bf16),
        pltpu.VMEM((heads, rows, size), bf16),
        pltpu.VMEM((heads, rows, 1), f32),
        pltpu.VMEM((both, size, length), f32),
        pltpu.VMEM((both, size, length), f32),
    ]
    if not first:
        scratch.append(pltpu.VMEM((heads, rows, size), f32))
    return pl.pallas_call(
        partial(attn_bwd_kernel, dims, seq_count, heads, size, key_ys, first),
        out_shape=tuple(shapes),
        in_specs=[pl.BlockSpec(memory_space=pltpu.SMEM)]
        + vmem_specs(4 + len(kvs) + len(before)),
        out_specs=tuple(vmem_specs(len(shapes))),
        scratch_shapes=scratch,
        compiler_params=pltpu.CompilerParams(vmem_limit_bytes=VMEM),
        name="attn_bwd",
    )(pos, vec, q, dc, c, *kvs, *before)


def gelu_parts(pre):
    square = pre * pre
    tanh = jnp.tanh(0.7978845608028654 * (pre + 0.044715 * pre * square))
    hidden = 0.5 * pre * (1.0 + tanh)
    slope = 0.5 * (1.0 + tanh) + 0.5 * pre * (1.0 - tanh * tanh) * (
        0.7978845608028654 * (1.0 + 0.134145 * square)
    )
    return hidden.astype(bf16), slope


def accumulate(out_ref, acc_ref, value):
    step = pl.program_id(0)

    @pl.when(step == 0)
    def _():
        acc_ref[...] = value

    @pl.when(step > 0)
    def _():
        acc_ref[...] += value

    @pl.when(step == pl.num_programs(0) - 1)
    def _():
        out_ref[...] = acc_ref[...].astype(out_ref.dtype)


def expert_own_kernel(rows_ref, dy_ref, weight_ref, y_ref, db_ref, g_ref, du_ref, y_acc, db_acc):
    hidden, slope = gelu_parts(dot_nn(rows_ref[...], weight_ref[0, 0]))
    g_ref[0] = hidden
    accumulate(y_ref, y_acc, dot_nt(hidden, weight_ref[0, 1]))
    du = (dot_nn(dy_ref[...], weight_ref[0, 1]) * slope).astype(bf16)
    du_ref[0] = du
    accumulate(db_ref, db_acc, dot_nt(du, weight_ref[0, 0]))


def expert_fwd_kernel(rows_ref, weight_ref, y_ref, g_ref, slope_ref, y_acc):
    hidden, slope = gelu_parts(dot_nn(rows_ref[...], weight_ref[0, 0]))
    g_ref[0] = hidden
    slope_ref[0] = slope.astype(bf16)
    accumulate(y_ref, y_acc, dot_nt(hidden, weight_ref[0, 1]))


def expert_bwd_kernel(dy_ref, slope_ref, weight_ref, db_ref, du_ref, db_acc):
    du = (dot_nn(dy_ref[...], weight_ref[0, 1]) * slope_ref[0].astype(f32)).astype(bf16)
    du_ref[0] = du
    accumulate(db_ref, db_acc, dot_nt(du, weight_ref[0, 0]))


def expert_call(kernel, name, rows, kept_in, up_down, out_type, wholes):
    count = rows[0].shape[0]
    n_z, _, width, hidden = up_down.shape
    whole = pl.BlockSpec((count, width), lambda i: (0, 0))
    weight = pl.BlockSpec((1, 2, width, hidden), lambda i: (i, 0, 0, 0))
    kept = pl.BlockSpec((1, count, hidden), lambda i: (i, 0, 0))
    kept_out = 1 if kept_in else 2
    return pl.pallas_call(
        kernel,
        grid=(n_z,),
        out_shape=(jax.ShapeDtypeStruct((count, width), out_type),) * wholes
        + (jax.ShapeDtypeStruct((n_z, count, hidden), bf16),) * kept_out,
        in_specs=[whole] * len(rows) + [kept] * len(kept_in) + [weight],
        out_specs=(whole,) * wholes + (kept,) * kept_out,
        scratch_shapes=[pltpu.VMEM((count, width), f32)] * wholes,
        compiler_params=pltpu.CompilerParams(vmem_limit_bytes=VMEM),
        name=name,
    )(*rows, *kept_in, up_down)


def expert_grad_kernel(b_ref, b_other, dy_ref, dy_other, du_ref, du_other, g_ref, g_other, out_ref):
    grad_up = dot_tn(b_ref[...], du_ref[0]) + dot_tn(b_other[...], du_other[0])
    out_ref[0, 0] = grad_up.astype(bf16)
    grad_down = dot_tn(dy_ref[...], g_ref[0]) + dot_tn(dy_other[...], g_other[0])
    out_ref[0, 1] = grad_down.astype(bf16)


def expert_grad(rows, kept):
    width = rows[2].shape[1]
    n_z, _, hidden = kept[0].shape
    return pl.pallas_call(
        expert_grad_kernel,
        grid=(n_z,),
        out_shape=jax.ShapeDtypeStruct((n_z, 2, width, hidden), bf16),
        in_specs=[pl.BlockSpec((v.shape[0], width), lambda i: (0, 0)) for v in rows]
        + [pl.BlockSpec((1,) + v.shape[1:], lambda i: (i, 0, 0)) for v in kept],
        out_specs=pl.BlockSpec((1, 2, width, hidden), lambda i: (i, 0, 0, 0)),
        compiler_params=pltpu.CompilerParams(vmem_limit_bytes=VMEM),
        name="expert_grad",
    )(*rows, *kept)


def weight_grad_kernel(a_ref, grad_ref, out_grad_ref, context_ref, small_ref, out_ref):
    cut = grad_ref.shape[1]
    wide = cut + small_ref.shape[1]
    out_ref[:, :cut] = dot_tn(a_ref[...], grad_ref[...]).astype(bf16)
    out_ref[:, cut:wide] = small_ref[...].astype(bf16)
    out_ref[:, wide:] = dot_tn(out_grad_ref[...], context_ref[...]).astype(bf16)


def weight_grad(a, grad, out_grad, context, small):
    width = a.shape[1]
    columns = grad.shape[1] + small.shape[1] + context.shape[1]
    return pl.pallas_call(
        weight_grad_kernel,
        out_shape=jax.ShapeDtypeStruct((width, columns), bf16),
        in_specs=vmem_specs(5),
        out_specs=vmem_specs(1)[0],
        compiler_params=pltpu.CompilerParams(vmem_limit_bytes=VMEM),
        name="weight_grad",
    )(a, grad, out_grad, context, small)


def local(
    tokens,
    cotangent,
    gain_attn,
    query_w,
    key_w,
    value_w,
    output_w,
    rel_table,
    rel_bucket,
    gain_ffn,
    router_w,
    routes,
    expert_in,
    expert_out,
):
    seq_count, local_len, width = tokens.shape
    tok = seq_count * local_len
    n_dp, n_seq = lax.axis_size("dp"), lax.axis_size("seq")
    head_count = rel_table.shape[1]
    inner = query_w.shape[1]
    size = inner // head_count
    n_z = math.gcd(head_count, n_seq)
    n_y = n_seq // n_z
    heads = head_count // n_z
    part = heads * size
    experts = router_w.shape[1]
    capacity = 2 * tok // experts
    table_rows = rel_table.shape[0]
    buckets = table_rows * n_seq
    w_rows = query_w.shape[0]
    dims = (n_z, n_y, local_len)
    dp, seq = lax.axis_index("dp"), lax.axis_index("seq")
    z, y = seq // n_y, seq % n_y
    dp_bits, y_bits, z_bits = bits_of(n_dp), bits_of(n_y), bits_of(n_z)

    def swap_z(value, k):
        return swap(value, "seq", k * n_y) if k else value

    def swap_y(value, k):
        return swap(value, "seq", k) if k else value

    def swap_dp(value, k):
        return swap(value, "dp", k) if k else value

    extra = jnp.concatenate([gain_attn[:, None], gain_ffn[:, None], router_w], axis=1)
    extra = jnp.broadcast_to(extra[None], (n_z, w_rows, 2 + experts))
    table_at = part * 3 + 2 + experts
    table = rel_table.reshape(table_rows, n_z, heads).transpose(1, 0, 2)
    table = jnp.pad(table, ((0, 0), (0, w_rows - table_rows), (0, 0)))
    joined = [w.reshape(w_rows, n_z, part).transpose(1, 0, 2) for w in (query_w, key_w, value_w)]
    pack = jnp.concatenate(joined + [extra, table], axis=2)
    packed = -(-pack.shape[2] // 128) * 128
    pack = jnp.pad(pack, ((0, 0), (0, 0), (0, packed - pack.shape[2])))
    by_partner = unxor([pack[j] for j in range(n_z)], z)
    out_t = output_w.T
    by_partner = [jnp.concatenate([v, out_t], axis=1) for v in by_partner]
    gathered = jnp.stack(unxor([swap_z(by_partner[k], k) for k in range(n_z)], z))

    x_own = tokens.reshape(tok, width)
    upward = [(i, i + n_y) for i in range(n_seq - n_y)]
    downward = [(i + n_y, i) for i in range(n_seq - n_y)]
    below, above = [x_own], [x_own]
    for _ in range(n_z - 1):
        below.append(lax.ppermute(below[-1], "seq", upward))
        above.append(lax.ppermute(above[-1], "seq", downward))
    x_parts = [x_own]
    for k in range(1, n_z):
        chosen = x_own
        for j in range(n_z):
            source = j ^ k
            value = below[j - source] if source < j else above[source - j]
            chosen = jnp.where(z == j, value, chosen)
        x_parts.append(chosen)

    for bit in y_bits:
        gathered = grow(gathered, "seq", bit, (y & bit) != 0)
    route_ids = routes.reshape(tok)
    choose = route_ids[:, None] == jnp.arange(experts, dtype=jnp.int32)[None, :]
    choose_f = choose.astype(f32)
    before = jnp.arange(tok)[:, None] > jnp.arange(tok)[None, :]
    earlier = dot_nn(before.astype(bf16), choose.astype(bf16))
    slot = jnp.sum(earlier * choose_f, axis=1).astype(jnp.int32)
    place = (route_ids ^ dp) * capacity + slot
    place_hot = jnp.arange(experts * capacity, dtype=jnp.int32)[:, None] == place[None, :]
    place_b = place_hot.astype(bf16)

    def to_experts(values):
        sent = dot_nn(place_b, values).astype(bf16).reshape(experts, capacity, -1)
        return [swap_dp(sent[k], k) for k in range(n_dp)]

    def weigh(values, rows):
        gates = rows[:, width : width + 1].astype(f32) + rows[:, width + 1 : width + 2].astype(f32)
        return (values.astype(f32) * gates).astype(bf16)

    def to_others(parts, *others):
        moved = [swap_y(v, k) for k in range(1, n_y) for v in parts]
        return jnp.concatenate([after(v, *others) for v in moved], axis=0)

    def from_experts(total):
        blocks = total.astype(bf16).reshape(n_dp, capacity, width)
        back = [swap_dp(blocks[k], k) for k in range(n_dp)]
        return dot_tn(place_b, jnp.concatenate(back, axis=0))

    def add_others(own, values):
        split = values.reshape(n_y - 1, n_dp * capacity, width)
        for k in range(1, n_y):
            own = own + swap_y(split[k - 1], k).astype(f32)
        return own

    upstream_b = cotangent.reshape(tok, width)
    upstream = upstream_b.astype(f32)

    for bit in reversed(dp_bits):
        gathered = grow(gathered, "dp", bit, (dp & bit) != 0)
    n_bits, m_bits = len(y_bits), len(dp_bits)
    order = tuple(reversed(range(m_bits))) + (m_bits + n_bits,)
    order = order + tuple(range(m_bits, m_bits + n_bits)) + (m_bits + n_bits + 1, m_bits + n_bits + 2)
    gathered = gathered.transpose(order).reshape(width, packed + inner)
    out_t = gathered[:, packed:]
    w_qkv = gathered[:, : 3 * part]
    gain_a = gathered[:, 3 * part].astype(f32)
    gain_f = gathered[:, 3 * part + 1].astype(f32)
    w_router = gathered[:, 3 * part + 2 : 3 * part + 2 + experts]
    table = gathered.reshape(n_dp, n_seq, w_rows, packed + inner)[0, :, :table_rows, table_at : table_at + heads]
    table = table.reshape(buckets, heads)

    z_groups = [[j * n_y + i for j in range(n_z)] for i in range(n_y)]
    up_down = jnp.stack([expert_in[0], expert_out[0]])
    x_all, up_down = lax.optimization_barrier((jnp.concatenate(x_parts, axis=0), up_down))
    up_down = lax.all_gather(up_down, "seq", axis=0, axis_index_groups=z_groups)

    x_all = x_all.astype(f32)
    scale_all = lax.rsqrt(jnp.mean(x_all * x_all, axis=-1, keepdims=True) + epsilon)
    normed_all = (x_all * scale_all * gain_a).astype(bf16)
    kv = dot_nn(normed_all, w_qkv[:, part:]).astype(bf16)
    kvs = [swap_y(kv, k) for k in range(n_y)]
    q = dot_nn(normed_all, w_qkv[:, :part]).astype(bf16)
    d_rows = to_experts(after(upstream_b, x_all))
    span = 2 * n_seq * local_len
    bucket_pad = jnp.concatenate([rel_bucket, jnp.full((1,), -1, jnp.int32)])
    bucket_hot = bucket_pad[None, :] == jnp.arange(buckets, dtype=jnp.int32)[:, None]
    table_pad = jnp.pad(table, ((0, 0), (0, 8 - heads)))
    vec = dot_tn(table_pad, bucket_hot.astype(bf16))
    pos = jnp.stack([z, y]).astype(jnp.int32)
    others = tuple(range(1, n_y))
    shape = (dims, seq_count, heads, size)
    before = attn_fwd(*shape, (0,), pos, vec, q, kvs[:1])
    d_rows = [after(v, *before) for v in d_rows]
    d_own = jnp.concatenate(d_rows, axis=0)
    context_parts, context_f = attn_fwd(*shape, others, pos, vec, q, kvs[1:], before)
    d_other = to_others(d_rows, context_parts)
    context_parts = context_parts.reshape(n_z, tok, part)
    context = [swap_z(context_parts[k], k) for k in range(n_z)]
    context = jnp.concatenate(unxor(context, z), axis=1)

    inputs = x_own.astype(f32)
    hidden_attn = inputs + dot_nt(context, out_t)
    scale_f = lax.rsqrt(jnp.mean(hidden_attn * hidden_attn, axis=-1, keepdims=True) + epsilon)
    normed_f = (hidden_attn * scale_f * gain_f).astype(bf16)
    logits = dot_nn(normed_f, w_router)
    router_p = jax.nn.softmax(logits, axis=-1)
    gate = jnp.sum(router_p * choose_f, axis=-1)

    gate_high = gate.astype(bf16)
    gate_low = (gate - gate_high.astype(f32)).astype(bf16)
    b_gate = jnp.stack([gate_high, gate_low], axis=1)
    b_gate = jnp.pad(b_gate, ((0, 0), (0, 126)))
    b_rows = to_experts(jnp.concatenate([normed_f, b_gate], axis=1))
    b_own = jnp.concatenate(b_rows, axis=0)
    dy_own = weigh(d_own, b_own)
    y_own, db_own, g_own, du_own = expert_call(
        expert_own_kernel, "expert_own", (b_own, dy_own), (), up_down, f32, 2
    )
    b_other = to_others(b_rows, y_own)
    dy_other = weigh(d_other, b_other)
    y_other, g_other, slope = expert_call(
        expert_fwd_kernel, "expert_fwd", (b_other,), (), up_down, bf16, 1
    )
    y_total = add_others(y_own, y_other)
    db_other, du_other = expert_call(
        expert_bwd_kernel, "expert_bwd", (dy_other,), (slope,), up_down, bf16, 1
    )
    db_total = add_others(db_own, db_other)
    y_total, b_late, dy_late = lax.optimization_barrier((y_total, b_other, dy_other))
    expert_tok = from_experts(y_total)
    grad_normed = from_experts(db_total)
    grad_up_down = expert_grad(
        (b_own, b_late, dy_own, dy_late), (du_own, du_other, g_own, g_other)
    )
    grad_up_down = lax.psum_scatter(
        grad_up_down, "seq", scatter_dimension=0, axis_index_groups=z_groups, tiled=True
    )
    grad_up = grad_up_down[:, 0].astype(f32)
    grad_down = grad_up_down[:, 1].astype(f32)

    mixed = (hidden_attn + gate[:, None] * expert_tok).astype(bf16).reshape(tokens.shape)
    grad_gate = jnp.sum(upstream * expert_tok, axis=-1)
    grad_logits = grad_gate[:, None] * router_p * (choose_f - gate[:, None])
    grad_router = lax.dot_general(
        normed_f.astype(f32), grad_logits, (((0,), (0,)), ((), ())), precision=highest
    )
    grad_normed = grad_normed + lax.dot_general(
        grad_logits, w_router.astype(f32), (((1,), (1,)), ((), ())), precision=highest
    )
    scaled = gain_f * grad_normed
    grad_hidden = upstream + scale_f * scaled
    grad_hidden = grad_hidden - hidden_attn * scale_f**3 * jnp.mean(
        scaled * hidden_attn, axis=-1, keepdims=True
    )
    grad_gain_f = jnp.sum(grad_normed * hidden_attn * scale_f, axis=0)
    grad_attn = grad_hidden.astype(bf16)

    grad_ctx = dot_nn(grad_attn, out_t).astype(bf16)
    grad_ctx = unxor([grad_ctx[:, j * part : (j + 1) * part] for j in range(n_z)], z)
    grad_ctx = jnp.concatenate([swap_z(grad_ctx[k], k) for k in range(n_z)], axis=0)
    grad_q, diag, *grad_kvs = attn_bwd(
        *shape, others, pos, vec, q, grad_ctx, context_f, kvs[1:]
    )
    arrived = [swap_y(grad_kvs[k - 1], k) for k in range(1, n_y)]
    grad_q, diag, grad_kv = attn_bwd(
        *shape, (0,), pos, vec, q, grad_ctx, context_f, kvs[:1], (grad_q, diag)
    )
    for value in arrived:
        grad_kv = grad_kv + value.astype(f32)
    grad_qkv = jnp.concatenate([grad_q, grad_kv.astype(bf16)], axis=1)
    grad_a_part = dot_nt(grad_qkv, w_qkv)
    grad_a_parts = grad_a_part.reshape(n_z, tok, width)
    grad_a_in = [swap_z(grad_a_parts[k].astype(bf16), k) for k in range(1, n_z)]

    grad_gain_a = jnp.sum(grad_a_part * x_all * scale_all, axis=0)
    diag = jnp.roll(diag, local_len - 1, axis=1)
    grad_table = lax.dot_general(
        diag, bucket_hot.astype(f32), (((1,), (1,)), ((), ())), precision=highest
    )
    grad_table = grad_table[:heads].T.reshape(1, n_seq, table_rows, heads)
    grad_table = jnp.pad(grad_table, ((0, 0), (0, 0), (0, w_rows - table_rows), (0, 0)))
    grad_table = jnp.broadcast_to(grad_table, (n_dp, n_seq, w_rows, heads)).reshape(width, heads)
    small = [grad_gain_a[:, None], grad_gain_f[:, None], grad_router, grad_table]
    small = jnp.concatenate(small, axis=1)
    small = jnp.pad(small, ((0, 0), (0, packed - 3 * part - small.shape[1])))
    value = weight_grad(normed_all, grad_qkv, grad_attn, context, small)
    value = after(value, grad_a_in[0])
    value = value.reshape((2,) * m_bits + (n_z,) + (2,) * n_bits + (w_rows, packed + inner))
    for i, bit in enumerate(dp_bits):
        value = halve(value, m_bits - 1 - i, "dp", bit, (dp & bit) != 0)
    value = after(value, *grad_a_in)
    value = after(value, grad_up_down)
    for i, bit in enumerate(y_bits):
        value = halve(value, n_bits - i, "seq", bit, (y & bit) != 0)
    parts = unxor([value[j] for j in range(n_z)], z)
    summed = unxor([swap_z(parts[k], k) for k in range(n_z)], z)
    grad_query, grad_key, grad_value = (
        jnp.concatenate([v[:, i * part : (i + 1) * part] for v in summed], axis=1).astype(f32)
        for i in range(3)
    )
    total = sum(v[:, 3 * part :].astype(f32) for v in summed)
    grad_gain_attn = total[:, 0]
    grad_gain_ffn = total[:, 1]
    grad_router = total[:, 2 : 2 + experts]
    grad_output = total[:, packed - 3 * part :].T
    grad_table = jnp.concatenate(
        [v[:table_rows, table_at : table_at + heads] for v in summed], axis=1
    ).astype(f32)

    grad_a = grad_a_parts[0]
    grad_a, grad_output = lax.optimization_barrier((grad_a, grad_output))
    for value in grad_a_in:
        grad_a = grad_a + value.astype(f32)
    scale_a = scale_all[:tok]
    scaled_a = gain_a * grad_a
    grad_x = grad_hidden + scale_a * scaled_a
    grad_x = grad_x - inputs * scale_a**3 * jnp.mean(scaled_a * inputs, axis=-1, keepdims=True)
    grad_tokens = grad_x.reshape(tokens.shape)

    return (
        mixed,
        grad_tokens,
        grad_gain_attn,
        grad_query,
        grad_key,
        grad_value,
        grad_output,
        grad_table,
        grad_gain_ffn,
        grad_router,
        grad_up,
        grad_down,
    )


def solution(mesh):
    vector = P(("dp", "seq"))
    matrix = P(("dp", "seq"), None)
    rows = P("dp", "seq", None)
    expert = P("dp", None, "seq")
    last = P(None, ("dp", "seq"))
    table = P("seq", None)
    return jax.shard_map(
        local,
        mesh=mesh,
        in_specs=(
            rows,
            rows,
            vector,
            matrix,
            matrix,
            matrix,
            last,
            table,
            P(),
            vector,
            matrix,
            P("dp", "seq", None, None),
            expert,
            expert,
        ),
        out_specs=(
            rows,
            rows,
            vector,
            matrix,
            matrix,
            matrix,
            last,
            table,
            vector,
            matrix,
            expert,
            expert,
        ),
        check_vma=False,
    )
```

time: 483 us -> 423 us (0.88)
  starting transfers between devices: 110 us -> 62 us
  waiting for transfers between devices: 177 us -> 139 us
  Pallas kernels: 92.7 us -> 121 us
    ppermute x62 -> x45, starting transfers between devices: 110 us -> 45.5 us  [swap(): return lax.ppermute(value, axis, [(i, i ^ mask) for i in range(size)])]
    ppermute x62 -> x45, waiting for transfers between devices: 176 us -> 128 us  [swap(): return lax.ppermute(value, axis, [(i, i ^ mask) for i in range(size)])]
    pallas_call x3 -> x8, Pallas kernels: 78.6 us -> 110 us  [the longest x2 43.7 us: attn_bwd(): pl.pallas_call(partial(attn_bwd_kernel, dims, seq_count, heads, size, key...]
    ppermute x0 -> x6, starting transfers between devices: none -> 16.5 us  [the longest x3 12.6 us: local(): below.append(lax.ppermute(below[-1], 'seq', upward))]
    ppermute x0 -> x6, waiting for transfers between devices: none -> 11.4 us  [the longest x3 5.74 us: local(): below.append(lax.ppermute(below[-1], 'seq', upward))]
    pallas_call x2 -> x1, Pallas kernels: 14.1 us -> 10.9 us  [expert_grad(): pl.pallas_call(expert_grad_kernel, grid=(n_z,), out_shape=jax.ShapeDtypeS...]
  transfers between devices with their start and end apart: 66 -> 53, of which waited for: 31 -> 26; matrix products, arithmetic and copies ran while one was open for 15% -> 15% of each run, Pallas kernels for 13% -> 29%
where the time goes in v2:
time: 423 us; the launch traced here: 416 us
  waiting for transfers between devices  139 us (33%)
  Pallas kernels  121 us (29%)
  starting transfers between devices  62 us (15%)
  other arithmetic  36 us (9%)
  local copies, waits for them, and re-layouts  25.1 us (6%)
  matrix products  16.8 us (4%)
  between operations  15.5 us (4%)
    ppermute x45, waiting for transfers between devices, swap(): return lax.ppermute(value, axis, [(i, i ^ mask) for i in range(size)])  128 us
    ppermute x45, starting transfers between devices, swap(): return lax.ppermute(value, axis, [(i, i ^ mask) for i in range(size)])  45.5 us
    pallas_call x2, Pallas kernels, attn_bwd(): pl.pallas_call(partial(attn_bwd_kernel, dims, seq_count, heads, size, key...  43.7 us
    pallas_call x3, Pallas kernels, expert_call(): pl.pallas_call(kernel, grid=(n_z,), out_shape=(jax.ShapeDtypeStruct((coun...  32.4 us
    pallas_call x2, Pallas kernels, attn_fwd(): pl.pallas_call(partial(attn_fwd_kernel, dims, seq_count, heads, size, key...  28.9 us
    ppermute x3, starting transfers between devices, local(): below.append(lax.ppermute(below[-1], 'seq', upward))  12.6 us
    pallas_call x1, Pallas kernels, expert_grad(): pl.pallas_call(expert_grad_kernel, grid=(n_z,), out_shape=jax.ShapeDtypeS...  10.9 us
  transfers between devices with their start and end apart: 53, of which 26 were waited for; matrix products, arithmetic and copies ran while one was open for 15% of the time, Pallas kernels for 29%

profile of v2, /device:TPU:0, one launch (start us, length us, event | category | flops | bytes accessed | tf_op | source)
XLA Modules:
  0.0 415.8 jit_solution(17361730789413756430)
XLA Ops:
  12.5 5.1 %collective-permute-start = (bf16[24,1408]{1,0:T(8,128)(2,1)S(1)}, bf16[24,1408]{1,0:T(8,128)(2,1)S(1)}, u32[]{:S(2)}, u32[]{:S(2)}) collective-permute-start(bf16[24,1408]{1,0:T(8,128)(2,1)S(1)} %get-tuple-element.244), channel_id=1, source_target_pairs={{0,6},{1,7},{2,4},{3,5},{4,2},{5,3},{6,0},{7,1},{8,14},{9,15},{10,... | collective-permute-start | bytes 202760 | tf_op jit(solution)/shard_map/ppermute | solution.py:32
  20.2 3.1 collective-permute-done.1
  25.1 3.0 collective-permute-start.6
  35.0 5.1 %collective-permute-start.8 = (bf16[256,768]{1,0:T(8,128)(2,1)S(1)}, bf16[256,768]{1,0:T(8,128)(2,1)}, u32[]{:S(2)}, u32[]{:S(2)}) collective-permute-start(bf16[256,768]{1,0:T(8,128)(2,1)S(1)} %collective-permute-done.6), channel_id=1, source_target_pairs={{0,2},{1,3},{2,4},{3,5},{4,6},{5,7},{8,10},{9,11},{10,12},{11,13},... | collective-permute-start | bytes 1179656 | tf_op jit(solution)/shard_map/ppermute | solution.py:476
  42.6 2.9 collective-permute-done.8
  45.5 4.5 %collective-permute-start.10 = (bf16[256,768]{1,0:T(8,128)(2,1)}, bf16[256,768]{1,0:T(8,128)(2,1)S(1)}, u32[]{:S(2)}, u32[]{:S(2)}) collective-permute-start(bf16[256,768]{1,0:T(8,128)(2,1)} %collective-permute-done.8), channel_id=1, source_target_pairs={{0,2},{1,3},{2,4},{3,5},{4,6},{5,7},{8,10},{9,11},{10,12},{11,13},... | collective-permute-start | bytes 1179656 | tf_op jit(solution)/shard_map/ppermute | solution.py:476
  55.6 5.0 %collective-permute-done.11 = bf16[256,768]{1,0:T(8,128)(2,1)S(1)} collective-permute-done((bf16[256,768]{1,0:T(8,128)(2,1)}, bf16[256,768]{1,0:T(8,128)(2,1)S(1)}, u32[]{:S(2)}, u32[]{:S(2)}) %collective-permute-start.11) | collective-permute-done | bytes 393248 | tf_op jit(solution)/shard_map/ppermute | solution.py:477
  76.2 13.5 %attn_fwd.2.refs_1_ = f32[3,1024,128]{2,1,0:T(8,128)} custom-call(s32[2]{0:T(128)} %pad_add_fusion.1.pos_ref, f32[8,4096]{1,0:T(8,128)} %fusion.33.vec_ref, bf16[1024,192]{1,0:T(8,128)(2,1)} %convolution_convert_fusion.3.q_ref, bf16[1024,384]{1,0:T(8,128)(2,1)} %convolution_convert_fusion.1.refs_0_.refs_2_), custom_call_target="tpu_custom_call" | custom-call | tf_op jit(solution)/shard_map/attn_fwd/pallas_call | solution.py:248
  89.7 15.5 %attn_fwd.3 = (bf16[1024,192]{1,0:T(8,128)(2,1)}, f32[3,1024,128]{2,1,0:T(8,128)}) custom-call(s32[2]{0:T(128)} %pad_add_fusion.1.pos_ref, f32[8,4096]{1,0:T(8,128)} %fusion.33.vec_ref, bf16[1024,192]{1,0:T(8,128)(2,1)} %convolution_convert_fusion.3.q_ref, bf16[1024,384]{1,0:T(8,128)(2,1)} %collective-permute-done.12.refs_0_.refs_2_, ...), custom_call_target="tpu_custom_call" | custom-call | tf_op jit(solution)/shard_map/attn_fwd/pallas_call | solution.py:248
  107.5 3.2 collective-permute-start.15
  111.5 5.7 %collective-permute-done.13 = bf16[256,192]{1,0:T(8,128)(2,1)S(1)} collective-permute-done((bf16[256,192]{1,0:T(8,128)(2,1)S(1)}, bf16[256,192]{1,0:T(8,128)(2,1)S(1)}, u32[]{:S(2)}, u32[]{:S(2)}) %collective-permute-start.13) | collective-permute-done | bytes 98336 | tf_op jit(solution)/shard_map/ppermute | solution.py:32
  117.3 14.0 %collective-permute-done.14 = bf16[256,192]{1,0:T(8,128)(2,1)S(1)} collective-permute-done((bf16[256,192]{1,0:T(8,128)(2,1)S(1)}, bf16[256,192]{1,0:T(8,128)(2,1)S(1)}, u32[]{:S(2)}, u32[]{:S(2)}) %collective-permute-start.14) | collective-permute-done | bytes 98336 | tf_op jit(solution)/shard_map/ppermute | solution.py:32
  139.7 13.7 %collective-permute-done.20 = bf16[128,768]{1,0:T(8,128)(2,1)S(1)} collective-permute-done((bf16[128,768]{1,0:T(8,128)(2,1)S(1)}, bf16[128,768]{1,0:T(8,128)(2,1)S(1)}, u32[]{:S(2)}, u32[]{:S(2)}) %collective-permute-start.20) | collective-permute-done | bytes 196640 | tf_op jit(solution)/shard_map/ppermute | solution.py:32
  162.6 15.4 %expert_own.1 = (f32[512,768]{1,0:T(8,128)}, f32[512,768]{1,0:T(8,128)}, bf16[4,512,384]{2,1,0:T(8,128)(2,1)}, bf16[4,512,384]{2,1,0:T(8,128)(2,1)}) custom-call(bf16[512,896]{1,0:T(8,128)(2,1)} %copy-done, bf16[512,768]{1,0:T(8,128)(2,1)} %multiply_convert_fusion.2.dy_ref, bf16[4,2,768,384]{3,2,1,0:T(8,128)(2,1)} %bitcast.133), custom_call_target="tpu_custom_call" | custom-call | tf_op jit(solution)/shard_map/expert_own/pallas_call | solution.py:356
  185.5 8.6 %expert_fwd.1 = (bf16[512,768]{1,0:T(8,128)(2,1)}, bf16[4,512,384]{2,1,0:T(8,128)(2,1)}, bf16[4,512,384]{2,1,0:T(8,128)(2,1)}) custom-call(bf16[512,896]{1,0:T(8,128)(2,1)} %copy-done.4, bf16[4,2,768,384]{3,2,1,0:T(8,128)(2,1)} %bitcast.134), custom_call_target="tpu_custom_call" | custom-call | tf_op jit(solution)/shard_map/expert_fwd/pallas_call | solution.py:356
  198.9 8.4 %expert_bwd.1 = (bf16[512,768]{1,0:T(8,128)(2,1)}, bf16[4,512,384]{2,1,0:T(8,128)(2,1)}) custom-call(bf16[512,768]{1,0:T(8,128)(2,1)} %multiply_convert_fusion.1.dy_ref.dy_other, bf16[4,512,384]{2,1,0:T(8,128)(2,1)} %get-tuple-element.72.slope_ref, bf16[4,2,768,384]{3,2,1,0:T(8,128)(2,1)} %bitcast.135), custom_call_target="tpu_custom_call" | custom-call | tf_op jit(solution)/shard_map/expert_bwd/pallas_call | solution.py:356
  207.9 6.9 %collective-permute-done.26 = bf16[512,768]{1,0:T(8,128)(2,1)S(1)} collective-permute-done((bf16[512,768]{1,0:T(8,128)(2,1)}, bf16[512,768]{1,0:T(8,128)(2,1)S(1)}, u32[]{:S(2)}, u32[]{:S(2)}) %collective-permute-start.26) | collective-permute-done | bytes 786464 | tf_op jit(solution)/shard_map/ppermute | solution.py:32
  214.9 10.9 %expert_grad.1 = bf16[4,2,768,384]{3,2,1,0:T(8,128)(2,1)} custom-call(bf16[512,896]{1,0:T(8,128)(2,1)} %copy-done, bf16[512,896]{1,0:T(8,128)(2,1)} %copy-done.4, bf16[512,768]{1,0:T(8,128)(2,1)} %multiply_convert_fusion.2.dy_ref, bf16[512,768]{1,0:T(8,128)(2,1)} %multiply_convert_fusion.1.dy_ref.dy_other, bf16[4,512,384]{2,1,0:T(8,128)(2,1)} %get-tuple-element.85.du_ref, ...), custom_call_target="tpu_custom_call" | custom-call | tf_op jit(solution)/shard_map/expert_grad/pallas_call | solution.py:379
  233.3 4.1 collective-permute-done.32
  241.6 4.2 %collective-permute-done.36 = bf16[128,768]{1,0:T(8,128)(2,1)S(1)} collective-permute-done((bf16[128,768]{1,0:T(8,128)(2,1)S(1)}, bf16[128,768]{1,0:T(8,128)(2,1)S(1)}, u32[]{:S(2)}, u32[]{:S(2)}) %collective-permute-start.36) | collective-permute-done | bytes 196640 | tf_op jit(solution)/shard_map/ppermute | solution.py:32
  248.7 4.9 %collective-permute-start.40 = (bf16[256,192]{1,0:T(8,128)(2,1)S(1)}, bf16[256,192]{1,0:T(8,128)(2,1)S(1)}, u32[]{:S(2)}, u32[]{:S(2)}) collective-permute-start(bf16[256,192]{1,0:T(8,128)(2,1)S(1)} %get-tuple-element.215), channel_id=1, source_target_pairs={{0,6},{1,7},{2,4},{3,5},{4,2},{5,3},{6,0},{7,1},{8,14},{9,15},{10,... | collective-permute-start | bytes 294920 | tf_op jit(solution)/shard_map/ppermute | solution.py:32
  254.2 6.5 %collective-permute-done.40 = bf16[256,192]{1,0:T(8,128)(2,1)S(1)} collective-permute-done((bf16[256,192]{1,0:T(8,128)(2,1)S(1)}, bf16[256,192]{1,0:T(8,128)(2,1)S(1)}, u32[]{:S(2)}, u32[]{:S(2)}) %collective-permute-start.40) | collective-permute-done | bytes 98336 | tf_op jit(solution)/shard_map/ppermute | solution.py:32
  260.7 15.5 %collective-permute-done.39 = bf16[256,192]{1,0:T(8,128)(2,1)S(1)} collective-permute-done((bf16[256,192]{1,0:T(8,128)(2,1)S(1)}, bf16[256,192]{1,0:T(8,128)(2,1)S(1)}, u32[]{:S(2)}, u32[]{:S(2)}) %collective-permute-start.39) | collective-permute-done | bytes 98336 | tf_op jit(solution)/shard_map/ppermute | solution.py:32
  277.1 21.1 %attn_bwd.2 = (f32[3,1024,64]{2,1,0:T(8,128)}, f32[8,4096]{1,0:T(8,128)}, bf16[1024,384]{1,0:T(8,128)(2,1)}) custom-call(s32[2]{0:T(128)} %pad_add_fusion.1.pos_ref, f32[8,4096]{1,0:T(8,128)} %fusion.33.vec_ref, bf16[1024,192]{1,0:T(8,128)(2,1)} %convolution_convert_fusion.3.q_ref, bf16[1024,192]{1,0:T(8,128)(2,1)} %pad_maximum_fusion.7.refs_0_, ...), custom_call_target="tpu_custom_call" | custom-call | tf_op jit(solution)/shard_map/attn_bwd/pallas_call | solution.py:289
  300.2 22.7 %attn_bwd.3 = (bf16[1024,192]{1,0:T(8,128)(2,1)}, f32[8,4096]{1,0:T(8,128)}, f32[1024,384]{1,0:T(8,128)}) custom-call(s32[2]{0:T(128)} %pad_add_fusion.1.pos_ref, f32[8,4096]{1,0:T(8,128)} %fusion.33.vec_ref, bf16[1024,192]{1,0:T(8,128)(2,1)} %convolution_convert_fusion.3.q_ref, bf16[1024,192]{1,0:T(8,128)(2,1)} %pad_maximum_fusion.7.refs_0_, ...), custom_call_target="tpu_custom_call" | custom-call | tf_op jit(solution)/shard_map/attn_bwd/pallas_call | solution.py:289
  326.4 4.4 %multiply_reduce_fusion = (f32[768]{0:T(1024)S(1)}, bf16[1024,768]{1,0:T(8,128)(2,1)S(1)}, f32[1024,768]{1,0:T(8,128)}) fusion(bf16[1024,768]{1,0:T(8,128)(2,1)S(1)} %pad_maximum_fusion.1, f32[1024]{0:T(1024)S(1)} %copy-done.33, bf16[768,1408]{1,0:T(8,128)(2,1)} %bitcast.144, bf16[1024,384]{1,0:T(8,128)(2,1)S(1)} %add_convert_fusion, ...), kind=kOutput, calls=%fused_computation | convolution fusion | flops 912260352 | bytes 8461312 | tf_op jit(solution)/shard_map/dot_general | solution.py:27
  334.9 5.2 %weight_grad.1 = bf16[768,1408]{1,0:T(8,128)(2,1)} custom-call(bf16[1024,768]{1,0:T(8,128)(2,1)} %copy-done.3, bf16[1024,576]{1,0:T(8,128)(2,1)} %pad_maximum_fusion.2.grad_ref, bf16[256,768]{1,0:T(8,128)(2,1)} %copy-done.13, bf16[256,768]{1,0:T(8,128)(2,1)} %copy-done.12, f32[768,64]{1,0:T(8,128)} %pad.29.small_ref), custom_call_target="tpu_custom_call" | custom-call | tf_op jit(solution)/shard_map/weight_grad/pallas_call | solution.py:402
  344.6 2.8 collective-permute-done.43
  351.0 12.6 %collective-permute-done.44 = bf16[4,2,24,1408]{3,2,0,1:T(8,128)(2,1)} collective-permute-done((bf16[4,2,24,1408]{3,2,0,1:T(8,128)(2,1)S(1)}, bf16[4,2,24,1408]{3,2,0,1:T(8,128)(2,1)}, u32[]{:S(2)}, u32[]{:S(2)}) %collective-permute-start.44) | collective-permute-done | bytes 540704 | tf_op jit(solution)/shard_map/ppermute | solution.py:32
  364.9 20.8 %collective-permute-done.45 = bf16[256,768]{1,0:T(8,128)(2,1)S(1)} collective-permute-done((bf16[256,768]{1,0:T(8,128)(2,1)}, bf16[256,768]{1,0:T(8,128)(2,1)S(1)}, u32[]{:S(2)}, u32[]{:S(2)}) %collective-permute-start.45) | collective-permute-done | bytes 393248 | tf_op jit(solution)/shard_map/ppermute | solution.py:32
  387.3 6.1 %collective-permute-done.47 = bf16[4,24,1408]{2,1,0:T(8,128)(2,1)S(1)} collective-permute-done((bf16[4,24,1408]{2,1,0:T(8,128)(2,1)S(1)}, bf16[4,24,1408]{2,1,0:T(8,128)(2,1)S(1)}, u32[]{:S(2)}, u32[]{:S(2)}) %collective-permute-start.47) | collective-permute-done | bytes 270368 | tf_op jit(solution)/shard_map/ppermute | solution.py:32
  395.2 2.9 collective-permute-start.50
  (299 shorter events, 122.1 us)
Async XLA Ops:
  7.2 155.5 %all-gather.3.cloned.1.call-start = ((), (), s32[]{:S(2)}) async-start(), calls=%async_computation.2 | async-start | bytes 5898240 | tf_op jit(solution)/shard_map/all_gather | solution.py:542
  28.0 12.1 %collective-permute-start.7 = (bf16[256,768]{1,0:T(8,128)(2,1)S(1)}, bf16[256,768]{1,0:T(8,128)(2,1)}, u32[]{:S(2)}, u32[]{:S(2)}) collective-permute-start(bf16[256,768]{1,0:T(8,128)(2,1)S(1)} %bitcast.138), channel_id=1, source_target_pairs={{2,0},{3,1},{4,2},{5,3},{6,4},{7,5},{10,8},{11,9},{12,10},{13,11},... | collective-permute-start | bytes 1179656 | tf_op jit(solution)/shard_map/ppermute | solution.py:477
  31.7 20.2 %collective-permute-start.4 = (bf16[2,4,24,1408]{3,2,0,1:T(8,128)(2,1)S(1)}, bf16[2,4,24,1408]{3,2,0,1:T(8,128)(2,1)}, u32[]{:S(2)}, u32[]{:S(2)}) collective-permute-start(bf16[2,4,24,1408]{3,2,0,1:T(8,128)(2,1)S(1)} %pad_maximum_fusion.6), channel_id=1, source_target_pairs={{0,16},{8,24},{16,0},{24,8},{1,17},{9,25},{17,1},{25,9},{2,18},{10... | collective-permute-start | bytes 1622024 | tf_op jit(solution)/shard_map/ppermute | solution.py:32
  62.1 323.5 %reduce-scatter.2.cloned.1.call-start = ((), (), s32[]{:S(2)}) async-start(), calls=%async_computation.1 | async-start | bytes 5898240 | tf_op jit(solution)/shard_map/reduce_scatter | solution.py:602
  68.4 21.3 %collective-permute-start.12 = (bf16[1024,384]{1,0:T(8,128)(2,1)}, bf16[1024,384]{1,0:T(8,128)(2,1)}, u32[]{:S(2)}, u32[]{:S(2)}) collective-permute-start(bf16[1024,384]{1,0:T(8,128)(2,1)} %convolution_convert_fusion.1.refs_0_.refs_2_), channel_id=1, source_target_pairs={{0,1},{1,0},{2,3},{3,2},{4,5},{5,4},{6,7},{7,6},{8,9},{9,8},{10,11... | collective-permute-start | bytes 2359304 | tf_op jit(solution)/shard_map/ppermute | solution.py:32
  106.4 24.8 %collective-permute-start.14 = (bf16[256,192]{1,0:T(8,128)(2,1)S(1)}, bf16[256,192]{1,0:T(8,128)(2,1)S(1)}, u32[]{:S(2)}, u32[]{:S(2)}) collective-permute-start(bf16[256,192]{1,0:T(8,128)(2,1)S(1)} %get-tuple-element.210), channel_id=1, source_target_pairs={{0,4},{1,5},{2,6},{3,7},{4,0},{5,1},{6,2},{7,3},{8,12},{9,13},{10,... | collective-permute-start | bytes 294920 | tf_op jit(solution)/shard_map/ppermute | solution.py:32
  107.5 23.7 %collective-permute-start.15 = (bf16[256,192]{1,0:T(8,128)(2,1)S(1)}, bf16[256,192]{1,0:T(8,128)(2,1)S(1)}, u32[]{:S(2)}, u32[]{:S(2)}) collective-permute-start(bf16[256,192]{1,0:T(8,128)(2,1)S(1)} %get-tuple-element.209), channel_id=1, source_target_pairs={{0,2},{1,3},{2,0},{3,1},{4,6},{5,7},{6,4},{7,5},{8,10},{9,11},{10,... | collective-permute-start | bytes 294920 | tf_op jit(solution)/shard_map/ppermute | solution.py:32
  111.5 28.1 %collective-permute-start.21 = (bf16[128,768]{1,0:T(8,128)(2,1)}, bf16[128,768]{1,0:T(8,128)(2,1)}, u32[]{:S(2)}, u32[]{:S(2)}) collective-permute-start(bf16[128,768]{1,0:T(8,128)(2,1)} %get-tuple-element.204), channel_id=1, source_target_pairs={{0,24},{8,16},{16,8},{24,0},{1,25},{9,17},{17,9},{25,1},{2,26},{10... | collective-permute-start | bytes 589832 | tf_op jit(solution)/shard_map/ppermute | solution.py:32
  136.2 19.3 %collective-permute-start.16 = (bf16[128,896]{1,0:T(8,128)(2,1)S(1)}, bf16[128,896]{1,0:T(8,128)(2,1)}, u32[]{:S(2)}, u32[]{:S(2)}) collective-permute-start(bf16[128,896]{1,0:T(8,128)(2,1)S(1)} %get-tuple-element.189), channel_id=1, source_target_pairs={{0,8},{8,0},{16,24},{24,16},{1,9},{9,1},{17,25},{25,17},{2,10},{10... | collective-permute-start | bytes 688136 | tf_op jit(solution)/shard_map/ppermute | solution.py:32
  136.3 20.7 %collective-permute-start.17 = (bf16[128,896]{1,0:T(8,128)(2,1)S(1)}, bf16[128,896]{1,0:T(8,128)(2,1)}, u32[]{:S(2)}, u32[]{:S(2)}) collective-permute-start(bf16[128,896]{1,0:T(8,128)(2,1)S(1)} %get-tuple-element.188), channel_id=1, source_target_pairs={{0,16},{8,24},{16,0},{24,8},{1,17},{9,25},{17,1},{25,9},{2,18},{10... | collective-permute-start | bytes 688136 | tf_op jit(solution)/shard_map/ppermute | solution.py:32
  137.8 19.8 %collective-permute-start.18 = (bf16[128,896]{1,0:T(8,128)(2,1)S(1)}, bf16[128,896]{1,0:T(8,128)(2,1)}, u32[]{:S(2)}, u32[]{:S(2)}) collective-permute-start(bf16[128,896]{1,0:T(8,128)(2,1)S(1)} %get-tuple-element.187), channel_id=1, source_target_pairs={{0,24},{8,16},{16,8},{24,0},{1,25},{9,17},{17,9},{25,1},{2,26},{10... | collective-permute-start | bytes 688136 | tf_op jit(solution)/shard_map/ppermute | solution.py:32
  138.2 15.3 %collective-permute-start.20 = (bf16[128,768]{1,0:T(8,128)(2,1)S(1)}, bf16[128,768]{1,0:T(8,128)(2,1)S(1)}, u32[]{:S(2)}, u32[]{:S(2)}) collective-permute-start(bf16[128,768]{1,0:T(8,128)(2,1)S(1)} %copy-done.29), channel_id=1, source_target_pairs={{0,16},{8,24},{16,0},{24,8},{1,17},{9,25},{17,1},{25,9},{2,18},{10... | collective-permute-start | bytes 589832 | tf_op jit(solution)/shard_map/ppermute | solution.py:32
  139.6 13.8 %collective-permute-start.19 = (bf16[128,768]{1,0:T(8,128)(2,1)S(1)}, bf16[128,768]{1,0:T(8,128)(2,1)S(1)}, u32[]{:S(2)}, u32[]{:S(2)}) collective-permute-start(bf16[128,768]{1,0:T(8,128)(2,1)S(1)} %copy-done.28), channel_id=1, source_target_pairs={{0,8},{8,0},{16,24},{24,16},{1,9},{9,1},{17,25},{25,17},{2,10},{10... | collective-permute-start | bytes 589832 | tf_op jit(solution)/shard_map/ppermute | solution.py:32
  153.4 42.1 %collective-permute-start.30 = (bf16[128,768]{1,0:T(8,128)(2,1)}, bf16[128,768]{1,0:T(8,128)(2,1)}, u32[]{:S(2)}, u32[]{:S(2)}) collective-permute-start(bf16[128,768]{1,0:T(8,128)(2,1)} %collective-permute-done.21), channel_id=1, source_target_pairs={{0,1},{1,0},{2,3},{3,2},{4,5},{5,4},{6,7},{7,6},{8,9},{9,8},{10,11... | collective-permute-start | bytes 589832 | tf_op jit(solution)/shard_map/ppermute | solution.py:32
  155.0 23.1 %collective-permute-start.22 = (bf16[128,896]{1,0:T(8,128)(2,1)S(1)}, bf16[128,896]{1,0:T(8,128)(2,1)}, u32[]{:S(2)}, u32[]{:S(2)}) collective-permute-start(bf16[128,896]{1,0:T(8,128)(2,1)S(1)} %get-tuple-element.186), channel_id=1, source_target_pairs={{0,1},{1,0},{2,3},{3,2},{4,5},{5,4},{6,7},{7,6},{8,9},{9,8},{10,11... | collective-permute-start | bytes 688136 | tf_op jit(solution)/shard_map/ppermute | solution.py:32
  155.5 23.1 %collective-permute-start.23 = (bf16[128,896]{1,0:T(8,128)(2,1)}, bf16[128,896]{1,0:T(8,128)(2,1)}, u32[]{:S(2)}, u32[]{:S(2)}) collective-permute-start(bf16[128,896]{1,0:T(8,128)(2,1)} %collective-permute-done.16), channel_id=1, source_target_pairs={{0,1},{1,0},{2,3},{3,2},{4,5},{5,4},{6,7},{7,6},{8,9},{9,8},{10,11... | collective-permute-start | bytes 688136 | tf_op jit(solution)/shard_map/ppermute | solution.py:32
  157.0 23.1 %collective-permute-start.24 = (bf16[128,896]{1,0:T(8,128)(2,1)}, bf16[128,896]{1,0:T(8,128)(2,1)}, u32[]{:S(2)}, u32[]{:S(2)}) collective-permute-start(bf16[128,896]{1,0:T(8,128)(2,1)} %collective-permute-done.17), channel_id=1, source_target_pairs={{0,1},{1,0},{2,3},{3,2},{4,5},{5,4},{6,7},{7,6},{8,9},{9,8},{10,11... | collective-permute-start | bytes 688136 | tf_op jit(solution)/shard_map/ppermute | solution.py:32
  157.6 24.1 %collective-permute-start.25 = (bf16[128,896]{1,0:T(8,128)(2,1)}, bf16[128,896]{1,0:T(8,128)(2,1)}, u32[]{:S(2)}, u32[]{:S(2)}) collective-permute-start(bf16[128,896]{1,0:T(8,128)(2,1)} %collective-permute-done.18), channel_id=1, source_target_pairs={{0,1},{1,0},{2,3},{3,2},{4,5},{5,4},{6,7},{7,6},{8,9},{9,8},{10,11... | collective-permute-start | bytes 688136 | tf_op jit(solution)/shard_map/ppermute | solution.py:32
  178.0 17.5 %collective-permute-start.29 = (bf16[128,768]{1,0:T(8,128)(2,1)S(1)}, bf16[128,768]{1,0:T(8,128)(2,1)S(1)}, u32[]{:S(2)}, u32[]{:S(2)}) collective-permute-start(bf16[128,768]{1,0:T(8,128)(2,1)S(1)} %copy-done.25), channel_id=1, source_target_pairs={{0,1},{1,0},{2,3},{3,2},{4,5},{5,4},{6,7},{7,6},{8,9},{9,8},{10,11... | collective-permute-start | bytes 589832 | tf_op jit(solution)/shard_map/ppermute | solution.py:32
  178.7 16.9 %collective-permute-start.28 = (bf16[128,768]{1,0:T(8,128)(2,1)S(1)}, bf16[128,768]{1,0:T(8,128)(2,1)S(1)}, u32[]{:S(2)}, u32[]{:S(2)}) collective-permute-start(bf16[128,768]{1,0:T(8,128)(2,1)S(1)} %copy-done.27), channel_id=1, source_target_pairs={{0,1},{1,0},{2,3},{3,2},{4,5},{5,4},{6,7},{7,6},{8,9},{9,8},{10,11... | collective-permute-start | bytes 589832 | tf_op jit(solution)/shard_map/ppermute | solution.py:32
  180.1 15.4 %collective-permute-start.27 = (bf16[128,768]{1,0:T(8,128)(2,1)S(1)}, bf16[128,768]{1,0:T(8,128)(2,1)S(1)}, u32[]{:S(2)}, u32[]{:S(2)}) collective-permute-start(bf16[128,768]{1,0:T(8,128)(2,1)S(1)} %get-tuple-element.55), channel_id=1, source_target_pairs={{0,1},{1,0},{2,3},{3,2},{4,5},{5,4},{6,7},{7,6},{8,9},{9,8},{10,11... | collective-permute-start | bytes 589832 | tf_op jit(solution)/shard_map/ppermute | solution.py:32
  194.1 20.7 %collective-permute-start.26 = (bf16[512,768]{1,0:T(8,128)(2,1)}, bf16[512,768]{1,0:T(8,128)(2,1)S(1)}, u32[]{:S(2)}, u32[]{:S(2)}) collective-permute-start(bf16[512,768]{1,0:T(8,128)(2,1)} %get-tuple-element.65), channel_id=1, source_target_pairs={{0,1},{1,0},{2,3},{3,2},{4,5},{5,4},{6,7},{7,6},{8,9},{9,8},{10,11... | collective-permute-start | bytes 2359304 | tf_op jit(solution)/shard_map/ppermute | solution.py:32
  207.3 21.1 %collective-permute-start.34 = (bf16[512,768]{1,0:T(8,128)(2,1)}, bf16[512,768]{1,0:T(8,128)(2,1)}, u32[]{:S(2)}, u32[]{:S(2)}) collective-permute-start(bf16[512,768]{1,0:T(8,128)(2,1)} %get-tuple-element.73), channel_id=1, source_target_pairs={{0,1},{1,0},{2,3},{3,2},{4,5},{5,4},{6,7},{7,6},{8,9},{9,8},{10,11... | collective-permute-start | bytes 2359304 | tf_op jit(solution)/shard_map/ppermute | solution.py:32
  230.4 15.4 %collective-permute-start.36 = (bf16[128,768]{1,0:T(8,128)(2,1)S(1)}, bf16[128,768]{1,0:T(8,128)(2,1)S(1)}, u32[]{:S(2)}, u32[]{:S(2)}) collective-permute-start(bf16[128,768]{1,0:T(8,128)(2,1)S(1)} %get-tuple-element.197), channel_id=1, source_target_pairs={{0,16},{8,24},{16,0},{24,8},{1,17},{9,25},{17,1},{25,9},{2,18},{10... | collective-permute-start | bytes 589832 | tf_op jit(solution)/shard_map/ppermute | solution.py:32
  233.2 12.7 %collective-permute-start.35 = (bf16[128,768]{1,0:T(8,128)(2,1)S(1)}, bf16[128,768]{1,0:T(8,128)(2,1)S(1)}, u32[]{:S(2)}, u32[]{:S(2)}) collective-permute-start(bf16[128,768]{1,0:T(8,128)(2,1)S(1)} %get-tuple-element.198), channel_id=1, source_target_pairs={{0,8},{8,0},{16,24},{24,16},{1,9},{9,1},{17,25},{25,17},{2,10},{10... | collective-permute-start | bytes 589832 | tf_op jit(solution)/shard_map/ppermute | solution.py:32
  248.7 12.0 %collective-permute-start.40 = (bf16[256,192]{1,0:T(8,128)(2,1)S(1)}, bf16[256,192]{1,0:T(8,128)(2,1)S(1)}, u32[]{:S(2)}, u32[]{:S(2)}) collective-permute-start(bf16[256,192]{1,0:T(8,128)(2,1)S(1)} %get-tuple-element.215), channel_id=1, source_target_pairs={{0,6},{1,7},{2,4},{3,5},{4,2},{5,3},{6,0},{7,1},{8,14},{9,15},{10,... | collective-permute-start | bytes 294920 | tf_op jit(solution)/shard_map/ppermute | solution.py:32
  253.6 22.6 %collective-permute-start.39 = (bf16[256,192]{1,0:T(8,128)(2,1)S(1)}, bf16[256,192]{1,0:T(8,128)(2,1)S(1)}, u32[]{:S(2)}, u32[]{:S(2)}) collective-permute-start(bf16[256,192]{1,0:T(8,128)(2,1)S(1)} %get-tuple-element.214), channel_id=1, source_target_pairs={{0,4},{1,5},{2,6},{3,7},{4,0},{5,1},{6,2},{7,3},{8,12},{9,13},{10,... | collective-permute-start | bytes 294920 | tf_op jit(solution)/shard_map/ppermute | solution.py:32
  253.6 22.6 %collective-permute-start.38 = (bf16[256,192]{1,0:T(8,128)(2,1)S(1)}, bf16[256,192]{1,0:T(8,128)(2,1)S(1)}, u32[]{:S(2)}, u32[]{:S(2)}) collective-permute-start(bf16[256,192]{1,0:T(8,128)(2,1)S(1)} %get-tuple-element.213), channel_id=1, source_target_pairs={{0,2},{1,3},{2,0},{3,1},{4,6},{5,7},{6,4},{7,5},{8,10},{9,11},{10,... | collective-permute-start | bytes 294920 | tf_op jit(solution)/shard_map/ppermute | solution.py:32
  298.2 26.3 %collective-permute-start.41 = (bf16[1024,384]{1,0:T(8,128)(2,1)}, bf16[1024,384]{1,0:T(8,128)(2,1)}, u32[]{:S(2)}, u32[]{:S(2)}) collective-permute-start(bf16[1024,384]{1,0:T(8,128)(2,1)} %get-tuple-element.79), channel_id=1, source_target_pairs={{0,1},{1,0},{2,3},{3,2},{4,5},{5,4},{6,7},{7,6},{8,9},{9,8},{10,11... | collective-permute-start | bytes 2359304 | tf_op jit(solution)/shard_map/ppermute | solution.py:32
  349.1 14.5 %collective-permute-start.44 = (bf16[4,2,24,1408]{3,2,0,1:T(8,128)(2,1)S(1)}, bf16[4,2,24,1408]{3,2,0,1:T(8,128)(2,1)}, u32[]{:S(2)}, u32[]{:S(2)}) collective-permute-start(bf16[4,2,24,1408]{3,2,0,1:T(8,128)(2,1)S(1)} %select_bitcast_fusion.3), channel_id=1, source_target_pairs={{0,16},{8,24},{16,0},{24,8},{1,17},{9,25},{17,1},{25,9},{2,18},{10... | collective-permute-start | bytes 1622024 | tf_op jit(solution)/shard_map/ppermute | solution.py:32
  349.2 15.7 %collective-permute-start.46 = (bf16[256,768]{1,0:T(8,128)(2,1)}, bf16[256,768]{1,0:T(8,128)(2,1)S(1)}, u32[]{:S(2)}, u32[]{:S(2)}) collective-permute-start(bf16[256,768]{1,0:T(8,128)(2,1)} %get-tuple-element.178), channel_id=1, source_target_pairs={{0,6},{1,7},{2,4},{3,5},{4,2},{5,3},{6,0},{7,1},{8,14},{9,15},{10,... | collective-permute-start | bytes 1179656 | tf_op jit(solution)/shard_map/ppermute | solution.py:32
  349.8 35.9 %collective-permute-start.45 = (bf16[256,768]{1,0:T(8,128)(2,1)}, bf16[256,768]{1,0:T(8,128)(2,1)S(1)}, u32[]{:S(2)}, u32[]{:S(2)}) collective-permute-start(bf16[256,768]{1,0:T(8,128)(2,1)} %get-tuple-element.179), channel_id=1, source_target_pairs={{0,4},{1,5},{2,6},{3,7},{4,0},{5,1},{6,2},{7,3},{8,12},{9,13},{10,... | collective-permute-start | bytes 1179656 | tf_op jit(solution)/shard_map/ppermute | solution.py:32
  (64 other events, 455.5 us)
Sparse Core Ops, SparseCore 0:
  62.2 98.2 all-gather.2
  226.0 96.2 reduce-scatter.1

commit v3 on v2

--- a/solution.py
+++ b/solution.py
@@ -13,6 +13,10 @@
 bf16 = jnp.bfloat16
 f32 = jnp.float32
 VMEM = 56 * 1024 * 1024
+
+
+def effort(flops):
+    return pl.CostEstimate(flops=int(flops), transcendentals=0, bytes_accessed=int(flops) // 320)
 
 
 def dot_nn(left, right):
@@ -143,7 +147,7 @@
                     out_ref[head, rows, size : size + 1] = top + jnp.log(total)
             return carry
 
-        return lax.fori_loop(0, n_z, query_step, carry)
+        return lax.fori_loop(0, n_z, query_step, carry, unroll=2)
 
     lax.fori_loop(0, heads, head_step, 0)
     if not first:
@@ -195,7 +199,8 @@
                 bias = jnp.concatenate([tile_ref[:, c] for c in columns], axis=1)
                 prob = jnp.exp(dot_nn(q, kt_ref[index]) + bias - c_ref[head, rows, size : size + 1])
                 dprob = dot_nn(dc, vt_ref[index])
-                ds = (prob * (dprob - delta_ref[head, rows, :])).astype(bf16)
+                ds_f = prob * (dprob - delta_ref[head, rows, :])
+                ds = ds_f.astype(bf16)
                 dq = dot_nn(ds, k_ref[index])
                 if not first:
                     dq = dq + dq_in[head, rows, :]
@@ -203,11 +208,10 @@
                 dk_ref[index] += dot_tn(q, ds)
                 dv_ref[index] += dot_tn(dc, prob.astype(bf16))
                 for i, c in enumerate(columns):
-                    part = ds[:, i * local_len : (i + 1) * local_len]
-                    grad_ref[:, c] += part.astype(f32)
+                    grad_ref[:, c] += ds_f[:, i * local_len : (i + 1) * local_len]
             return carry
 
-        lax.fori_loop(0, n_z, query_step, 0)
+        lax.fori_loop(0, n_z, query_step, 0, unroll=2)
         folded = grad_ref[...]
         width = folded.shape[1]
         while folded.shape[0] > 1:
@@ -258,6 +262,7 @@
             pltpu.VMEM((heads, rows, size), bf16),
         ],
         compiler_params=pltpu.CompilerParams(vmem_limit_bytes=VMEM),
+        cost_estimate=effort(5000 * heads * rows * length),
         name="attn_fwd",
     )(pos, vec, q, *kvs, *before)
 
@@ -294,6 +299,7 @@
         out_specs=tuple(vmem_specs(len(shapes))),
         scratch_shapes=scratch,
         compiler_params=pltpu.CompilerParams(vmem_limit_bytes=VMEM),
+        cost_estimate=effort(7500 * heads * rows * length),
         name="attn_bwd",
     )(pos, vec, q, dc, c, *kvs, *before)
 
@@ -362,6 +368,7 @@
         out_specs=(whole,) * wholes + (kept,) * kept_out,
         scratch_shapes=[pltpu.VMEM((count, width), f32)] * wholes,
         compiler_params=pltpu.CompilerParams(vmem_limit_bytes=VMEM),
+        cost_estimate=effort(12 * count * width * hidden * n_z * wholes),
         name=name,
     )(*rows, *kept_in, up_down)
 
@@ -384,6 +391,7 @@
         + [pl.BlockSpec((1,) + v.shape[1:], lambda i: (i, 0, 0)) for v in kept],
         out_specs=pl.BlockSpec((1, 2, width, hidden), lambda i: (i, 0, 0, 0)),
         compiler_params=pltpu.CompilerParams(vmem_limit_bytes=VMEM),
+        cost_estimate=effort(5 * 2 * sum(v.shape[0] for v in rows) * width * hidden * n_z),
         name="expert_grad",
     )(*rows, *kept)
 
@@ -405,6 +413,7 @@
         in_specs=vmem_specs(5),
         out_specs=vmem_specs(1)[0],
         compiler_params=pltpu.CompilerParams(vmem_limit_bytes=VMEM),
+        cost_estimate=effort(4 * 2 * a.shape[0] * width * columns),
         name="weight_grad",
     )(a, grad, out_grad, context, small)
 
@@ -561,7 +570,7 @@
     d_own = jnp.concatenate(d_rows, axis=0)
     context_parts, context_f = attn_fwd(*shape, others, pos, vec, q, kvs[1:], before)
     d_other = to_others(d_rows, context_parts)
-    context_parts = context_parts.reshape(n_z, tok, part)
+    context_parts = after(context_parts, *d_rows).reshape(n_z, tok, part)
     context = [swap_z(context_parts[k], k) for k in range(n_z)]
     context = jnp.concatenate(unxor(context, z), axis=1)
 
@@ -593,12 +602,11 @@
         expert_bwd_kernel, "expert_bwd", (dy_other,), (slope,), up_down, bf16, 1
     )
     db_total = add_others(db_own, db_other)
-    y_total, b_late, dy_late = lax.optimization_barrier((y_total, b_other, dy_other))
-    expert_tok = from_experts(y_total)
+    grad_up_down = expert_grad(
+        (b_own, b_other, dy_own, dy_other), (du_own, du_other, g_own, g_other)
+    )
+    expert_tok = from_experts(after(y_total, grad_up_down))
     grad_normed = from_experts(db_total)
-    grad_up_down = expert_grad(
-        (b_own, b_late, dy_own, dy_late), (du_own, du_other, g_own, g_other)
-    )
     grad_up_down = lax.psum_scatter(
         grad_up_down, "seq", scatter_dimension=0, axis_index_groups=z_groups, tiled=True
     )
@@ -635,11 +643,17 @@
     for value in arrived:
         grad_kv = grad_kv + value.astype(f32)
     grad_qkv = jnp.concatenate([grad_q, grad_kv.astype(bf16)], axis=1)
-    grad_a_part = dot_nt(grad_qkv, w_qkv)
-    grad_a_parts = grad_a_part.reshape(n_z, tok, width)
-    grad_a_in = [swap_z(grad_a_parts[k].astype(bf16), k) for k in range(1, n_z)]
-
-    grad_gain_a = jnp.sum(grad_a_part * x_all * scale_all, axis=0)
+    odd, even = list(range(1, n_z, 2)), list(range(0, n_z, 2))
+
+    def take(value, blocks):
+        value = value.reshape(n_z, tok, value.shape[1])
+        return jnp.concatenate([value[k] for k in blocks], axis=0)
+
+    sent = dot_nt(take(grad_qkv, odd), w_qkv)
+    got = swap_z(sent.astype(bf16), 1)
+    kept = dot_nt(take(grad_qkv, even), w_qkv)
+    grad_gain_a = jnp.sum(sent * take(x_all * scale_all, odd), axis=0)
+    grad_gain_a = grad_gain_a + jnp.sum(kept * take(x_all * scale_all, even), axis=0)
     diag = jnp.roll(diag, local_len - 1, axis=1)
     grad_table = lax.dot_general(
         diag, bucket_hot.astype(f32), (((1,), (1,)), ((), ())), precision=highest
@@ -651,14 +665,19 @@
     small = jnp.concatenate(small, axis=1)
     small = jnp.pad(small, ((0, 0), (0, packed - 3 * part - small.shape[1])))
     value = weight_grad(normed_all, grad_qkv, grad_attn, context, small)
-    value = after(value, grad_a_in[0])
     value = value.reshape((2,) * m_bits + (n_z,) + (2,) * n_bits + (w_rows, packed + inner))
     for i, bit in enumerate(dp_bits):
         value = halve(value, m_bits - 1 - i, "dp", bit, (dp & bit) != 0)
-    value = after(value, *grad_a_in)
-    value = after(value, grad_up_down)
+    got = after(got, value)
+    grad_a = (kept + got.astype(f32)).reshape(n_z // 2, tok, width)
+    for bit in bits_of(n_z // 2):
+        half = [k for k in range(0, grad_a.shape[0], 2)]
+        far = jnp.concatenate([grad_a[k + 1] for k in half]).astype(bf16)
+        far = swap_z(far, 2 * bit).astype(f32).reshape(len(half), tok, width)
+        grad_a = jnp.stack([grad_a[k] for k in half]) + far
     for i, bit in enumerate(y_bits):
         value = halve(value, n_bits - i, "seq", bit, (y & bit) != 0)
+    value = after(value, grad_up_down)
     parts = unxor([value[j] for j in range(n_z)], z)
     summed = unxor([swap_z(parts[k], k) for k in range(n_z)], z)
     grad_query, grad_key, grad_value = (
@@ -674,10 +693,7 @@
         [v[:table_rows, table_at : table_at + heads] for v in summed], axis=1
     ).astype(f32)
 
-    grad_a = grad_a_parts[0]
-    grad_a, grad_output = lax.optimization_barrier((grad_a, grad_output))
-    for value in grad_a_in:
-        grad_a = grad_a + value.astype(f32)
+    grad_a = grad_a[0]
     scale_a = scale_all[:tok]
     scaled_a = gain_a * grad_a
     grad_x = grad_hidden + scale_a * scaled_a

time: 423 us -> 410 us (0.969)
  waiting for transfers between devices: 139 us -> 120 us
  other arithmetic: 36 us -> 42.5 us
    ppermute x45 -> x44, waiting for transfers between devices: 128 us -> 109 us  [swap(): return lax.ppermute(value, axis, [(i, i ^ mask) for i in range(size)])]
    ppermute x45 -> x44, starting transfers between devices: 45.5 us -> 48.6 us  [swap(): return lax.ppermute(value, axis, [(i, i ^ mask) for i in range(size)])]
    unnamed x94 -> x80, local copies, waits for them, and re-layouts: 7.72 us -> 9.61 us
  transfers between devices with their start and end apart: 53 -> 52, of which waited for: 26 -> 21; matrix products, arithmetic and copies ran while one was open for 15% -> 16% of each run, Pallas kernels for 29% -> 27%
where the time goes in v3:
time: 410 us; the launch traced here: 402 us
  waiting for transfers between devices  120 us (29%)
  Pallas kernels  118 us (29%)
  starting transfers between devices  64.8 us (16%)
  other arithmetic  42.5 us (10%)
  local copies, waits for them, and re-layouts  26.7 us (7%)
  between operations  15.2 us (4%)
  matrix products  14.7 us (4%)
    ppermute x44, waiting for transfers between devices, swap(): return lax.ppermute(value, axis, [(i, i ^ mask) for i in range(size)])  109 us
    ppermute x44, starting transfers between devices, swap(): return lax.ppermute(value, axis, [(i, i ^ mask) for i in range(size)])  48.6 us
    pallas_call x2, Pallas kernels, attn_bwd(): pl.pallas_call(partial(attn_bwd_kernel, dims, seq_count, heads, size, key...  42.8 us
    pallas_call x3, Pallas kernels, expert_call(): pl.pallas_call(kernel, grid=(n_z,), out_shape=(jax.ShapeDtypeStruct((coun...  32.3 us
    pallas_call x2, Pallas kernels, attn_fwd(): pl.pallas_call(partial(attn_fwd_kernel, dims, seq_count, heads, size, key...  26.9 us
    ppermute x3, starting transfers between devices, local(): below.append(lax.ppermute(below[-1], 'seq', upward))  12.2 us
    pallas_call x1, Pallas kernels, expert_grad(): pl.pallas_call(expert_grad_kernel, grid=(n_z,), out_shape=jax.ShapeDtypeS...  11 us
    unnamed x80, local copies, waits for them, and re-layouts  9.61 us
  transfers between devices with their start and end apart: 52, of which 21 were waited for; matrix products, arithmetic and copies ran while one was open for 16% of the time, Pallas kernels for 27%

profile of v3, /device:TPU:0, one launch (start us, length us, event | category | flops | bytes accessed | tf_op | source)
XLA Modules:
  0.0 402.2 jit_solution(4212371200788710944)
XLA Ops:
  12.5 5.1 %collective-permute-start = (bf16[24,1408]{1,0:T(8,128)(2,1)S(1)}, bf16[24,1408]{1,0:T(8,128)(2,1)S(1)}, u32[]{:S(2)}, u32[]{:S(2)}) collective-permute-start(bf16[24,1408]{1,0:T(8,128)(2,1)S(1)} %get-tuple-element.243), channel_id=1, source_target_pairs={{0,6},{1,7},{2,4},{3,5},{4,2},{5,3},{6,0},{7,1},{8,14},{9,15},{10,... | collective-permute-start | bytes 202760 | tf_op jit(solution)/shard_map/ppermute | solution.py:36
  18.2 3.3 collective-permute-start.6
  25.3 6.3 %collective-permute-done.3 = bf16[4,24,1408]{2,1,0:T(8,128)(2,1)S(1)} collective-permute-done((bf16[4,24,1408]{2,1,0:T(8,128)(2,1)S(1)}, bf16[4,24,1408]{2,1,0:T(8,128)(2,1)S(1)}, u32[]{:S(2)}, u32[]{:S(2)}) %collective-permute-start.3) | collective-permute-done | bytes 270368 | tf_op jit(solution)/shard_map/ppermute | solution.py:36
  33.5 3.7 collective-permute-start.8
  42.5 5.2 %collective-permute-start.10 = (bf16[256,768]{1,0:T(8,128)(2,1)}, bf16[256,768]{1,0:T(8,128)(2,1)}, u32[]{:S(2)}, u32[]{:S(2)}) collective-permute-start(bf16[256,768]{1,0:T(8,128)(2,1)} %collective-permute-done.8), channel_id=1, source_target_pairs={{0,2},{1,3},{2,4},{3,5},{4,6},{5,7},{8,10},{9,11},{10,12},{11,13},... | collective-permute-start | bytes 1179656 | tf_op jit(solution)/shard_map/ppermute | solution.py:485
  54.6 4.3 %collective-permute-done.11 = bf16[256,768]{1,0:T(8,128)(2,1)} collective-permute-done((bf16[256,768]{1,0:T(8,128)(2,1)}, bf16[256,768]{1,0:T(8,128)(2,1)}, u32[]{:S(2)}, u32[]{:S(2)}) %collective-permute-start.11) | collective-permute-done | bytes 393248 | tf_op jit(solution)/shard_map/ppermute | solution.py:486
  75.4 12.3 %attn_fwd.2.refs_1_ = f32[3,1024,128]{2,1,0:T(8,128)} custom-call(s32[2]{0:T(128)} %pad_add_fusion.1.pos_ref, f32[8,4096]{1,0:T(8,128)} %fusion.44.vec_ref, bf16[1024,192]{1,0:T(8,128)(2,1)} %convolution_convert_fusion.3.q_ref, bf16[1024,384]{1,0:T(8,128)(2,1)} %copy-done.34), custom_call_target="tpu_custom_call" | custom-call | flops 15728640000 | bytes 49152000 | tf_op jit(solution)/shard_map/attn_fwd/pallas_call | solution.py:252
  88.6 14.6 %attn_fwd.3 = (bf16[1024,192]{1,0:T(8,128)(2,1)}, f32[3,1024,128]{2,1,0:T(8,128)}) custom-call(s32[2]{0:T(128)} %pad_add_fusion.1.pos_ref, f32[8,4096]{1,0:T(8,128)} %fusion.44.vec_ref, bf16[1024,192]{1,0:T(8,128)(2,1)} %convolution_convert_fusion.3.q_ref, bf16[1024,384]{1,0:T(8,128)(2,1)} %copy-done.35, f32[3,1024,128]{2,1,0:T(8,128)} %attn_fwd.2.refs_1_), custom_call_target="tpu_custom_call" | custom-call | flops 15728640000 | bytes 49152000 | tf_op jit(solution)/shard_map/attn_fwd/pallas_call | solution.py:252
  105.1 3.6 collective-permute-start.16
  111.5 4.7 %collective-permute-done.16 = bf16[256,192]{1,0:T(8,128)(2,1)S(1)} collective-permute-done((bf16[256,192]{1,0:T(8,128)(2,1)}, bf16[256,192]{1,0:T(8,128)(2,1)S(1)}, u32[]{:S(2)}, u32[]{:S(2)}) %collective-permute-start.16) | collective-permute-done | bytes 98336 | tf_op jit(solution)/shard_map/ppermute | solution.py:36
  117.5 15.0 %collective-permute-done.17 = bf16[256,192]{1,0:T(8,128)(2,1)S(1)} collective-permute-done((bf16[256,192]{1,0:T(8,128)(2,1)}, bf16[256,192]{1,0:T(8,128)(2,1)S(1)}, u32[]{:S(2)}, u32[]{:S(2)}) %collective-permute-start.17) | collective-permute-done | bytes 98336 | tf_op jit(solution)/shard_map/ppermute | solution.py:36
  143.9 5.8 %collective-permute-done.20 = bf16[128,896]{1,0:T(8,128)(2,1)} collective-permute-done((bf16[128,896]{1,0:T(8,128)(2,1)S(1)}, bf16[128,896]{1,0:T(8,128)(2,1)}, u32[]{:S(2)}, u32[]{:S(2)}) %collective-permute-start.20) | collective-permute-done | bytes 229408 | tf_op jit(solution)/shard_map/ppermute | solution.py:36
  156.4 4.2 %all-gather.3.cloned.1.call-done = bf16[8,768,384]{2,1,0:T(8,128)(2,1)} async-done(((bf16[2,768,384]{2,1,0:T(8,128)(2,1)}), bf16[8,768,384]{2,1,0:T(8,128)(2,1)}) %all-gather.3.cloned.1.call-update) | async-done | bytes 4718608 | tf_op jit(solution)/shard_map/all_gather | solution.py:551
  160.7 15.3 %expert_own.1 = (f32[512,768]{1,0:T(8,128)}, f32[512,768]{1,0:T(8,128)}, bf16[4,512,384]{2,1,0:T(8,128)(2,1)}, bf16[4,512,384]{2,1,0:T(8,128)(2,1)}) custom-call(bf16[512,896]{1,0:T(8,128)(2,1)} %copy-done.13, bf16[512,768]{1,0:T(8,128)(2,1)} %multiply_convert_fusion.2.dy_ref, bf16[4,2,768,384]{3,2,1,0:T(8,128)(2,1)} %bitcast.170), custom_call_target="tpu_custom_call" | custom-call | flops 14495514624 | bytes 45298484 | tf_op jit(solution)/shard_map/expert_own/pallas_call | solution.py:362
  180.8 9.0 %expert_fwd.1 = (bf16[512,768]{1,0:T(8,128)(2,1)}, bf16[4,512,384]{2,1,0:T(8,128)(2,1)}, bf16[4,512,384]{2,1,0:T(8,128)(2,1)}) custom-call(bf16[512,896]{1,0:T(8,128)(2,1)} %copy-done.23, bf16[4,2,768,384]{3,2,1,0:T(8,128)(2,1)} %bitcast.171), custom_call_target="tpu_custom_call" | custom-call | flops 7247757312 | bytes 22649240 | tf_op jit(solution)/shard_map/expert_fwd/pallas_call | solution.py:362
  194.8 8.0 %expert_bwd.1 = (bf16[512,768]{1,0:T(8,128)(2,1)}, bf16[4,512,384]{2,1,0:T(8,128)(2,1)}) custom-call(bf16[512,768]{1,0:T(8,128)(2,1)} %multiply_convert_fusion.1.dy_ref.dy_other, bf16[4,512,384]{2,1,0:T(8,128)(2,1)} %get-tuple-element.68.slope_ref, bf16[4,2,768,384]{3,2,1,0:T(8,128)(2,1)} %bitcast.172), custom_call_target="tpu_custom_call" | custom-call | flops 7247757312 | bytes 22649240 | tf_op jit(solution)/shard_map/expert_bwd/pallas_call | solution.py:362
  203.4 11.0 %expert_grad.1 = bf16[4,2,768,384]{3,2,1,0:T(8,128)(2,1)} custom-call(bf16[512,896]{1,0:T(8,128)(2,1)} %copy-done.13, bf16[512,896]{1,0:T(8,128)(2,1)} %copy-done.23, bf16[512,768]{1,0:T(8,128)(2,1)} %multiply_convert_fusion.2.dy_ref, bf16[512,768]{1,0:T(8,128)(2,1)} %multiply_convert_fusion.1.dy_ref.dy_other, ...), custom_call_target="tpu_custom_call" | custom-call | flops 24159191040 | bytes 75497472 | tf_op jit(solution)/shard_map/expert_grad/pallas_call | solution.py:386
  218.2 9.3 %collective-permute-done.34 = bf16[512,768]{1,0:T(8,128)(2,1)} collective-permute-done((bf16[512,768]{1,0:T(8,128)(2,1)}, bf16[512,768]{1,0:T(8,128)(2,1)}, u32[]{:S(2)}, u32[]{:S(2)}) %collective-permute-start.34) | collective-permute-done | bytes 786464 | tf_op jit(solution)/shard_map/ppermute | solution.py:36
  232.1 4.1 %collective-permute-done.37 = bf16[128,768]{1,0:T(8,128)(2,1)S(1)} collective-permute-done((bf16[128,768]{1,0:T(8,128)(2,1)S(1)}, bf16[128,768]{1,0:T(8,128)(2,1)S(1)}, u32[]{:S(2)}, u32[]{:S(2)}) %collective-permute-start.37) | collective-permute-done | bytes 196640 | tf_op jit(solution)/shard_map/ppermute | solution.py:36
  236.2 4.2 %collective-permute-done.36 = bf16[128,768]{1,0:T(8,128)(2,1)S(1)} collective-permute-done((bf16[128,768]{1,0:T(8,128)(2,1)S(1)}, bf16[128,768]{1,0:T(8,128)(2,1)S(1)}, u32[]{:S(2)}, u32[]{:S(2)}) %collective-permute-start.36) | collective-permute-done | bytes 196640 | tf_op jit(solution)/shard_map/ppermute | solution.py:36
  243.9 3.7 collective-permute-start.38
  247.9 6.3 %collective-permute-done.40 = bf16[256,192]{1,0:T(8,128)(2,1)S(1)} collective-permute-done((bf16[256,192]{1,0:T(8,128)(2,1)S(1)}, bf16[256,192]{1,0:T(8,128)(2,1)S(1)}, u32[]{:S(2)}, u32[]{:S(2)}) %collective-permute-start.40) | collective-permute-done | bytes 98336 | tf_op jit(solution)/shard_map/ppermute | solution.py:36
  254.2 14.0 %collective-permute-done.39 = bf16[256,192]{1,0:T(8,128)(2,1)S(1)} collective-permute-done((bf16[256,192]{1,0:T(8,128)(2,1)S(1)}, bf16[256,192]{1,0:T(8,128)(2,1)S(1)}, u32[]{:S(2)}, u32[]{:S(2)}) %collective-permute-start.39) | collective-permute-done | bytes 98336 | tf_op jit(solution)/shard_map/ppermute | solution.py:36
  269.1 20.4 %attn_bwd.2 = (f32[3,1024,64]{2,1,0:T(8,128)}, f32[8,4096]{1,0:T(8,128)}, bf16[1024,384]{1,0:T(8,128)(2,1)}) custom-call(s32[2]{0:T(128)} %pad_add_fusion.1.pos_ref, f32[8,4096]{1,0:T(8,128)} %fusion.44.vec_ref, bf16[1024,192]{1,0:T(8,128)(2,1)} %convolution_convert_fusion.3.q_ref, bf16[1024,192]{1,0:T(8,128)(2,1)} %pad_maximum_fusion.7.refs_0_, ...), custom_call_target="tpu_custom_call" | custom-call | flops 23592960000 | bytes 73728000 | tf_op jit(solution)/shard_map/attn_bwd/pallas_call | solution.py:294
  291.1 22.3 %attn_bwd.3 = (bf16[1024,192]{1,0:T(8,128)(2,1)}, f32[8,4096]{1,0:T(8,128)}, f32[1024,384]{1,0:T(8,128)}) custom-call(s32[2]{0:T(128)} %pad_add_fusion.1.pos_ref, f32[8,4096]{1,0:T(8,128)} %fusion.44.vec_ref, bf16[1024,192]{1,0:T(8,128)(2,1)} %convolution_convert_fusion.3.q_ref, bf16[1024,192]{1,0:T(8,128)(2,1)} %pad_maximum_fusion.7.refs_0_, ...), custom_call_target="tpu_custom_call" | custom-call | flops 23592960000 | bytes 73728000 | tf_op jit(solution)/shard_map/attn_bwd/pallas_call | solution.py:294
  325.3 5.2 %weight_grad.1 = bf16[768,1408]{1,0:T(8,128)(2,1)} custom-call(bf16[1024,768]{1,0:T(8,128)(2,1)} %copy-done.11, bf16[1024,576]{1,0:T(8,128)(2,1)} %pad_maximum_fusion.grad_ref, bf16[256,768]{1,0:T(8,128)(2,1)} %copy-done.22, bf16[256,768]{1,0:T(8,128)(2,1)} %copy-done.20, f32[768,64]{1,0:T(8,128)} %pad.29.small_ref), custom_call_target="tpu_custom_call" | custom-call | flops 8858370048 | bytes 27682406 | tf_op jit(solution)/shard_map/weight_grad/pallas_call | solution.py:410
  332.5 2.8 collective-permute-done.43
  340.7 11.7 %collective-permute-done.44 = bf16[4,2,24,1408]{3,2,0,1:T(8,128)(2,1)} collective-permute-done((bf16[4,2,24,1408]{3,2,0,1:T(8,128)(2,1)}, bf16[4,2,24,1408]{3,2,0,1:T(8,128)(2,1)}, u32[]{:S(2)}, u32[]{:S(2)}) %collective-permute-start.44) | collective-permute-done | bytes 540704 | tf_op jit(solution)/shard_map/ppermute | solution.py:36
  353.7 5.1 %collective-permute-done.42 = bf16[512,768]{1,0:T(8,128)(2,1)S(1)} collective-permute-done((bf16[512,768]{1,0:T(8,128)(2,1)}, bf16[512,768]{1,0:T(8,128)(2,1)S(1)}, u32[]{:S(2)}, u32[]{:S(2)}) %collective-permute-start.42) | collective-permute-done | bytes 786464 | tf_op jit(solution)/shard_map/ppermute | solution.py:36
  362.0 4.2 %collective-permute-done.46 = bf16[4,24,1408]{2,1,0:T(8,128)(2,1)S(1)} collective-permute-done((bf16[4,24,1408]{2,1,0:T(8,128)(2,1)S(1)}, bf16[4,24,1408]{2,1,0:T(8,128)(2,1)S(1)}, u32[]{:S(2)}, u32[]{:S(2)}) %collective-permute-start.46) | collective-permute-done | bytes 270368 | tf_op jit(solution)/shard_map/ppermute | solution.py:36
  366.3 12.4 %collective-permute-done.45 = bf16[256,768]{1,0:T(8,128)(2,1)S(1)} collective-permute-done((bf16[256,768]{1,0:T(8,128)(2,1)S(1)}, bf16[256,768]{1,0:T(8,128)(2,1)S(1)}, u32[]{:S(2)}, u32[]{:S(2)}) %collective-permute-start.45) | collective-permute-done | bytes 393248 | tf_op jit(solution)/shard_map/ppermute | solution.py:36
  380.2 3.5 collective-permute-start.47
  (287 shorter events, 126.2 us)
Async XLA Ops:
  7.2 153.5 %all-gather.3.cloned.1.call-start = ((), (), s32[]{:S(2)}) async-start(), calls=%async_computation.2 | async-start | bytes 5898240 | tf_op jit(solution)/shard_map/all_gather | solution.py:551
  18.2 15.3 %collective-permute-start.6 = (bf16[256,768]{1,0:T(8,128)(2,1)S(1)}, bf16[256,768]{1,0:T(8,128)(2,1)S(1)}, u32[]{:S(2)}, u32[]{:S(2)}) collective-permute-start(bf16[256,768]{1,0:T(8,128)(2,1)S(1)} %bitcast.133), channel_id=1, source_target_pairs={{0,2},{1,3},{2,4},{3,5},{4,6},{5,7},{8,10},{9,11},{10,12},{11,13},... | collective-permute-start | bytes 1179656 | tf_op jit(solution)/shard_map/ppermute | solution.py:485
  21.6 15.7 %collective-permute-start.7 = (bf16[256,768]{1,0:T(8,128)(2,1)S(1)}, bf16[256,768]{1,0:T(8,128)(2,1)S(1)}, u32[]{:S(2)}, u32[]{:S(2)}) collective-permute-start(bf16[256,768]{1,0:T(8,128)(2,1)S(1)} %bitcast.134), channel_id=1, source_target_pairs={{2,0},{3,1},{4,2},{5,3},{6,4},{7,5},{10,8},{11,9},{12,10},{13,11},... | collective-permute-start | bytes 1179656 | tf_op jit(solution)/shard_map/ppermute | solution.py:486
  31.7 17.3 %collective-permute-start.4 = (bf16[2,4,24,1408]{3,2,0,1:T(8,128)(2,1)S(1)}, bf16[2,4,24,1408]{3,2,0,1:T(8,128)(2,1)}, u32[]{:S(2)}, u32[]{:S(2)}) collective-permute-start(bf16[2,4,24,1408]{3,2,0,1:T(8,128)(2,1)S(1)} %pad_maximum_fusion.6), channel_id=1, source_target_pairs={{0,16},{8,24},{16,0},{24,8},{1,17},{9,25},{17,1},{25,9},{2,18},{10... | collective-permute-start | bytes 1622024 | tf_op jit(solution)/shard_map/ppermute | solution.py:36
  39.8 47.9 %collective-permute-start.13 = (bf16[128,768]{1,0:T(8,128)(2,1)}, bf16[128,768]{1,0:T(8,128)(2,1)}, u32[]{:S(2)}, u32[]{:S(2)}) collective-permute-start(bf16[128,768]{1,0:T(8,128)(2,1)} %get-tuple-element.204), channel_id=1, source_target_pairs={{0,8},{8,0},{16,24},{24,16},{1,9},{9,1},{17,25},{25,17},{2,10},{10... | collective-permute-start | bytes 589832 | tf_op jit(solution)/shard_map/ppermute | solution.py:36
  39.8 47.9 %collective-permute-start.14 = (bf16[128,768]{1,0:T(8,128)(2,1)}, bf16[128,768]{1,0:T(8,128)(2,1)}, u32[]{:S(2)}, u32[]{:S(2)}) collective-permute-start(bf16[128,768]{1,0:T(8,128)(2,1)} %get-tuple-element.203), channel_id=1, source_target_pairs={{0,16},{8,24},{16,0},{24,8},{1,17},{9,25},{17,1},{25,9},{2,18},{10... | collective-permute-start | bytes 589832 | tf_op jit(solution)/shard_map/ppermute | solution.py:36
  42.5 11.5 %collective-permute-start.10 = (bf16[256,768]{1,0:T(8,128)(2,1)}, bf16[256,768]{1,0:T(8,128)(2,1)}, u32[]{:S(2)}, u32[]{:S(2)}) collective-permute-start(bf16[256,768]{1,0:T(8,128)(2,1)} %collective-permute-done.8), channel_id=1, source_target_pairs={{0,2},{1,3},{2,4},{3,5},{4,6},{5,7},{8,10},{9,11},{10,12},{11,13},... | collective-permute-start | bytes 1179656 | tf_op jit(solution)/shard_map/ppermute | solution.py:485
  54.0 33.7 %collective-permute-start.15 = (bf16[128,768]{1,0:T(8,128)(2,1)}, bf16[128,768]{1,0:T(8,128)(2,1)}, u32[]{:S(2)}, u32[]{:S(2)}) collective-permute-start(bf16[128,768]{1,0:T(8,128)(2,1)} %get-tuple-element.202), channel_id=1, source_target_pairs={{0,24},{8,16},{16,8},{24,0},{1,25},{9,17},{17,9},{25,1},{2,26},{10... | collective-permute-start | bytes 589832 | tf_op jit(solution)/shard_map/ppermute | solution.py:36
  60.5 319.7 %reduce-scatter.2.cloned.1.call-start = ((), (), s32[]{:S(2)}) async-start(), calls=%async_computation.1 | async-start | bytes 5898240 | tf_op jit(solution)/shard_map/reduce_scatter | solution.py:610
  70.5 17.2 %collective-permute-start.12 = (bf16[1024,384]{1,0:T(8,128)(2,1)S(1)}, bf16[1024,384]{1,0:T(8,128)(2,1)S(1)}, u32[]{:S(2)}, u32[]{:S(2)}) collective-permute-start(bf16[1024,384]{1,0:T(8,128)(2,1)S(1)} %convolution_convert_fusion.1.refs_0_.refs_2_), channel_id=1, source_target_pairs={{0,1},{1,0},{2,3},{3,2},{4,5},{5,4},{6,7},{7,6},{8,9},{9,8},{10,11... | collective-permute-start | bytes 2359304 | tf_op jit(solution)/shard_map/ppermute | solution.py:36
  108.7 23.8 %collective-permute-start.17 = (bf16[256,192]{1,0:T(8,128)(2,1)}, bf16[256,192]{1,0:T(8,128)(2,1)S(1)}, u32[]{:S(2)}, u32[]{:S(2)}) collective-permute-start(bf16[256,192]{1,0:T(8,128)(2,1)} %get-tuple-element.209), channel_id=1, source_target_pairs={{0,4},{1,5},{2,6},{3,7},{4,0},{5,1},{6,2},{7,3},{8,12},{9,13},{10,... | collective-permute-start | bytes 294920 | tf_op jit(solution)/shard_map/ppermute | solution.py:36
  108.7 25.3 %collective-permute-start.18 = (bf16[256,192]{1,0:T(8,128)(2,1)S(1)}, bf16[256,192]{1,0:T(8,128)(2,1)}, u32[]{:S(2)}, u32[]{:S(2)}) collective-permute-start(bf16[256,192]{1,0:T(8,128)(2,1)S(1)} %get-tuple-element.208), channel_id=1, source_target_pairs={{0,2},{1,3},{2,0},{3,1},{4,6},{5,7},{6,4},{7,5},{8,10},{9,11},{10,... | collective-permute-start | bytes 294920 | tf_op jit(solution)/shard_map/ppermute | solution.py:36
  109.5 28.8 %collective-permute-start.30 = (bf16[128,768]{1,0:T(8,128)(2,1)}, bf16[128,768]{1,0:T(8,128)(2,1)}, u32[]{:S(2)}, u32[]{:S(2)}) collective-permute-start(bf16[128,768]{1,0:T(8,128)(2,1)} %collective-permute-done.15), channel_id=1, source_target_pairs={{0,1},{1,0},{2,3},{3,2},{4,5},{5,4},{6,7},{7,6},{8,9},{9,8},{10,11... | collective-permute-start | bytes 589832 | tf_op jit(solution)/shard_map/ppermute | solution.py:36
  110.8 28.3 %collective-permute-start.29 = (bf16[128,768]{1,0:T(8,128)(2,1)}, bf16[128,768]{1,0:T(8,128)(2,1)}, u32[]{:S(2)}, u32[]{:S(2)}) collective-permute-start(bf16[128,768]{1,0:T(8,128)(2,1)} %collective-permute-done.14), channel_id=1, source_target_pairs={{0,1},{1,0},{2,3},{3,2},{4,5},{5,4},{6,7},{7,6},{8,9},{9,8},{10,11... | collective-permute-start | bytes 589832 | tf_op jit(solution)/shard_map/ppermute | solution.py:36
  116.2 25.6 %collective-permute-start.28 = (bf16[128,768]{1,0:T(8,128)(2,1)}, bf16[128,768]{1,0:T(8,128)(2,1)}, u32[]{:S(2)}, u32[]{:S(2)}) collective-permute-start(bf16[128,768]{1,0:T(8,128)(2,1)} %collective-permute-done.13), channel_id=1, source_target_pairs={{0,1},{1,0},{2,3},{3,2},{4,5},{5,4},{6,7},{7,6},{8,9},{9,8},{10,11... | collective-permute-start | bytes 589832 | tf_op jit(solution)/shard_map/ppermute | solution.py:36
  138.2 12.0 %collective-permute-start.21 = (bf16[128,896]{1,0:T(8,128)(2,1)S(1)}, bf16[128,896]{1,0:T(8,128)(2,1)}, u32[]{:S(2)}, u32[]{:S(2)}) collective-permute-start(bf16[128,896]{1,0:T(8,128)(2,1)S(1)} %get-tuple-element.186), channel_id=1, source_target_pairs={{0,24},{8,16},{16,8},{24,0},{1,25},{9,17},{17,9},{25,1},{2,26},{10... | collective-permute-start | bytes 688136 | tf_op jit(solution)/shard_map/ppermute | solution.py:36
  141.8 34.2 %collective-permute-start.22 = (bf16[128,896]{1,0:T(8,128)(2,1)S(1)}, bf16[128,896]{1,0:T(8,128)(2,1)}, u32[]{:S(2)}, u32[]{:S(2)}) collective-permute-start(bf16[128,896]{1,0:T(8,128)(2,1)S(1)} %get-tuple-element.185), channel_id=1, source_target_pairs={{0,1},{1,0},{2,3},{3,2},{4,5},{5,4},{6,7},{7,6},{8,9},{9,8},{10,11... | collective-permute-start | bytes 688136 | tf_op jit(solution)/shard_map/ppermute | solution.py:36
  142.5 33.5 %collective-permute-start.23 = (bf16[128,896]{1,0:T(8,128)(2,1)}, bf16[128,896]{1,0:T(8,128)(2,1)}, u32[]{:S(2)}, u32[]{:S(2)}) collective-permute-start(bf16[128,896]{1,0:T(8,128)(2,1)} %collective-permute-done.19), channel_id=1, source_target_pairs={{0,1},{1,0},{2,3},{3,2},{4,5},{5,4},{6,7},{7,6},{8,9},{9,8},{10,11... | collective-permute-start | bytes 688136 | tf_op jit(solution)/shard_map/ppermute | solution.py:36
  149.6 26.4 %collective-permute-start.24 = (bf16[128,896]{1,0:T(8,128)(2,1)}, bf16[128,896]{1,0:T(8,128)(2,1)}, u32[]{:S(2)}, u32[]{:S(2)}) collective-permute-start(bf16[128,896]{1,0:T(8,128)(2,1)} %collective-permute-done.20), channel_id=1, source_target_pairs={{0,1},{1,0},{2,3},{3,2},{4,5},{5,4},{6,7},{7,6},{8,9},{9,8},{10,11... | collective-permute-start | bytes 688136 | tf_op jit(solution)/shard_map/ppermute | solution.py:36
  150.2 26.7 %collective-permute-start.25 = (bf16[128,896]{1,0:T(8,128)(2,1)}, bf16[128,896]{1,0:T(8,128)(2,1)}, u32[]{:S(2)}, u32[]{:S(2)}) collective-permute-start(bf16[128,896]{1,0:T(8,128)(2,1)} %collective-permute-done.21), channel_id=1, source_target_pairs={{0,1},{1,0},{2,3},{3,2},{4,5},{5,4},{6,7},{7,6},{8,9},{9,8},{10,11... | collective-permute-start | bytes 688136 | tf_op jit(solution)/shard_map/ppermute | solution.py:36
  191.0 23.5 %collective-permute-start.26 = (bf16[512,768]{1,0:T(8,128)(2,1)}, bf16[512,768]{1,0:T(8,128)(2,1)}, u32[]{:S(2)}, u32[]{:S(2)}) collective-permute-start(bf16[512,768]{1,0:T(8,128)(2,1)} %get-tuple-element.62), channel_id=1, source_target_pairs={{0,1},{1,0},{2,3},{3,2},{4,5},{5,4},{6,7},{7,6},{8,9},{9,8},{10,11... | collective-permute-start | bytes 2359304 | tf_op jit(solution)/shard_map/ppermute | solution.py:36
  202.9 24.7 %collective-permute-start.34 = (bf16[512,768]{1,0:T(8,128)(2,1)}, bf16[512,768]{1,0:T(8,128)(2,1)}, u32[]{:S(2)}, u32[]{:S(2)}) collective-permute-start(bf16[512,768]{1,0:T(8,128)(2,1)} %get-tuple-element.74), channel_id=1, source_target_pairs={{0,1},{1,0},{2,3},{3,2},{4,5},{5,4},{6,7},{7,6},{8,9},{9,8},{10,11... | collective-permute-start | bytes 2359304 | tf_op jit(solution)/shard_map/ppermute | solution.py:36
  216.3 14.3 %collective-permute-start.33 = (bf16[128,768]{1,0:T(8,128)(2,1)S(1)}, bf16[128,768]{1,0:T(8,128)(2,1)S(1)}, u32[]{:S(2)}, u32[]{:S(2)}) collective-permute-start(bf16[128,768]{1,0:T(8,128)(2,1)S(1)} %get-tuple-element.201), channel_id=1, source_target_pairs={{0,24},{8,16},{16,8},{24,0},{1,25},{9,17},{17,9},{25,1},{2,26},{10... | collective-permute-start | bytes 589832 | tf_op jit(solution)/shard_map/ppermute | solution.py:36
  216.8 14.1 %collective-permute-start.32 = (bf16[128,768]{1,0:T(8,128)(2,1)S(1)}, bf16[128,768]{1,0:T(8,128)(2,1)S(1)}, u32[]{:S(2)}, u32[]{:S(2)}) collective-permute-start(bf16[128,768]{1,0:T(8,128)(2,1)S(1)} %get-tuple-element.199), channel_id=1, source_target_pairs={{0,16},{8,24},{16,0},{24,8},{1,17},{9,25},{17,1},{25,9},{2,18},{10... | collective-permute-start | bytes 589832 | tf_op jit(solution)/shard_map/ppermute | solution.py:36
  218.0 13.0 %collective-permute-start.31 = (bf16[128,768]{1,0:T(8,128)(2,1)S(1)}, bf16[128,768]{1,0:T(8,128)(2,1)S(1)}, u32[]{:S(2)}, u32[]{:S(2)}) collective-permute-start(bf16[128,768]{1,0:T(8,128)(2,1)S(1)} %get-tuple-element.200), channel_id=1, source_target_pairs={{0,8},{8,0},{16,24},{24,16},{1,9},{9,1},{17,25},{25,17},{2,10},{10... | collective-permute-start | bytes 589832 | tf_op jit(solution)/shard_map/ppermute | solution.py:36
  229.1 11.3 %collective-permute-start.36 = (bf16[128,768]{1,0:T(8,128)(2,1)S(1)}, bf16[128,768]{1,0:T(8,128)(2,1)S(1)}, u32[]{:S(2)}, u32[]{:S(2)}) collective-permute-start(bf16[128,768]{1,0:T(8,128)(2,1)S(1)} %get-tuple-element.196), channel_id=1, source_target_pairs={{0,16},{8,24},{16,0},{24,8},{1,17},{9,25},{17,1},{25,9},{2,18},{10... | collective-permute-start | bytes 589832 | tf_op jit(solution)/shard_map/ppermute | solution.py:36
  243.9 24.3 %collective-permute-start.39 = (bf16[256,192]{1,0:T(8,128)(2,1)S(1)}, bf16[256,192]{1,0:T(8,128)(2,1)S(1)}, u32[]{:S(2)}, u32[]{:S(2)}) collective-permute-start(bf16[256,192]{1,0:T(8,128)(2,1)S(1)} %get-tuple-element.213), channel_id=1, source_target_pairs={{0,4},{1,5},{2,6},{3,7},{4,0},{5,1},{6,2},{7,3},{8,12},{9,13},{10,... | collective-permute-start | bytes 294920 | tf_op jit(solution)/shard_map/ppermute | solution.py:36
  243.9 24.3 %collective-permute-start.38 = (bf16[256,192]{1,0:T(8,128)(2,1)S(1)}, bf16[256,192]{1,0:T(8,128)(2,1)S(1)}, u32[]{:S(2)}, u32[]{:S(2)}) collective-permute-start(bf16[256,192]{1,0:T(8,128)(2,1)S(1)} %get-tuple-element.212), channel_id=1, source_target_pairs={{0,2},{1,3},{2,0},{3,1},{4,6},{5,7},{6,4},{7,5},{8,10},{9,11},{10,... | collective-permute-start | bytes 294920 | tf_op jit(solution)/shard_map/ppermute | solution.py:36
  289.6 26.1 %collective-permute-start.41 = (bf16[1024,384]{1,0:T(8,128)(2,1)}, bf16[1024,384]{1,0:T(8,128)(2,1)}, u32[]{:S(2)}, u32[]{:S(2)}) collective-permute-start(bf16[1024,384]{1,0:T(8,128)(2,1)} %get-tuple-element.80), channel_id=1, source_target_pairs={{0,1},{1,0},{2,3},{3,2},{4,5},{5,4},{6,7},{7,6},{8,9},{9,8},{10,11... | collective-permute-start | bytes 2359304 | tf_op jit(solution)/shard_map/ppermute | solution.py:36
  337.8 14.6 %collective-permute-start.44 = (bf16[4,2,24,1408]{3,2,0,1:T(8,128)(2,1)}, bf16[4,2,24,1408]{3,2,0,1:T(8,128)(2,1)}, u32[]{:S(2)}, u32[]{:S(2)}) collective-permute-start(bf16[4,2,24,1408]{3,2,0,1:T(8,128)(2,1)} %select_bitcast_fusion.3), channel_id=1, source_target_pairs={{0,16},{8,24},{16,0},{24,8},{1,17},{9,25},{17,1},{25,9},{2,18},{10... | collective-permute-start | bytes 1622024 | tf_op jit(solution)/shard_map/ppermute | solution.py:36
  339.2 19.5 %collective-permute-start.42 = (bf16[512,768]{1,0:T(8,128)(2,1)}, bf16[512,768]{1,0:T(8,128)(2,1)S(1)}, u32[]{:S(2)}, u32[]{:S(2)}) collective-permute-start(bf16[512,768]{1,0:T(8,128)(2,1)} %get-tuple-element.174), channel_id=1, source_target_pairs={{0,2},{1,3},{2,0},{3,1},{4,6},{5,7},{6,4},{7,5},{8,10},{9,11},{10,... | collective-permute-start | bytes 2359304 | tf_op jit(solution)/shard_map/ppermute | solution.py:36
  359.7 19.1 %collective-permute-start.45 = (bf16[256,768]{1,0:T(8,128)(2,1)S(1)}, bf16[256,768]{1,0:T(8,128)(2,1)S(1)}, u32[]{:S(2)}, u32[]{:S(2)}) collective-permute-start(bf16[256,768]{1,0:T(8,128)(2,1)S(1)} %slice.654), channel_id=1, source_target_pairs={{0,4},{1,5},{2,6},{3,7},{4,0},{5,1},{6,2},{7,3},{8,12},{9,13},{10,... | collective-permute-start | bytes 1179656 | tf_op jit(solution)/shard_map/ppermute | solution.py:36
  (56 other events, 475.9 us)
Sparse Core Ops, SparseCore 0:
  60.6 99.9 all-gather.2
  214.6 91.9 reduce-scatter.1

commit v4 on v3

--- a/solution.py
+++ b/solution.py
@@ -517,16 +517,16 @@
         moved = [swap_y(v, k) for k in range(1, n_y) for v in parts]
         return jnp.concatenate([after(v, *others) for v in moved], axis=0)
 
-    def from_experts(total):
+    def from_experts(total, *others):
         blocks = total.astype(bf16).reshape(n_dp, capacity, width)
         back = [swap_dp(blocks[k], k) for k in range(n_dp)]
+        if others:
+            back = [after(v, *others) for v in back]
         return dot_tn(place_b, jnp.concatenate(back, axis=0))
 
-    def add_others(own, values):
+    def swap_others(values):
         split = values.reshape(n_y - 1, n_dp * capacity, width)
-        for k in range(1, n_y):
-            own = own + swap_y(split[k - 1], k).astype(f32)
-        return own
+        return [swap_y(split[k - 1], k) for k in range(1, n_y)]
 
     upstream_b = cotangent.reshape(tok, width)
     upstream = upstream_b.astype(f32)
@@ -589,24 +589,27 @@
     b_rows = to_experts(jnp.concatenate([normed_f, b_gate], axis=1))
     b_own = jnp.concatenate(b_rows, axis=0)
     dy_own = weigh(d_own, b_own)
-    y_own, db_own, g_own, du_own = expert_call(
-        expert_own_kernel, "expert_own", (b_own, dy_own), (), up_down, f32, 2
-    )
-    b_other = to_others(b_rows, y_own)
+    b_other = to_others(b_rows)
     dy_other = weigh(d_other, b_other)
     y_other, g_other, slope = expert_call(
         expert_fwd_kernel, "expert_fwd", (b_other,), (), up_down, bf16, 1
     )
-    y_total = add_others(y_own, y_other)
     db_other, du_other = expert_call(
         expert_bwd_kernel, "expert_bwd", (dy_other,), (slope,), up_down, bf16, 1
     )
-    db_total = add_others(db_own, db_other)
+    y_got = swap_others(y_other)
+    db_got = swap_others(db_other)
+    b_own = after(b_own, db_other, *y_got)
+    y_own, db_own, g_own, du_own = expert_call(
+        expert_own_kernel, "expert_own", (b_own, dy_own), (), up_down, f32, 2
+    )
+    y_total = y_own + sum(v.astype(f32) for v in y_got)
+    db_total = db_own + sum(v.astype(f32) for v in db_got)
+    expert_tok = from_experts(y_total)
     grad_up_down = expert_grad(
-        (b_own, b_other, dy_own, dy_other), (du_own, du_other, g_own, g_other)
-    )
-    expert_tok = from_experts(after(y_total, grad_up_down))
-    grad_normed = from_experts(db_total)
+        (b_own, b_other, after(dy_own, db_total), dy_other), (du_own, du_other, g_own, g_other)
+    )
+    grad_normed = from_experts(db_total, grad_up_down)
     grad_up_down = lax.psum_scatter(
         grad_up_down, "seq", scatter_dimension=0, axis_index_groups=z_groups, tiled=True
     )
@@ -673,11 +676,13 @@
     for bit in bits_of(n_z // 2):
         half = [k for k in range(0, grad_a.shape[0], 2)]
         far = jnp.concatenate([grad_a[k + 1] for k in half]).astype(bf16)
-        far = swap_z(far, 2 * bit).astype(f32).reshape(len(half), tok, width)
-        grad_a = jnp.stack([grad_a[k] for k in half]) + far
+        far = swap_z(far, 2 * bit)
+        grad_a = jnp.stack([grad_a[k] for k in half])
+        if len(half) > 1:
+            grad_a = grad_a + far.astype(f32).reshape(len(half), tok, width)
     for i, bit in enumerate(y_bits):
         value = halve(value, n_bits - i, "seq", bit, (y & bit) != 0)
-    value = after(value, grad_up_down)
+    value = after(value, grad_a, grad_up_down)
     parts = unxor([value[j] for j in range(n_z)], z)
     summed = unxor([swap_z(parts[k], k) for k in range(n_z)], z)
     grad_query, grad_key, grad_value = (
@@ -693,7 +698,8 @@
         [v[:table_rows, table_at : table_at + heads] for v in summed], axis=1
     ).astype(f32)
 
-    grad_a = grad_a[0]
+    far, grad_output = lax.optimization_barrier((far, grad_output))
+    grad_a = grad_a[0] + far.astype(f32)
     scale_a = scale_all[:tok]
     scaled_a = gain_a * grad_a
     grad_x = grad_hidden + scale_a * scaled_a

time: 410 us -> 404 us (0.985)
  starting transfers between devices: 64.8 us -> 78.5 us
  waiting for transfers between devices: 120 us -> 108 us
    ppermute x44, starting transfers between devices: 48.6 us -> 59.4 us  [swap(): return lax.ppermute(value, axis, [(i, i ^ mask) for i in range(size)])]
    ppermute x44, waiting for transfers between devices: 109 us -> 98.4 us  [swap(): return lax.ppermute(value, axis, [(i, i ^ mask) for i in range(size)])]
    unnamed x80 -> x81, local copies, waits for them, and re-layouts: 9.61 us -> 5.13 us
  transfers between devices with their start and end apart: 52 -> 52, of which waited for: 21 -> 25; matrix products, arithmetic and copies ran while one was open for 16% -> 15% of each run, Pallas kernels for 27% -> 28%
where the time goes in v4:
time: 404 us; the launch traced here: 397 us
  Pallas kernels  119 us (29%)
  waiting for transfers between devices  108 us (27%)
  starting transfers between devices  78.5 us (19%)
  other arithmetic  39.4 us (10%)
  local copies, waits for them, and re-layouts  23.6 us (6%)
  between operations  15.2 us (4%)
  matrix products  14.2 us (4%)
    ppermute x44, waiting for transfers between devices, swap(): return lax.ppermute(value, axis, [(i, i ^ mask) for i in range(size)])  98.4 us
    ppermute x44, starting transfers between devices, swap(): return lax.ppermute(value, axis, [(i, i ^ mask) for i in range(size)])  59.4 us
    pallas_call x2, Pallas kernels, attn_bwd(): pl.pallas_call(partial(attn_bwd_kernel, dims, seq_count, heads, size, key...  43.1 us
    pallas_call x3, Pallas kernels, expert_call(): pl.pallas_call(kernel, grid=(n_z,), out_shape=(jax.ShapeDtypeStruct((coun...  32.1 us
    pallas_call x2, Pallas kernels, attn_fwd(): pl.pallas_call(partial(attn_fwd_kernel, dims, seq_count, heads, size, key...  27.2 us
    ppermute x3, starting transfers between devices, local(): below.append(lax.ppermute(below[-1], 'seq', upward))  15.2 us
    pallas_call x1, Pallas kernels, expert_grad(): pl.pallas_call(expert_grad_kernel, grid=(n_z,), out_shape=jax.ShapeDtypeS...  10.9 us
  transfers between devices with their start and end apart: 52, of which 25 were waited for; matrix products, arithmetic and copies ran while one was open for 15% of the time, Pallas kernels for 28%

profile of v4, /device:TPU:0, one launch (start us, length us, event | category | flops | bytes accessed | tf_op | source)
XLA Modules:
  0.0 397.2 jit_solution(17740237309915829517)
XLA Ops:
  12.5 3.1 collective-permute-start.2
  19.5 4.6 %collective-permute-start.6 = (bf16[256,768]{1,0:T(8,128)(2,1)S(1)}, bf16[256,768]{1,0:T(8,128)(2,1)S(1)}, u32[]{:S(2)}, u32[]{:S(2)}) collective-permute-start(bf16[256,768]{1,0:T(8,128)(2,1)S(1)} %bitcast.134), channel_id=1, source_target_pairs={{0,2},{1,3},{2,4},{3,5},{4,6},{5,7},{8,10},{9,11},{10,12},{11,13},... | collective-permute-start | bytes 1179656 | tf_op jit(solution)/shard_map/ppermute | solution.py:485
  26.8 4.7 %collective-permute-done.3 = bf16[4,24,1408]{2,1,0:T(8,128)(2,1)S(1)} collective-permute-done((bf16[4,24,1408]{2,1,0:T(8,128)(2,1)S(1)}, bf16[4,24,1408]{2,1,0:T(8,128)(2,1)S(1)}, u32[]{:S(2)}, u32[]{:S(2)}) %collective-permute-start.3) | collective-permute-done | bytes 270368 | tf_op jit(solution)/shard_map/ppermute | solution.py:36
  34.6 5.3 %collective-permute-start.8 = (bf16[256,768]{1,0:T(8,128)(2,1)S(1)}, bf16[256,768]{1,0:T(8,128)(2,1)}, u32[]{:S(2)}, u32[]{:S(2)}) collective-permute-start(bf16[256,768]{1,0:T(8,128)(2,1)S(1)} %collective-permute-done.6), channel_id=1, source_target_pairs={{0,2},{1,3},{2,4},{3,5},{4,6},{5,7},{8,10},{9,11},{10,12},{11,13},... | collective-permute-start | bytes 1179656 | tf_op jit(solution)/shard_map/ppermute | solution.py:485
  45.6 5.3 %collective-permute-start.10 = (bf16[256,768]{1,0:T(8,128)(2,1)}, bf16[256,768]{1,0:T(8,128)(2,1)}, u32[]{:S(2)}, u32[]{:S(2)}) collective-permute-start(bf16[256,768]{1,0:T(8,128)(2,1)} %collective-permute-done.8), channel_id=1, source_target_pairs={{0,2},{1,3},{2,4},{3,5},{4,6},{5,7},{8,10},{9,11},{10,12},{11,13},... | collective-permute-start | bytes 1179656 | tf_op jit(solution)/shard_map/ppermute | solution.py:485
  68.9 12.7 %attn_fwd.2.refs_1_ = f32[3,1024,128]{2,1,0:T(8,128)} custom-call(s32[2]{0:T(128)} %pad_add_fusion.1.pos_ref, f32[8,4096]{1,0:T(8,128)} %fusion.44.vec_ref, bf16[1024,192]{1,0:T(8,128)(2,1)} %convolution_convert_fusion.3.q_ref, bf16[1024,384]{1,0:T(8,128)(2,1)} %copy-done.34), custom_call_target="tpu_custom_call" | custom-call | flops 15728640000 | bytes 49152000 | tf_op jit(solution)/shard_map/attn_fwd/pallas_call | solution.py:252
  81.5 3.7 collective-permute-done.12.refs_0_.refs_2_
  86.1 14.5 %attn_fwd.3 = (bf16[1024,192]{1,0:T(8,128)(2,1)}, f32[3,1024,128]{2,1,0:T(8,128)}) custom-call(s32[2]{0:T(128)} %pad_add_fusion.1.pos_ref, f32[8,4096]{1,0:T(8,128)} %fusion.44.vec_ref, bf16[1024,192]{1,0:T(8,128)(2,1)} %convolution_convert_fusion.3.q_ref, bf16[1024,384]{1,0:T(8,128)(2,1)} %copy-done.35, f32[3,1024,128]{2,1,0:T(8,128)} %attn_fwd.2.refs_1_), custom_call_target="tpu_custom_call" | custom-call | flops 15728640000 | bytes 49152000 | tf_op jit(solution)/shard_map/attn_fwd/pallas_call | solution.py:252
  103.2 3.4 collective-permute-start.17
  109.0 8.5 %collective-permute-done.18 = bf16[256,192]{1,0:T(8,128)(2,1)S(1)} collective-permute-done((bf16[256,192]{1,0:T(8,128)(2,1)}, bf16[256,192]{1,0:T(8,128)(2,1)S(1)}, u32[]{:S(2)}, u32[]{:S(2)}) %collective-permute-start.18) | collective-permute-done | bytes 98336 | tf_op jit(solution)/shard_map/ppermute | solution.py:36
  119.1 4.9 %collective-permute-done.17 = bf16[256,192]{1,0:T(8,128)(2,1)S(1)} collective-permute-done((bf16[256,192]{1,0:T(8,128)(2,1)}, bf16[256,192]{1,0:T(8,128)(2,1)S(1)}, u32[]{:S(2)}, u32[]{:S(2)}) %collective-permute-start.17) | collective-permute-done | bytes 98336 | tf_op jit(solution)/shard_map/ppermute | solution.py:36
  134.2 2.8 collective-permute-done.21
  137.7 4.8 %collective-permute-done.20 = bf16[128,896]{1,0:T(8,128)(2,1)S(1)} collective-permute-done((bf16[128,896]{1,0:T(8,128)(2,1)S(1)}, bf16[128,896]{1,0:T(8,128)(2,1)S(1)}, u32[]{:S(2)}, u32[]{:S(2)}) %collective-permute-start.20) | collective-permute-done | bytes 229408 | tf_op jit(solution)/shard_map/ppermute | solution.py:36
  147.3 3.7 collective-permute-done.28
  151.0 4.4 %collective-permute-done.27 = bf16[128,896]{1,0:T(8,128)(2,1)S(1)} collective-permute-done((bf16[128,896]{1,0:T(8,128)(2,1)S(1)}, bf16[128,896]{1,0:T(8,128)(2,1)S(1)}, u32[]{:S(2)}, u32[]{:S(2)}) %collective-permute-start.27) | collective-permute-done | bytes 229408 | tf_op jit(solution)/shard_map/ppermute | solution.py:36
  156.6 4.2 %all-gather.3.cloned.1.call-done = bf16[8,768,384]{2,1,0:T(8,128)(2,1)} async-done(((bf16[2,768,384]{2,1,0:T(8,128)(2,1)}), bf16[8,768,384]{2,1,0:T(8,128)(2,1)}) %all-gather.3.cloned.1.call-update) | async-done | bytes 4718608 | tf_op jit(solution)/shard_map/all_gather | solution.py:551
  160.8 8.6 %expert_fwd.1 = (bf16[512,768]{1,0:T(8,128)(2,1)}, bf16[4,512,384]{2,1,0:T(8,128)(2,1)}, bf16[4,512,384]{2,1,0:T(8,128)(2,1)}) custom-call(bf16[512,896]{1,0:T(8,128)(2,1)} %copy-done.14, bf16[4,2,768,384]{3,2,1,0:T(8,128)(2,1)} %bitcast.170), custom_call_target="tpu_custom_call" | custom-call | flops 7247757312 | bytes 22649240 | tf_op jit(solution)/shard_map/expert_fwd/pallas_call | solution.py:362
  173.3 8.1 %expert_bwd.1 = (bf16[512,768]{1,0:T(8,128)(2,1)}, bf16[4,512,384]{2,1,0:T(8,128)(2,1)}) custom-call(bf16[512,768]{1,0:T(8,128)(2,1)} %multiply_convert_fusion.2.dy_ref.dy_other, bf16[4,512,384]{2,1,0:T(8,128)(2,1)} %get-tuple-element.64.slope_ref, bf16[4,2,768,384]{3,2,1,0:T(8,128)(2,1)} %bitcast.171), custom_call_target="tpu_custom_call" | custom-call | flops 7247757312 | bytes 22649240 | tf_op jit(solution)/shard_map/expert_bwd/pallas_call | solution.py:362
  181.9 8.1 %collective-permute-done.30 = bf16[512,768]{1,0:T(8,128)(2,1)S(1)} collective-permute-done((bf16[512,768]{1,0:T(8,128)(2,1)}, bf16[512,768]{1,0:T(8,128)(2,1)S(1)}, u32[]{:S(2)}, u32[]{:S(2)}) %collective-permute-start.30) | collective-permute-done | bytes 786464 | tf_op jit(solution)/shard_map/ppermute | solution.py:36
  190.1 15.4 %expert_own.1 = (f32[512,768]{1,0:T(8,128)}, f32[512,768]{1,0:T(8,128)}, bf16[4,512,384]{2,1,0:T(8,128)(2,1)}, bf16[4,512,384]{2,1,0:T(8,128)(2,1)}) custom-call(bf16[512,896]{1,0:T(8,128)(2,1)} %copy-done.13, bf16[512,768]{1,0:T(8,128)(2,1)} %multiply_convert_fusion.1.dy_ref, bf16[4,2,768,384]{3,2,1,0:T(8,128)(2,1)} %bitcast.172), custom_call_target="tpu_custom_call" | custom-call | flops 14495514624 | bytes 45298484 | tf_op jit(solution)/shard_map/expert_own/pallas_call | solution.py:362
  215.0 10.9 %expert_grad.1 = bf16[4,2,768,384]{3,2,1,0:T(8,128)(2,1)} custom-call(bf16[512,896]{1,0:T(8,128)(2,1)} %copy-done.13, bf16[512,896]{1,0:T(8,128)(2,1)} %copy-done.14, bf16[512,768]{1,0:T(8,128)(2,1)} %multiply_convert_fusion.1.dy_ref, bf16[512,768]{1,0:T(8,128)(2,1)} %multiply_convert_fusion.2.dy_ref.dy_other, ...), custom_call_target="tpu_custom_call" | custom-call | flops 24159191040 | bytes 75497472 | tf_op jit(solution)/shard_map/expert_grad/pallas_call | solution.py:386
  238.6 9.0 %collective-permute-done.38 = bf16[256,192]{1,0:T(8,128)(2,1)S(1)} collective-permute-done((bf16[256,192]{1,0:T(8,128)(2,1)S(1)}, bf16[256,192]{1,0:T(8,128)(2,1)S(1)}, u32[]{:S(2)}, u32[]{:S(2)}) %collective-permute-start.38) | collective-permute-done | bytes 98336 | tf_op jit(solution)/shard_map/ppermute | solution.py:36
  249.8 6.3 %collective-permute-done.40 = bf16[256,192]{1,0:T(8,128)(2,1)S(1)} collective-permute-done((bf16[256,192]{1,0:T(8,128)(2,1)S(1)}, bf16[256,192]{1,0:T(8,128)(2,1)S(1)}, u32[]{:S(2)}, u32[]{:S(2)}) %collective-permute-start.40) | collective-permute-done | bytes 98336 | tf_op jit(solution)/shard_map/ppermute | solution.py:36
  257.1 20.5 %attn_bwd.2 = (f32[3,1024,64]{2,1,0:T(8,128)}, f32[8,4096]{1,0:T(8,128)}, bf16[1024,384]{1,0:T(8,128)(2,1)}) custom-call(s32[2]{0:T(128)} %pad_add_fusion.1.pos_ref, f32[8,4096]{1,0:T(8,128)} %fusion.44.vec_ref, bf16[1024,192]{1,0:T(8,128)(2,1)} %convolution_convert_fusion.3.q_ref, bf16[1024,192]{1,0:T(8,128)(2,1)} %pad_maximum_fusion.8.refs_0_, ...), custom_call_target="tpu_custom_call" | custom-call | flops 23592960000 | bytes 73728000 | tf_op jit(solution)/shard_map/attn_bwd/pallas_call | solution.py:294
  279.2 22.6 %attn_bwd.3 = (bf16[1024,192]{1,0:T(8,128)(2,1)}, f32[8,4096]{1,0:T(8,128)}, f32[1024,384]{1,0:T(8,128)}) custom-call(s32[2]{0:T(128)} %pad_add_fusion.1.pos_ref, f32[8,4096]{1,0:T(8,128)} %fusion.44.vec_ref, bf16[1024,192]{1,0:T(8,128)(2,1)} %convolution_convert_fusion.3.q_ref, bf16[1024,192]{1,0:T(8,128)(2,1)} %pad_maximum_fusion.8.refs_0_, ...), custom_call_target="tpu_custom_call" | custom-call | flops 23592960000 | bytes 73728000 | tf_op jit(solution)/shard_map/attn_bwd/pallas_call | solution.py:294
  313.8 5.2 %weight_grad.1 = bf16[768,1408]{1,0:T(8,128)(2,1)} custom-call(bf16[1024,768]{1,0:T(8,128)(2,1)} %copy-done.11, bf16[1024,576]{1,0:T(8,128)(2,1)} %pad_maximum_fusion.grad_ref, bf16[256,768]{1,0:T(8,128)(2,1)} %copy-done.23, bf16[256,768]{1,0:T(8,128)(2,1)} %copy-done.21, f32[768,64]{1,0:T(8,128)} %pad.29.small_ref), custom_call_target="tpu_custom_call" | custom-call | flops 8858370048 | bytes 27682406 | tf_op jit(solution)/shard_map/weight_grad/pallas_call | solution.py:410
  328.0 9.6 %collective-permute-start.42 = (bf16[512,768]{1,0:T(8,128)(2,1)}, bf16[512,768]{1,0:T(8,128)(2,1)}, u32[]{:S(2)}, u32[]{:S(2)}) collective-permute-start(bf16[512,768]{1,0:T(8,128)(2,1)} %get-tuple-element.180), channel_id=1, source_target_pairs={{0,2},{1,3},{2,0},{3,1},{4,6},{5,7},{6,4},{7,5},{8,10},{9,11},{10,... | collective-permute-start | bytes 2359304 | tf_op jit(solution)/shard_map/ppermute | solution.py:36
  338.3 3.1 collective-permute-done.44
  342.7 12.8 %collective-permute-done.42 = bf16[512,768]{1,0:T(8,128)(2,1)} collective-permute-done((bf16[512,768]{1,0:T(8,128)(2,1)}, bf16[512,768]{1,0:T(8,128)(2,1)}, u32[]{:S(2)}, u32[]{:S(2)}) %collective-permute-start.42) | collective-permute-done | bytes 786464 | tf_op jit(solution)/shard_map/ppermute | solution.py:36
  358.1 3.7 collective-permute-start.45
  363.4 3.6 collective-permute-start.48
  371.4 11.6 %collective-permute-done.48 = bf16[24,1408]{1,0:T(8,128)(2,1)S(1)} collective-permute-done((bf16[24,1408]{1,0:T(8,128)(2,1)S(1)}, bf16[24,1408]{1,0:T(8,128)(2,1)S(1)}, u32[]{:S(2)}, u32[]{:S(2)}) %collective-permute-start.48) | collective-permute-done | bytes 67616 | tf_op jit(solution)/shard_map/ppermute | solution.py:36
  (288 shorter events, 132.1 us)
Async XLA Ops:
  7.2 153.6 %all-gather.3.cloned.1.call-start = ((), (), s32[]{:S(2)}) async-start(), calls=%async_computation.2 | async-start | bytes 5898240 | tf_op jit(solution)/shard_map/all_gather | solution.py:551
  18.2 15.1 %collective-permute-start.7 = (bf16[256,768]{1,0:T(8,128)(2,1)S(1)}, bf16[256,768]{1,0:T(8,128)(2,1)S(1)}, u32[]{:S(2)}, u32[]{:S(2)}) collective-permute-start(bf16[256,768]{1,0:T(8,128)(2,1)S(1)} %bitcast.133), channel_id=1, source_target_pairs={{2,0},{3,1},{4,2},{5,3},{6,4},{7,5},{10,8},{11,9},{12,10},{13,11},... | collective-permute-start | bytes 1179656 | tf_op jit(solution)/shard_map/ppermute | solution.py:486
  19.5 15.1 %collective-permute-start.6 = (bf16[256,768]{1,0:T(8,128)(2,1)S(1)}, bf16[256,768]{1,0:T(8,128)(2,1)S(1)}, u32[]{:S(2)}, u32[]{:S(2)}) collective-permute-start(bf16[256,768]{1,0:T(8,128)(2,1)S(1)} %bitcast.134), channel_id=1, source_target_pairs={{0,2},{1,3},{2,4},{3,5},{4,6},{5,7},{8,10},{9,11},{10,12},{11,13},... | collective-permute-start | bytes 1179656 | tf_op jit(solution)/shard_map/ppermute | solution.py:485
  31.7 19.2 %collective-permute-start.4 = (bf16[2,4,24,1408]{3,2,0,1:T(8,128)(2,1)S(1)}, bf16[2,4,24,1408]{3,2,0,1:T(8,128)(2,1)}, u32[]{:S(2)}, u32[]{:S(2)}) collective-permute-start(bf16[2,4,24,1408]{3,2,0,1:T(8,128)(2,1)S(1)} %pad_maximum_fusion.7), channel_id=1, source_target_pairs={{0,16},{8,24},{16,0},{24,8},{1,17},{9,25},{17,1},{25,9},{2,18},{10... | collective-permute-start | bytes 1622024 | tf_op jit(solution)/shard_map/ppermute | solution.py:36
  41.2 40.4 %collective-permute-start.15 = (bf16[128,768]{1,0:T(8,128)(2,1)}, bf16[128,768]{1,0:T(8,128)(2,1)}, u32[]{:S(2)}, u32[]{:S(2)}) collective-permute-start(bf16[128,768]{1,0:T(8,128)(2,1)} %get-tuple-element.208), channel_id=1, source_target_pairs={{0,24},{8,16},{16,8},{24,0},{1,25},{9,17},{17,9},{25,1},{2,26},{10... | collective-permute-start | bytes 589832 | tf_op jit(solution)/shard_map/ppermute | solution.py:36
  41.2 40.4 %collective-permute-start.14 = (bf16[128,768]{1,0:T(8,128)(2,1)}, bf16[128,768]{1,0:T(8,128)(2,1)}, u32[]{:S(2)}, u32[]{:S(2)}) collective-permute-start(bf16[128,768]{1,0:T(8,128)(2,1)} %get-tuple-element.209), channel_id=1, source_target_pairs={{0,16},{8,24},{16,0},{24,8},{1,17},{9,25},{17,1},{25,9},{2,18},{10... | collective-permute-start | bytes 589832 | tf_op jit(solution)/shard_map/ppermute | solution.py:36
  56.3 25.2 %collective-permute-start.13 = (bf16[128,768]{1,0:T(8,128)(2,1)}, bf16[128,768]{1,0:T(8,128)(2,1)}, u32[]{:S(2)}, u32[]{:S(2)}) collective-permute-start(bf16[128,768]{1,0:T(8,128)(2,1)} %get-tuple-element.210), channel_id=1, source_target_pairs={{0,8},{8,0},{16,24},{24,16},{1,9},{9,1},{17,25},{25,17},{2,10},{10... | collective-permute-start | bytes 589832 | tf_op jit(solution)/shard_map/ppermute | solution.py:36
  59.2 304.2 %reduce-scatter.2.cloned.1.call-start = ((), (), s32[]{:S(2)}) async-start(), calls=%async_computation.1 | async-start | bytes 5898240 | tf_op jit(solution)/shard_map/reduce_scatter | solution.py:613
  66.5 18.8 %collective-permute-start.12 = (bf16[1024,384]{1,0:T(8,128)(2,1)S(1)}, bf16[1024,384]{1,0:T(8,128)(2,1)S(1)}, u32[]{:S(2)}, u32[]{:S(2)}) collective-permute-start(bf16[1024,384]{1,0:T(8,128)(2,1)S(1)} %convolution_convert_fusion.1.refs_0_.refs_2_), channel_id=1, source_target_pairs={{0,1},{1,0},{2,3},{3,2},{4,5},{5,4},{6,7},{7,6},{8,9},{9,8},{10,11... | collective-permute-start | bytes 2359304 | tf_op jit(solution)/shard_map/ppermute | solution.py:36
  102.6 15.0 %collective-permute-start.18 = (bf16[256,192]{1,0:T(8,128)(2,1)}, bf16[256,192]{1,0:T(8,128)(2,1)S(1)}, u32[]{:S(2)}, u32[]{:S(2)}) collective-permute-start(bf16[256,192]{1,0:T(8,128)(2,1)} %get-tuple-element.214), channel_id=1, source_target_pairs={{0,2},{1,3},{2,0},{3,1},{4,6},{5,7},{6,4},{7,5},{8,10},{9,11},{10,... | collective-permute-start | bytes 294920 | tf_op jit(solution)/shard_map/ppermute | solution.py:36
  103.2 20.8 %collective-permute-start.17 = (bf16[256,192]{1,0:T(8,128)(2,1)}, bf16[256,192]{1,0:T(8,128)(2,1)S(1)}, u32[]{:S(2)}, u32[]{:S(2)}) collective-permute-start(bf16[256,192]{1,0:T(8,128)(2,1)} %get-tuple-element.215), channel_id=1, source_target_pairs={{0,4},{1,5},{2,6},{3,7},{4,0},{5,1},{6,2},{7,3},{8,12},{9,13},{10,... | collective-permute-start | bytes 294920 | tf_op jit(solution)/shard_map/ppermute | solution.py:36
  106.6 18.9 %collective-permute-start.16 = (bf16[256,192]{1,0:T(8,128)(2,1)S(1)}, bf16[256,192]{1,0:T(8,128)(2,1)}, u32[]{:S(2)}, u32[]{:S(2)}) collective-permute-start(bf16[256,192]{1,0:T(8,128)(2,1)S(1)} %get-tuple-element.216), channel_id=1, source_target_pairs={{0,6},{1,7},{2,4},{3,5},{4,2},{5,3},{6,0},{7,1},{8,14},{9,15},{10,... | collective-permute-start | bytes 294920 | tf_op jit(solution)/shard_map/ppermute | solution.py:36
  107.0 27.2 %collective-permute-start.22 = (bf16[128,768]{1,0:T(8,128)(2,1)}, bf16[128,768]{1,0:T(8,128)(2,1)}, u32[]{:S(2)}, u32[]{:S(2)}) collective-permute-start(bf16[128,768]{1,0:T(8,128)(2,1)} %get-tuple-element.54), channel_id=1, source_target_pairs={{0,1},{1,0},{2,3},{3,2},{4,5},{5,4},{6,7},{7,6},{8,9},{9,8},{10,11... | collective-permute-start | bytes 589832 | tf_op jit(solution)/shard_map/ppermute | solution.py:36
  108.5 21.2 %collective-permute-start.23 = (bf16[128,768]{1,0:T(8,128)(2,1)}, bf16[128,768]{1,0:T(8,128)(2,1)}, u32[]{:S(2)}, u32[]{:S(2)}) collective-permute-start(bf16[128,768]{1,0:T(8,128)(2,1)} %collective-permute-done.13), channel_id=1, source_target_pairs={{0,1},{1,0},{2,3},{3,2},{4,5},{5,4},{6,7},{7,6},{8,9},{9,8},{10,11... | collective-permute-start | bytes 589832 | tf_op jit(solution)/shard_map/ppermute | solution.py:36
  117.6 14.2 %collective-permute-start.24 = (bf16[128,768]{1,0:T(8,128)(2,1)}, bf16[128,768]{1,0:T(8,128)(2,1)}, u32[]{:S(2)}, u32[]{:S(2)}) collective-permute-start(bf16[128,768]{1,0:T(8,128)(2,1)} %collective-permute-done.14), channel_id=1, source_target_pairs={{0,1},{1,0},{2,3},{3,2},{4,5},{5,4},{6,7},{7,6},{8,9},{9,8},{10,11... | collective-permute-start | bytes 589832 | tf_op jit(solution)/shard_map/ppermute | solution.py:36
  129.7 12.8 %collective-permute-start.20 = (bf16[128,896]{1,0:T(8,128)(2,1)S(1)}, bf16[128,896]{1,0:T(8,128)(2,1)S(1)}, u32[]{:S(2)}, u32[]{:S(2)}) collective-permute-start(bf16[128,896]{1,0:T(8,128)(2,1)S(1)} %get-tuple-element.193), channel_id=1, source_target_pairs={{0,16},{8,24},{16,0},{24,8},{1,17},{9,25},{17,1},{25,9},{2,18},{10... | collective-permute-start | bytes 688136 | tf_op jit(solution)/shard_map/ppermute | solution.py:36
  169.5 20.6 %collective-permute-start.30 = (bf16[512,768]{1,0:T(8,128)(2,1)}, bf16[512,768]{1,0:T(8,128)(2,1)S(1)}, u32[]{:S(2)}, u32[]{:S(2)}) collective-permute-start(bf16[512,768]{1,0:T(8,128)(2,1)} %get-tuple-element.66), channel_id=1, source_target_pairs={{0,1},{1,0},{2,3},{3,2},{4,5},{5,4},{6,7},{7,6},{8,9},{9,8},{10,11... | collective-permute-start | bytes 2359304 | tf_op jit(solution)/shard_map/ppermute | solution.py:36
  181.4 24.5 %collective-permute-start.34 = (bf16[512,768]{1,0:T(8,128)(2,1)}, bf16[512,768]{1,0:T(8,128)(2,1)S(1)}, u32[]{:S(2)}, u32[]{:S(2)}) collective-permute-start(bf16[512,768]{1,0:T(8,128)(2,1)} %get-tuple-element.65), channel_id=1, source_target_pairs={{0,1},{1,0},{2,3},{3,2},{4,5},{5,4},{6,7},{7,6},{8,9},{9,8},{10,11... | collective-permute-start | bytes 2359304 | tf_op jit(solution)/shard_map/ppermute | solution.py:36
  210.8 16.0 %collective-permute-start.33 = (bf16[128,768]{1,0:T(8,128)(2,1)}, bf16[128,768]{1,0:T(8,128)(2,1)}, u32[]{:S(2)}, u32[]{:S(2)}) collective-permute-start(bf16[128,768]{1,0:T(8,128)(2,1)} %get-tuple-element.205), channel_id=1, source_target_pairs={{0,24},{8,16},{16,8},{24,0},{1,25},{9,17},{17,9},{25,1},{2,26},{10... | collective-permute-start | bytes 589832 | tf_op jit(solution)/shard_map/ppermute | solution.py:36
  210.8 16.0 %collective-permute-start.32 = (bf16[128,768]{1,0:T(8,128)(2,1)}, bf16[128,768]{1,0:T(8,128)(2,1)}, u32[]{:S(2)}, u32[]{:S(2)}) collective-permute-start(bf16[128,768]{1,0:T(8,128)(2,1)} %get-tuple-element.206), channel_id=1, source_target_pairs={{0,16},{8,24},{16,0},{24,8},{1,17},{9,25},{17,1},{25,9},{2,18},{10... | collective-permute-start | bytes 589832 | tf_op jit(solution)/shard_map/ppermute | solution.py:36
  211.5 15.2 %collective-permute-start.31 = (bf16[128,768]{1,0:T(8,128)(2,1)}, bf16[128,768]{1,0:T(8,128)(2,1)}, u32[]{:S(2)}, u32[]{:S(2)}) collective-permute-start(bf16[128,768]{1,0:T(8,128)(2,1)} %get-tuple-element.207), channel_id=1, source_target_pairs={{0,8},{8,0},{16,24},{24,16},{1,9},{9,1},{17,25},{25,17},{2,10},{10... | collective-permute-start | bytes 589832 | tf_op jit(solution)/shard_map/ppermute | solution.py:36
  212.6 13.3 %collective-permute-start.35 = (bf16[128,768]{1,0:T(8,128)(2,1)}, bf16[128,768]{1,0:T(8,128)(2,1)}, u32[]{:S(2)}, u32[]{:S(2)}) collective-permute-start(bf16[128,768]{1,0:T(8,128)(2,1)} %get-tuple-element.202), channel_id=1, source_target_pairs={{0,8},{8,0},{16,24},{24,16},{1,9},{9,1},{17,25},{25,17},{2,10},{10... | collective-permute-start | bytes 589832 | tf_op jit(solution)/shard_map/ppermute | solution.py:36
  233.0 14.7 %collective-permute-start.38 = (bf16[256,192]{1,0:T(8,128)(2,1)S(1)}, bf16[256,192]{1,0:T(8,128)(2,1)S(1)}, u32[]{:S(2)}, u32[]{:S(2)}) collective-permute-start(bf16[256,192]{1,0:T(8,128)(2,1)S(1)} %get-tuple-element.218), channel_id=1, source_target_pairs={{0,2},{1,3},{2,0},{3,1},{4,6},{5,7},{6,4},{7,5},{8,10},{9,11},{10,... | collective-permute-start | bytes 294920 | tf_op jit(solution)/shard_map/ppermute | solution.py:36
  235.4 14.4 %collective-permute-start.39 = (bf16[256,192]{1,0:T(8,128)(2,1)S(1)}, bf16[256,192]{1,0:T(8,128)(2,1)S(1)}, u32[]{:S(2)}, u32[]{:S(2)}) collective-permute-start(bf16[256,192]{1,0:T(8,128)(2,1)S(1)} %get-tuple-element.219), channel_id=1, source_target_pairs={{0,4},{1,5},{2,6},{3,7},{4,0},{5,1},{6,2},{7,3},{8,12},{9,13},{10,... | collective-permute-start | bytes 294920 | tf_op jit(solution)/shard_map/ppermute | solution.py:36
  236.9 19.3 %collective-permute-start.40 = (bf16[256,192]{1,0:T(8,128)(2,1)S(1)}, bf16[256,192]{1,0:T(8,128)(2,1)S(1)}, u32[]{:S(2)}, u32[]{:S(2)}) collective-permute-start(bf16[256,192]{1,0:T(8,128)(2,1)S(1)} %get-tuple-element.220), channel_id=1, source_target_pairs={{0,6},{1,7},{2,4},{3,5},{4,2},{5,3},{6,0},{7,1},{8,14},{9,15},{10,... | collective-permute-start | bytes 294920 | tf_op jit(solution)/shard_map/ppermute | solution.py:36
  277.5 26.6 %collective-permute-start.41 = (bf16[1024,384]{1,0:T(8,128)(2,1)}, bf16[1024,384]{1,0:T(8,128)(2,1)}, u32[]{:S(2)}, u32[]{:S(2)}) collective-permute-start(bf16[1024,384]{1,0:T(8,128)(2,1)} %get-tuple-element.84), channel_id=1, source_target_pairs={{0,1},{1,0},{2,3},{3,2},{4,5},{5,4},{6,7},{7,6},{8,9},{9,8},{10,11... | collective-permute-start | bytes 2359304 | tf_op jit(solution)/shard_map/ppermute | solution.py:36
  326.5 14.9 %collective-permute-start.44 = (bf16[4,2,24,1408]{3,2,0,1:T(8,128)(2,1)}, bf16[4,2,24,1408]{3,2,0,1:T(8,128)(2,1)}, u32[]{:S(2)}, u32[]{:S(2)}) collective-permute-start(bf16[4,2,24,1408]{3,2,0,1:T(8,128)(2,1)} %select_bitcast_fusion.3), channel_id=1, source_target_pairs={{0,16},{8,24},{16,0},{24,8},{1,17},{9,25},{17,1},{25,9},{2,18},{10... | collective-permute-start | bytes 1622024 | tf_op jit(solution)/shard_map/ppermute | solution.py:36
  328.0 27.5 %collective-permute-start.42 = (bf16[512,768]{1,0:T(8,128)(2,1)}, bf16[512,768]{1,0:T(8,128)(2,1)}, u32[]{:S(2)}, u32[]{:S(2)}) collective-permute-start(bf16[512,768]{1,0:T(8,128)(2,1)} %get-tuple-element.180), channel_id=1, source_target_pairs={{0,2},{1,3},{2,0},{3,1},{4,6},{5,7},{6,4},{7,5},{8,10},{9,11},{10,... | collective-permute-start | bytes 2359304 | tf_op jit(solution)/shard_map/ppermute | solution.py:36
  358.1 27.8 %collective-permute-start.45 = (bf16[256,768]{1,0:T(8,128)(2,1)}, bf16[256,768]{1,0:T(8,128)(2,1)S(1)}, u32[]{:S(2)}, u32[]{:S(2)}) collective-permute-start(bf16[256,768]{1,0:T(8,128)(2,1)} %slice.654), channel_id=1, source_target_pairs={{0,4},{1,5},{2,6},{3,7},{4,0},{5,1},{6,2},{7,3},{8,12},{9,13},{10,... | collective-permute-start | bytes 1179656 | tf_op jit(solution)/shard_map/ppermute | solution.py:36
  363.4 19.5 %collective-permute-start.48 = (bf16[24,1408]{1,0:T(8,128)(2,1)S(1)}, bf16[24,1408]{1,0:T(8,128)(2,1)S(1)}, u32[]{:S(2)}, u32[]{:S(2)}) collective-permute-start(bf16[24,1408]{1,0:T(8,128)(2,1)S(1)} %get-tuple-element.156), channel_id=1, source_target_pairs={{0,4},{1,5},{2,6},{3,7},{4,0},{5,1},{6,2},{7,3},{8,12},{9,13},{10,... | collective-permute-start | bytes 202760 | tf_op jit(solution)/shard_map/ppermute | solution.py:36
  367.0 15.9 %collective-permute-start.49 = (bf16[24,1408]{1,0:T(8,128)(2,1)S(1)}, bf16[24,1408]{1,0:T(8,128)(2,1)S(1)}, u32[]{:S(2)}, u32[]{:S(2)}) collective-permute-start(bf16[24,1408]{1,0:T(8,128)(2,1)S(1)} %get-tuple-element.226), channel_id=1, source_target_pairs={{0,2},{1,3},{2,0},{3,1},{4,6},{5,7},{6,4},{7,5},{8,10},{9,11},{10,... | collective-permute-start | bytes 202760 | tf_op jit(solution)/shard_map/ppermute | solution.py:36
  367.6 15.3 %collective-permute-start.47 = (bf16[24,1408]{1,0:T(8,128)(2,1)S(1)}, bf16[24,1408]{1,0:T(8,128)(2,1)S(1)}, u32[]{:S(2)}, u32[]{:S(2)}) collective-permute-start(bf16[24,1408]{1,0:T(8,128)(2,1)S(1)} %get-tuple-element.227), channel_id=1, source_target_pairs={{0,6},{1,7},{2,4},{3,5},{4,2},{5,3},{6,0},{7,1},{8,14},{9,15},{10,... | collective-permute-start | bytes 202760 | tf_op jit(solution)/shard_map/ppermute | solution.py:36
  (58 other events, 474.1 us)
Sparse Core Ops, SparseCore 0:
  59.3 101.5 all-gather.2
  226.0 96.5 reduce-scatter.1

commit v5 on v4

--- a/solution.py
+++ b/solution.py
@@ -396,26 +396,28 @@
     )(*rows, *kept)
 
 
-def weight_grad_kernel(a_ref, grad_ref, out_grad_ref, context_ref, small_ref, out_ref):
-    cut = grad_ref.shape[1]
+def weight_grad_kernel(a_ref, q_ref, kv_ref, out_grad_ref, context_ref, small_ref, out_ref):
+    part = q_ref.shape[1]
+    cut = part + kv_ref.shape[1]
     wide = cut + small_ref.shape[1]
-    out_ref[:, :cut] = dot_tn(a_ref[...], grad_ref[...]).astype(bf16)
+    out_ref[:, :part] = dot_tn(a_ref[...], q_ref[...]).astype(bf16)
+    out_ref[:, part:cut] = dot_tn(a_ref[...], kv_ref[...]).astype(bf16)
     out_ref[:, cut:wide] = small_ref[...].astype(bf16)
     out_ref[:, wide:] = dot_tn(out_grad_ref[...], context_ref[...]).astype(bf16)
 
 
-def weight_grad(a, grad, out_grad, context, small):
+def weight_grad(a, grad_q, grad_kv, out_grad, context, small):
     width = a.shape[1]
-    columns = grad.shape[1] + small.shape[1] + context.shape[1]
+    columns = grad_q.shape[1] + grad_kv.shape[1] + small.shape[1] + context.shape[1]
     return pl.pallas_call(
         weight_grad_kernel,
         out_shape=jax.ShapeDtypeStruct((width, columns), bf16),
-        in_specs=vmem_specs(5),
+        in_specs=vmem_specs(6),
         out_specs=vmem_specs(1)[0],
         compiler_params=pltpu.CompilerParams(vmem_limit_bytes=VMEM),
         cost_estimate=effort(4 * 2 * a.shape[0] * width * columns),
         name="weight_grad",
-    )(a, grad, out_grad, context, small)
+    )(a, grad_q, grad_kv, out_grad, context, small)
 
 
 def local(
@@ -645,7 +647,8 @@
     )
     for value in arrived:
         grad_kv = grad_kv + value.astype(f32)
-    grad_qkv = jnp.concatenate([grad_q, grad_kv.astype(bf16)], axis=1)
+    grad_kv = grad_kv.astype(bf16)
+    grad_qkv = jnp.concatenate([grad_q, grad_kv], axis=1)
     odd, even = list(range(1, n_z, 2)), list(range(0, n_z, 2))
 
     def take(value, blocks):
@@ -667,7 +670,7 @@
     small = [grad_gain_a[:, None], grad_gain_f[:, None], grad_router, grad_table]
     small = jnp.concatenate(small, axis=1)
     small = jnp.pad(small, ((0, 0), (0, packed - 3 * part - small.shape[1])))
-    value = weight_grad(normed_all, grad_qkv, grad_attn, context, small)
+    value = weight_grad(normed_all, grad_q, grad_kv, grad_attn, context, small)
     value = value.reshape((2,) * m_bits + (n_z,) + (2,) * n_bits + (w_rows, packed + inner))
     for i, bit in enumerate(dp_bits):
         value = halve(value, m_bits - 1 - i, "dp", bit, (dp & bit) != 0)

time: 404 us -> 405 us (level)
  transfers between devices with their start and end apart: 52 -> 52, of which waited for: 25 -> 25; matrix products, arithmetic and copies ran while one was open for 15% -> 16% of each run, Pallas kernels for 28% -> 28%
where the time goes in v5:
time: 405 us; the launch traced here: 397 us
  Pallas kernels  119 us (29%)
  waiting for transfers between devices  106 us (26%)
  starting transfers between devices  78.9 us (19%)
  other arithmetic  39 us (10%)
  local copies, waits for them, and re-layouts  23.7 us (6%)
  matrix products  15.4 us (4%)
  between operations  15.2 us (4%)
    ppermute x44, waiting for transfers between devices, swap(): return lax.ppermute(value, axis, [(i, i ^ mask) for i in range(size)])  99.4 us
    ppermute x44, starting transfers between devices, swap(): return lax.ppermute(value, axis, [(i, i ^ mask) for i in range(size)])  59.2 us
    pallas_call x2, Pallas kernels, attn_bwd(): pl.pallas_call(partial(attn_bwd_kernel, dims, seq_count, heads, size, key...  43.2 us
    pallas_call x3, Pallas kernels, expert_call(): pl.pallas_call(kernel, grid=(n_z,), out_shape=(jax.ShapeDtypeStruct((coun...  32.3 us
    pallas_call x2, Pallas kernels, attn_fwd(): pl.pallas_call(partial(attn_fwd_kernel, dims, seq_count, heads, size, key...  27.3 us
    ppermute x3, starting transfers between devices, local(): below.append(lax.ppermute(below[-1], 'seq', upward))  15.8 us
    pallas_call x1, Pallas kernels, expert_grad(): pl.pallas_call(expert_grad_kernel, grid=(n_z,), out_shape=jax.ShapeDtypeS...  10.9 us
  transfers between devices with their start and end apart: 52, of which 25 were waited for; matrix products, arithmetic and copies ran while one was open for 16% of the time, Pallas kernels for 28%

profile of v5, /device:TPU:0, one launch (start us, length us, event | category | flops | bytes accessed | tf_op | source)
XLA Modules:
  0.0 397.4 jit_solution(6352900184770234300)
XLA Ops:
  12.5 3.1 collective-permute-start.2
  19.5 5.3 %collective-permute-start.6 = (bf16[256,768]{1,0:T(8,128)(2,1)S(1)}, bf16[256,768]{1,0:T(8,128)(2,1)}, u32[]{:S(2)}, u32[]{:S(2)}) collective-permute-start(bf16[256,768]{1,0:T(8,128)(2,1)S(1)} %bitcast.134), channel_id=1, source_target_pairs={{0,2},{1,3},{2,4},{3,5},{4,6},{5,7},{8,10},{9,11},{10,12},{11,13},... | collective-permute-start | bytes 1179656 | tf_op jit(solution)/shard_map/ppermute | solution.py:487
  27.0 5.1 %collective-permute-done.3 = bf16[4,24,1408]{2,1,0:T(8,128)(2,1)S(1)} collective-permute-done((bf16[4,24,1408]{2,1,0:T(8,128)(2,1)S(1)}, bf16[4,24,1408]{2,1,0:T(8,128)(2,1)S(1)}, u32[]{:S(2)}, u32[]{:S(2)}) %collective-permute-start.3) | collective-permute-done | bytes 270368 | tf_op jit(solution)/shard_map/ppermute | solution.py:36
  35.1 5.3 %collective-permute-start.8 = (bf16[256,768]{1,0:T(8,128)(2,1)}, bf16[256,768]{1,0:T(8,128)(2,1)}, u32[]{:S(2)}, u32[]{:S(2)}) collective-permute-start(bf16[256,768]{1,0:T(8,128)(2,1)} %collective-permute-done.6), channel_id=1, source_target_pairs={{0,2},{1,3},{2,4},{3,5},{4,6},{5,7},{8,10},{9,11},{10,12},{11,13},... | collective-permute-start | bytes 1179656 | tf_op jit(solution)/shard_map/ppermute | solution.py:487
  45.7 5.2 %collective-permute-start.10 = (bf16[256,768]{1,0:T(8,128)(2,1)}, bf16[256,768]{1,0:T(8,128)(2,1)}, u32[]{:S(2)}, u32[]{:S(2)}) collective-permute-start(bf16[256,768]{1,0:T(8,128)(2,1)} %collective-permute-done.8), channel_id=1, source_target_pairs={{0,2},{1,3},{2,4},{3,5},{4,6},{5,7},{8,10},{9,11},{10,12},{11,13},... | collective-permute-start | bytes 1179656 | tf_op jit(solution)/shard_map/ppermute | solution.py:487
  70.1 12.7 %attn_fwd.2.refs_1_ = f32[3,1024,128]{2,1,0:T(8,128)} custom-call(s32[2]{0:T(128)} %pad_add_fusion.1.pos_ref, f32[8,4096]{1,0:T(8,128)} %fusion.51.vec_ref, bf16[1024,192]{1,0:T(8,128)(2,1)} %convolution_convert_fusion.3.q_ref, bf16[1024,384]{1,0:T(8,128)(2,1)} %copy-done.38), custom_call_target="tpu_custom_call" | custom-call | flops 15728640000 | bytes 49152000 | tf_op jit(solution)/shard_map/attn_fwd/pallas_call | solution.py:252
  82.9 3.6 collective-permute-done.12.refs_0_.refs_2_
  87.4 14.5 %attn_fwd.3 = (bf16[1024,192]{1,0:T(8,128)(2,1)}, f32[3,1024,128]{2,1,0:T(8,128)}) custom-call(s32[2]{0:T(128)} %pad_add_fusion.1.pos_ref, f32[8,4096]{1,0:T(8,128)} %fusion.51.vec_ref, bf16[1024,192]{1,0:T(8,128)(2,1)} %convolution_convert_fusion.3.q_ref, bf16[1024,384]{1,0:T(8,128)(2,1)} %copy-done.39, f32[3,1024,128]{2,1,0:T(8,128)} %attn_fwd.2.refs_1_), custom_call_target="tpu_custom_call" | custom-call | flops 15728640000 | bytes 49152000 | tf_op jit(solution)/shard_map/attn_fwd/pallas_call | solution.py:252
  109.6 8.2 %collective-permute-done.18 = bf16[256,192]{1,0:T(8,128)(2,1)S(1)} collective-permute-done((bf16[256,192]{1,0:T(8,128)(2,1)S(1)}, bf16[256,192]{1,0:T(8,128)(2,1)S(1)}, u32[]{:S(2)}, u32[]{:S(2)}) %collective-permute-start.18) | collective-permute-done | bytes 98336 | tf_op jit(solution)/shard_map/ppermute | solution.py:36
  119.4 5.0 %collective-permute-done.17 = bf16[256,192]{1,0:T(8,128)(2,1)S(1)} collective-permute-done((bf16[256,192]{1,0:T(8,128)(2,1)S(1)}, bf16[256,192]{1,0:T(8,128)(2,1)S(1)}, u32[]{:S(2)}, u32[]{:S(2)}) %collective-permute-start.17) | collective-permute-done | bytes 98336 | tf_op jit(solution)/shard_map/ppermute | solution.py:36
  136.6 3.7 collective-permute-done.21
  140.9 4.4 %collective-permute-done.20 = bf16[128,896]{1,0:T(8,128)(2,1)S(1)} collective-permute-done((bf16[128,896]{1,0:T(8,128)(2,1)S(1)}, bf16[128,896]{1,0:T(8,128)(2,1)S(1)}, u32[]{:S(2)}, u32[]{:S(2)}) %collective-permute-start.20) | collective-permute-done | bytes 229408 | tf_op jit(solution)/shard_map/ppermute | solution.py:36
  150.0 3.8 collective-permute-done.28
  153.8 4.3 %collective-permute-done.27 = bf16[128,896]{1,0:T(8,128)(2,1)S(1)} collective-permute-done((bf16[128,896]{1,0:T(8,128)(2,1)S(1)}, bf16[128,896]{1,0:T(8,128)(2,1)S(1)}, u32[]{:S(2)}, u32[]{:S(2)}) %collective-permute-start.27) | collective-permute-done | bytes 229408 | tf_op jit(solution)/shard_map/ppermute | solution.py:36
  160.8 8.6 %expert_fwd.1 = (bf16[512,768]{1,0:T(8,128)(2,1)}, bf16[4,512,384]{2,1,0:T(8,128)(2,1)}, bf16[4,512,384]{2,1,0:T(8,128)(2,1)}) custom-call(bf16[512,896]{1,0:T(8,128)(2,1)} %copy-done.13, bf16[4,2,768,384]{3,2,1,0:T(8,128)(2,1)} %bitcast.170), custom_call_target="tpu_custom_call" | custom-call | flops 7247757312 | bytes 22649240 | tf_op jit(solution)/shard_map/expert_fwd/pallas_call | solution.py:362
  173.3 8.2 %expert_bwd.1 = (bf16[512,768]{1,0:T(8,128)(2,1)}, bf16[4,512,384]{2,1,0:T(8,128)(2,1)}) custom-call(bf16[512,768]{1,0:T(8,128)(2,1)} %multiply_convert_fusion.2.dy_ref.dy_other, bf16[4,512,384]{2,1,0:T(8,128)(2,1)} %get-tuple-element.64.slope_ref, bf16[4,2,768,384]{3,2,1,0:T(8,128)(2,1)} %bitcast.171), custom_call_target="tpu_custom_call" | custom-call | flops 7247757312 | bytes 22649240 | tf_op jit(solution)/shard_map/expert_bwd/pallas_call | solution.py:362
  182.0 8.0 %collective-permute-done.30 = bf16[512,768]{1,0:T(8,128)(2,1)S(1)} collective-permute-done((bf16[512,768]{1,0:T(8,128)(2,1)}, bf16[512,768]{1,0:T(8,128)(2,1)S(1)}, u32[]{:S(2)}, u32[]{:S(2)}) %collective-permute-start.30) | collective-permute-done | bytes 786464 | tf_op jit(solution)/shard_map/ppermute | solution.py:36
  190.0 15.5 %expert_own.1 = (f32[512,768]{1,0:T(8,128)}, f32[512,768]{1,0:T(8,128)}, bf16[4,512,384]{2,1,0:T(8,128)(2,1)}, bf16[4,512,384]{2,1,0:T(8,128)(2,1)}) custom-call(bf16[512,896]{1,0:T(8,128)(2,1)} %copy-done.12, bf16[512,768]{1,0:T(8,128)(2,1)} %multiply_convert_fusion.1.dy_ref, bf16[4,2,768,384]{3,2,1,0:T(8,128)(2,1)} %bitcast.172), custom_call_target="tpu_custom_call" | custom-call | flops 14495514624 | bytes 45298484 | tf_op jit(solution)/shard_map/expert_own/pallas_call | solution.py:362
  214.8 10.9 %expert_grad.1 = bf16[4,2,768,384]{3,2,1,0:T(8,128)(2,1)} custom-call(bf16[512,896]{1,0:T(8,128)(2,1)} %copy-done.12, bf16[512,896]{1,0:T(8,128)(2,1)} %copy-done.13, bf16[512,768]{1,0:T(8,128)(2,1)} %multiply_convert_fusion.1.dy_ref, bf16[512,768]{1,0:T(8,128)(2,1)} %multiply_convert_fusion.2.dy_ref.dy_other, ...), custom_call_target="tpu_custom_call" | custom-call | flops 24159191040 | bytes 75497472 | tf_op jit(solution)/shard_map/expert_grad/pallas_call | solution.py:386
  233.2 5.1 %collective-permute-start.38 = (bf16[256,192]{1,0:T(8,128)(2,1)S(1)}, bf16[256,192]{1,0:T(8,128)(2,1)S(1)}, u32[]{:S(2)}, u32[]{:S(2)}) collective-permute-start(bf16[256,192]{1,0:T(8,128)(2,1)S(1)} %get-tuple-element.217), channel_id=1, source_target_pairs={{0,2},{1,3},{2,0},{3,1},{4,6},{5,7},{6,4},{7,5},{8,10},{9,11},{10,... | collective-permute-start | bytes 294920 | tf_op jit(solution)/shard_map/ppermute | solution.py:36
  241.1 11.6 %collective-permute-done.38 = bf16[256,192]{1,0:T(8,128)(2,1)S(1)} collective-permute-done((bf16[256,192]{1,0:T(8,128)(2,1)S(1)}, bf16[256,192]{1,0:T(8,128)(2,1)S(1)}, u32[]{:S(2)}, u32[]{:S(2)}) %collective-permute-start.38) | collective-permute-done | bytes 98336 | tf_op jit(solution)/shard_map/ppermute | solution.py:36
  252.7 6.2 %collective-permute-done.40 = bf16[256,192]{1,0:T(8,128)(2,1)S(1)} collective-permute-done((bf16[256,192]{1,0:T(8,128)(2,1)S(1)}, bf16[256,192]{1,0:T(8,128)(2,1)S(1)}, u32[]{:S(2)}, u32[]{:S(2)}) %collective-permute-start.40) | collective-permute-done | bytes 98336 | tf_op jit(solution)/shard_map/ppermute | solution.py:36
  259.8 20.6 %attn_bwd.2 = (f32[3,1024,64]{2,1,0:T(8,128)}, f32[8,4096]{1,0:T(8,128)}, bf16[1024,384]{1,0:T(8,128)(2,1)}) custom-call(s32[2]{0:T(128)} %pad_add_fusion.1.pos_ref, f32[8,4096]{1,0:T(8,128)} %fusion.51.vec_ref, bf16[1024,192]{1,0:T(8,128)(2,1)} %convolution_convert_fusion.3.q_ref, bf16[1024,192]{1,0:T(8,128)(2,1)} %pad_maximum_fusion.7.refs_0_, ...), custom_call_target="tpu_custom_call" | custom-call | flops 23592960000 | bytes 73728000 | tf_op jit(solution)/shard_map/attn_bwd/pallas_call | solution.py:294
  281.1 22.6 %attn_bwd.3 = (bf16[1024,192]{1,0:T(8,128)(2,1)}, f32[8,4096]{1,0:T(8,128)}, f32[1024,384]{1,0:T(8,128)}) custom-call(s32[2]{0:T(128)} %pad_add_fusion.1.pos_ref, f32[8,4096]{1,0:T(8,128)} %fusion.51.vec_ref, bf16[1024,192]{1,0:T(8,128)(2,1)} %convolution_convert_fusion.3.q_ref, bf16[1024,192]{1,0:T(8,128)(2,1)} %pad_maximum_fusion.7.refs_0_, ...), custom_call_target="tpu_custom_call" | custom-call | flops 23592960000 | bytes 73728000 | tf_op jit(solution)/shard_map/attn_bwd/pallas_call | solution.py:294
  314.1 5.2 %weight_grad.1 = bf16[768,1408]{1,0:T(8,128)(2,1)} custom-call(bf16[1024,768]{1,0:T(8,128)(2,1)} %copy-done.10, bf16[1024,192]{1,0:T(8,128)(2,1)} %get-tuple-element.82.q_ref, bf16[1024,384]{1,0:T(8,128)(2,1)} %copy-done.5, bf16[256,768]{1,0:T(8,128)(2,1)} %copy-done.22, bf16[256,768]{1,0:T(8,128)(2,1)} %copy-done.21, f32[768,64]{1,0:T(8,128)} %pad.29.small_ref), custom_call_target="tpu_custom_call" | custom-call | flops 8858370048 | bytes 27682406 | tf_op jit(solution)/shard_map/weight_grad/pallas_call | solution.py:412
  321.3 2.8 collective-permute-done.43
  328.3 9.4 %collective-permute-start.42 = (bf16[512,768]{1,0:T(8,128)(2,1)}, bf16[512,768]{1,0:T(8,128)(2,1)}, u32[]{:S(2)}, u32[]{:S(2)}) collective-permute-start(bf16[512,768]{1,0:T(8,128)(2,1)} %get-tuple-element.180), channel_id=1, source_target_pairs={{0,2},{1,3},{2,0},{3,1},{4,6},{5,7},{6,4},{7,5},{8,10},{9,11},{10,... | collective-permute-start | bytes 2359304 | tf_op jit(solution)/shard_map/ppermute | solution.py:36
  338.4 2.8 collective-permute-done.44
  342.5 13.1 %collective-permute-done.42 = bf16[512,768]{1,0:T(8,128)(2,1)} collective-permute-done((bf16[512,768]{1,0:T(8,128)(2,1)}, bf16[512,768]{1,0:T(8,128)(2,1)}, u32[]{:S(2)}, u32[]{:S(2)}) %collective-permute-start.42) | collective-permute-done | bytes 786464 | tf_op jit(solution)/shard_map/ppermute | solution.py:36
  358.2 3.8 collective-permute-start.45
  368.0 2.8 fusion.47
  370.8 12.3 %collective-permute-done.48 = bf16[24,1408]{1,0:T(8,128)(2,1)S(1)} collective-permute-done((bf16[24,1408]{1,0:T(8,128)(2,1)S(1)}, bf16[24,1408]{1,0:T(8,128)(2,1)S(1)}, u32[]{:S(2)}, u32[]{:S(2)}) %collective-permute-start.48) | collective-permute-done | bytes 67616 | tf_op jit(solution)/shard_map/ppermute | solution.py:36
  (295 shorter events, 128.1 us)
Async XLA Ops:
  7.2 153.6 %all-gather.3.cloned.1.call-start = ((), (), s32[]{:S(2)}) async-start(), calls=%async_computation.2 | async-start | bytes 5898240 | tf_op jit(solution)/shard_map/all_gather | solution.py:553
  18.2 15.7 %collective-permute-start.7 = (bf16[256,768]{1,0:T(8,128)(2,1)S(1)}, bf16[256,768]{1,0:T(8,128)(2,1)S(1)}, u32[]{:S(2)}, u32[]{:S(2)}) collective-permute-start(bf16[256,768]{1,0:T(8,128)(2,1)S(1)} %bitcast.133), channel_id=1, source_target_pairs={{2,0},{3,1},{4,2},{5,3},{6,4},{7,5},{10,8},{11,9},{12,10},{13,11},... | collective-permute-start | bytes 1179656 | tf_op jit(solution)/shard_map/ppermute | solution.py:488
  19.5 15.7 %collective-permute-start.6 = (bf16[256,768]{1,0:T(8,128)(2,1)S(1)}, bf16[256,768]{1,0:T(8,128)(2,1)}, u32[]{:S(2)}, u32[]{:S(2)}) collective-permute-start(bf16[256,768]{1,0:T(8,128)(2,1)S(1)} %bitcast.134), channel_id=1, source_target_pairs={{0,2},{1,3},{2,4},{3,5},{4,6},{5,7},{8,10},{9,11},{10,12},{11,13},... | collective-permute-start | bytes 1179656 | tf_op jit(solution)/shard_map/ppermute | solution.py:487
  32.3 18.6 %collective-permute-start.4 = (bf16[2,4,24,1408]{3,2,0,1:T(8,128)(2,1)S(1)}, bf16[2,4,24,1408]{3,2,0,1:T(8,128)(2,1)}, u32[]{:S(2)}, u32[]{:S(2)}) collective-permute-start(bf16[2,4,24,1408]{3,2,0,1:T(8,128)(2,1)S(1)} %pad_maximum_fusion.6), channel_id=1, source_target_pairs={{0,16},{8,24},{16,0},{24,8},{1,17},{9,25},{17,1},{25,9},{2,18},{10... | collective-permute-start | bytes 1622024 | tf_op jit(solution)/shard_map/ppermute | solution.py:36
  41.7 41.2 %collective-permute-start.15 = (bf16[128,768]{1,0:T(8,128)(2,1)}, bf16[128,768]{1,0:T(8,128)(2,1)}, u32[]{:S(2)}, u32[]{:S(2)}) collective-permute-start(bf16[128,768]{1,0:T(8,128)(2,1)} %get-tuple-element.207), channel_id=1, source_target_pairs={{0,24},{8,16},{16,8},{24,0},{1,25},{9,17},{17,9},{25,1},{2,26},{10... | collective-permute-start | bytes 589832 | tf_op jit(solution)/shard_map/ppermute | solution.py:36
  41.7 41.2 %collective-permute-start.14 = (bf16[128,768]{1,0:T(8,128)(2,1)}, bf16[128,768]{1,0:T(8,128)(2,1)}, u32[]{:S(2)}, u32[]{:S(2)}) collective-permute-start(bf16[128,768]{1,0:T(8,128)(2,1)} %get-tuple-element.208), channel_id=1, source_target_pairs={{0,16},{8,24},{16,0},{24,8},{1,17},{9,25},{17,1},{25,9},{2,18},{10... | collective-permute-start | bytes 589832 | tf_op jit(solution)/shard_map/ppermute | solution.py:36
  56.8 26.0 %collective-permute-start.13 = (bf16[128,768]{1,0:T(8,128)(2,1)}, bf16[128,768]{1,0:T(8,128)(2,1)}, u32[]{:S(2)}, u32[]{:S(2)}) collective-permute-start(bf16[128,768]{1,0:T(8,128)(2,1)} %get-tuple-element.209), channel_id=1, source_target_pairs={{0,8},{8,0},{16,24},{24,16},{1,9},{9,1},{17,25},{25,17},{2,10},{10... | collective-permute-start | bytes 589832 | tf_op jit(solution)/shard_map/ppermute | solution.py:36
  59.7 303.8 %reduce-scatter.2.cloned.1.call-start = ((), (), s32[]{:S(2)}) async-start(), calls=%async_computation.1 | async-start | bytes 5898240 | tf_op jit(solution)/shard_map/reduce_scatter | solution.py:615
  67.7 18.8 %collective-permute-start.12 = (bf16[1024,384]{1,0:T(8,128)(2,1)S(1)}, bf16[1024,384]{1,0:T(8,128)(2,1)S(1)}, u32[]{:S(2)}, u32[]{:S(2)}) collective-permute-start(bf16[1024,384]{1,0:T(8,128)(2,1)S(1)} %convolution_convert_fusion.1.refs_0_.refs_2_), channel_id=1, source_target_pairs={{0,1},{1,0},{2,3},{3,2},{4,5},{5,4},{6,7},{7,6},{8,9},{9,8},{10,11... | collective-permute-start | bytes 2359304 | tf_op jit(solution)/shard_map/ppermute | solution.py:36
  103.1 14.7 %collective-permute-start.18 = (bf16[256,192]{1,0:T(8,128)(2,1)S(1)}, bf16[256,192]{1,0:T(8,128)(2,1)S(1)}, u32[]{:S(2)}, u32[]{:S(2)}) collective-permute-start(bf16[256,192]{1,0:T(8,128)(2,1)S(1)} %get-tuple-element.213), channel_id=1, source_target_pairs={{0,2},{1,3},{2,0},{3,1},{4,6},{5,7},{6,4},{7,5},{8,10},{9,11},{10,... | collective-permute-start | bytes 294920 | tf_op jit(solution)/shard_map/ppermute | solution.py:36
  104.3 20.0 %collective-permute-start.17 = (bf16[256,192]{1,0:T(8,128)(2,1)S(1)}, bf16[256,192]{1,0:T(8,128)(2,1)S(1)}, u32[]{:S(2)}, u32[]{:S(2)}) collective-permute-start(bf16[256,192]{1,0:T(8,128)(2,1)S(1)} %get-tuple-element.214), channel_id=1, source_target_pairs={{0,4},{1,5},{2,6},{3,7},{4,0},{5,1},{6,2},{7,3},{8,12},{9,13},{10,... | collective-permute-start | bytes 294920 | tf_op jit(solution)/shard_map/ppermute | solution.py:36
  106.5 19.4 %collective-permute-start.16 = (bf16[256,192]{1,0:T(8,128)(2,1)S(1)}, bf16[256,192]{1,0:T(8,128)(2,1)}, u32[]{:S(2)}, u32[]{:S(2)}) collective-permute-start(bf16[256,192]{1,0:T(8,128)(2,1)S(1)} %get-tuple-element.215), channel_id=1, source_target_pairs={{0,6},{1,7},{2,4},{3,5},{4,2},{5,3},{6,0},{7,1},{8,14},{9,15},{10,... | collective-permute-start | bytes 294920 | tf_op jit(solution)/shard_map/ppermute | solution.py:36
  107.6 29.0 %collective-permute-start.22 = (bf16[128,768]{1,0:T(8,128)(2,1)S(1)}, bf16[128,768]{1,0:T(8,128)(2,1)}, u32[]{:S(2)}, u32[]{:S(2)}) collective-permute-start(bf16[128,768]{1,0:T(8,128)(2,1)S(1)} %get-tuple-element.54), channel_id=1, source_target_pairs={{0,1},{1,0},{2,3},{3,2},{4,5},{5,4},{6,7},{7,6},{8,9},{9,8},{10,11... | collective-permute-start | bytes 589832 | tf_op jit(solution)/shard_map/ppermute | solution.py:36
  109.1 23.4 %collective-permute-start.23 = (bf16[128,768]{1,0:T(8,128)(2,1)}, bf16[128,768]{1,0:T(8,128)(2,1)}, u32[]{:S(2)}, u32[]{:S(2)}) collective-permute-start(bf16[128,768]{1,0:T(8,128)(2,1)} %collective-permute-done.13), channel_id=1, source_target_pairs={{0,1},{1,0},{2,3},{3,2},{4,5},{5,4},{6,7},{7,6},{8,9},{9,8},{10,11... | collective-permute-start | bytes 589832 | tf_op jit(solution)/shard_map/ppermute | solution.py:36
  117.9 16.2 %collective-permute-start.24 = (bf16[128,768]{1,0:T(8,128)(2,1)}, bf16[128,768]{1,0:T(8,128)(2,1)}, u32[]{:S(2)}, u32[]{:S(2)}) collective-permute-start(bf16[128,768]{1,0:T(8,128)(2,1)} %collective-permute-done.14), channel_id=1, source_target_pairs={{0,1},{1,0},{2,3},{3,2},{4,5},{5,4},{6,7},{7,6},{8,9},{9,8},{10,11... | collective-permute-start | bytes 589832 | tf_op jit(solution)/shard_map/ppermute | solution.py:36
  134.4 13.0 %collective-permute-start.26 = (bf16[128,896]{1,0:T(8,128)(2,1)S(1)}, bf16[128,896]{1,0:T(8,128)(2,1)S(1)}, u32[]{:S(2)}, u32[]{:S(2)}) collective-permute-start(bf16[128,896]{1,0:T(8,128)(2,1)S(1)} %get-tuple-element.190), channel_id=1, source_target_pairs={{0,1},{1,0},{2,3},{3,2},{4,5},{5,4},{6,7},{7,6},{8,9},{9,8},{10,11... | collective-permute-start | bytes 688136 | tf_op jit(solution)/shard_map/ppermute | solution.py:36
  169.4 20.6 %collective-permute-start.30 = (bf16[512,768]{1,0:T(8,128)(2,1)}, bf16[512,768]{1,0:T(8,128)(2,1)S(1)}, u32[]{:S(2)}, u32[]{:S(2)}) collective-permute-start(bf16[512,768]{1,0:T(8,128)(2,1)} %get-tuple-element.66), channel_id=1, source_target_pairs={{0,1},{1,0},{2,3},{3,2},{4,5},{5,4},{6,7},{7,6},{8,9},{9,8},{10,11... | collective-permute-start | bytes 2359304 | tf_op jit(solution)/shard_map/ppermute | solution.py:36
  181.5 24.3 %collective-permute-start.34 = (bf16[512,768]{1,0:T(8,128)(2,1)}, bf16[512,768]{1,0:T(8,128)(2,1)S(1)}, u32[]{:S(2)}, u32[]{:S(2)}) collective-permute-start(bf16[512,768]{1,0:T(8,128)(2,1)} %get-tuple-element.65), channel_id=1, source_target_pairs={{0,1},{1,0},{2,3},{3,2},{4,5},{5,4},{6,7},{7,6},{8,9},{9,8},{10,11... | collective-permute-start | bytes 2359304 | tf_op jit(solution)/shard_map/ppermute | solution.py:36
  210.7 16.0 %collective-permute-start.33 = (bf16[128,768]{1,0:T(8,128)(2,1)}, bf16[128,768]{1,0:T(8,128)(2,1)}, u32[]{:S(2)}, u32[]{:S(2)}) collective-permute-start(bf16[128,768]{1,0:T(8,128)(2,1)} %get-tuple-element.204), channel_id=1, source_target_pairs={{0,24},{8,16},{16,8},{24,0},{1,25},{9,17},{17,9},{25,1},{2,26},{10... | collective-permute-start | bytes 589832 | tf_op jit(solution)/shard_map/ppermute | solution.py:36
  210.8 16.0 %collective-permute-start.32 = (bf16[128,768]{1,0:T(8,128)(2,1)}, bf16[128,768]{1,0:T(8,128)(2,1)}, u32[]{:S(2)}, u32[]{:S(2)}) collective-permute-start(bf16[128,768]{1,0:T(8,128)(2,1)} %get-tuple-element.205), channel_id=1, source_target_pairs={{0,16},{8,24},{16,0},{24,8},{1,17},{9,25},{17,1},{25,9},{2,18},{10... | collective-permute-start | bytes 589832 | tf_op jit(solution)/shard_map/ppermute | solution.py:36
  211.5 15.3 %collective-permute-start.31 = (bf16[128,768]{1,0:T(8,128)(2,1)}, bf16[128,768]{1,0:T(8,128)(2,1)}, u32[]{:S(2)}, u32[]{:S(2)}) collective-permute-start(bf16[128,768]{1,0:T(8,128)(2,1)} %get-tuple-element.206), channel_id=1, source_target_pairs={{0,8},{8,0},{16,24},{24,16},{1,9},{9,1},{17,25},{25,17},{2,10},{10... | collective-permute-start | bytes 589832 | tf_op jit(solution)/shard_map/ppermute | solution.py:36
  212.6 13.1 %collective-permute-start.35 = (bf16[128,768]{1,0:T(8,128)(2,1)}, bf16[128,768]{1,0:T(8,128)(2,1)}, u32[]{:S(2)}, u32[]{:S(2)}) collective-permute-start(bf16[128,768]{1,0:T(8,128)(2,1)} %get-tuple-element.201), channel_id=1, source_target_pairs={{0,8},{8,0},{16,24},{24,16},{1,9},{9,1},{17,25},{25,17},{2,10},{10... | collective-permute-start | bytes 589832 | tf_op jit(solution)/shard_map/ppermute | solution.py:36
  233.2 19.5 %collective-permute-start.38 = (bf16[256,192]{1,0:T(8,128)(2,1)S(1)}, bf16[256,192]{1,0:T(8,128)(2,1)S(1)}, u32[]{:S(2)}, u32[]{:S(2)}) collective-permute-start(bf16[256,192]{1,0:T(8,128)(2,1)S(1)} %get-tuple-element.217), channel_id=1, source_target_pairs={{0,2},{1,3},{2,0},{3,1},{4,6},{5,7},{6,4},{7,5},{8,10},{9,11},{10,... | collective-permute-start | bytes 294920 | tf_op jit(solution)/shard_map/ppermute | solution.py:36
  238.3 14.4 %collective-permute-start.39 = (bf16[256,192]{1,0:T(8,128)(2,1)S(1)}, bf16[256,192]{1,0:T(8,128)(2,1)S(1)}, u32[]{:S(2)}, u32[]{:S(2)}) collective-permute-start(bf16[256,192]{1,0:T(8,128)(2,1)S(1)} %get-tuple-element.218), channel_id=1, source_target_pairs={{0,4},{1,5},{2,6},{3,7},{4,0},{5,1},{6,2},{7,3},{8,12},{9,13},{10,... | collective-permute-start | bytes 294920 | tf_op jit(solution)/shard_map/ppermute | solution.py:36
  239.4 19.6 %collective-permute-start.40 = (bf16[256,192]{1,0:T(8,128)(2,1)S(1)}, bf16[256,192]{1,0:T(8,128)(2,1)S(1)}, u32[]{:S(2)}, u32[]{:S(2)}) collective-permute-start(bf16[256,192]{1,0:T(8,128)(2,1)S(1)} %get-tuple-element.219), channel_id=1, source_target_pairs={{0,6},{1,7},{2,4},{3,5},{4,2},{5,3},{6,0},{7,1},{8,14},{9,15},{10,... | collective-permute-start | bytes 294920 | tf_op jit(solution)/shard_map/ppermute | solution.py:36
  280.4 25.6 %collective-permute-start.41 = (bf16[1024,384]{1,0:T(8,128)(2,1)}, bf16[1024,384]{1,0:T(8,128)(2,1)S(1)}, u32[]{:S(2)}, u32[]{:S(2)}) collective-permute-start(bf16[1024,384]{1,0:T(8,128)(2,1)} %get-tuple-element.84), channel_id=1, source_target_pairs={{0,1},{1,0},{2,3},{3,2},{4,5},{5,4},{6,7},{7,6},{8,9},{9,8},{10,11... | collective-permute-start | bytes 2359304 | tf_op jit(solution)/shard_map/ppermute | solution.py:36
  326.6 14.6 %collective-permute-start.44 = (bf16[4,2,24,1408]{3,2,0,1:T(8,128)(2,1)}, bf16[4,2,24,1408]{3,2,0,1:T(8,128)(2,1)}, u32[]{:S(2)}, u32[]{:S(2)}) collective-permute-start(bf16[4,2,24,1408]{3,2,0,1:T(8,128)(2,1)} %select_bitcast_fusion.3), channel_id=1, source_target_pairs={{0,16},{8,24},{16,0},{24,8},{1,17},{9,25},{17,1},{25,9},{2,18},{10... | collective-permute-start | bytes 1622024 | tf_op jit(solution)/shard_map/ppermute | solution.py:36
  328.3 27.3 %collective-permute-start.42 = (bf16[512,768]{1,0:T(8,128)(2,1)}, bf16[512,768]{1,0:T(8,128)(2,1)}, u32[]{:S(2)}, u32[]{:S(2)}) collective-permute-start(bf16[512,768]{1,0:T(8,128)(2,1)} %get-tuple-element.180), channel_id=1, source_target_pairs={{0,2},{1,3},{2,0},{3,1},{4,6},{5,7},{6,4},{7,5},{8,10},{9,11},{10,... | collective-permute-start | bytes 2359304 | tf_op jit(solution)/shard_map/ppermute | solution.py:36
  358.2 27.9 %collective-permute-start.45 = (bf16[256,768]{1,0:T(8,128)(2,1)}, bf16[256,768]{1,0:T(8,128)(2,1)S(1)}, u32[]{:S(2)}, u32[]{:S(2)}) collective-permute-start(bf16[256,768]{1,0:T(8,128)(2,1)} %slice.646), channel_id=1, source_target_pairs={{0,4},{1,5},{2,6},{3,7},{4,0},{5,1},{6,2},{7,3},{8,12},{9,13},{10,... | collective-permute-start | bytes 1179656 | tf_op jit(solution)/shard_map/ppermute | solution.py:36
  363.6 19.6 %collective-permute-start.48 = (bf16[24,1408]{1,0:T(8,128)(2,1)S(1)}, bf16[24,1408]{1,0:T(8,128)(2,1)S(1)}, u32[]{:S(2)}, u32[]{:S(2)}) collective-permute-start(bf16[24,1408]{1,0:T(8,128)(2,1)S(1)} %get-tuple-element.156), channel_id=1, source_target_pairs={{0,4},{1,5},{2,6},{3,7},{4,0},{5,1},{6,2},{7,3},{8,12},{9,13},{10,... | collective-permute-start | bytes 202760 | tf_op jit(solution)/shard_map/ppermute | solution.py:36
  366.1 17.0 %collective-permute-start.49 = (bf16[24,1408]{1,0:T(8,128)(2,1)S(1)}, bf16[24,1408]{1,0:T(8,128)(2,1)S(1)}, u32[]{:S(2)}, u32[]{:S(2)}) collective-permute-start(bf16[24,1408]{1,0:T(8,128)(2,1)S(1)} %get-tuple-element.225), channel_id=1, source_target_pairs={{0,2},{1,3},{2,0},{3,1},{4,6},{5,7},{6,4},{7,5},{8,10},{9,11},{10,... | collective-permute-start | bytes 202760 | tf_op jit(solution)/shard_map/ppermute | solution.py:36
  366.7 16.4 %collective-permute-start.47 = (bf16[24,1408]{1,0:T(8,128)(2,1)S(1)}, bf16[24,1408]{1,0:T(8,128)(2,1)S(1)}, u32[]{:S(2)}, u32[]{:S(2)}) collective-permute-start(bf16[24,1408]{1,0:T(8,128)(2,1)S(1)} %get-tuple-element.226), channel_id=1, source_target_pairs={{0,6},{1,7},{2,4},{3,5},{4,2},{5,3},{6,0},{7,1},{8,14},{9,15},{10,... | collective-permute-start | bytes 202760 | tf_op jit(solution)/shard_map/ppermute | solution.py:36
  (62 other events, 484.5 us)
Sparse Core Ops, SparseCore 0:
  59.8 100.9 all-gather.2
  225.9 97.7 reduce-scatter.1
